TPU v7x, 256 devices: a whole 4x4x8 slice. The times are simulated.
256 devices in a mesh: dp: 64 (over y, z, core), rep: 4 (over x).
Axes of the slice: x: 4, y: 4, z: 8, core: 2. Of those that a mesh axis runs over, the one named last changes fastest.
Arguments:
- embeddings: bfloat16 [262144, 768], P(('dp', 'rep'))
- cluster_ids: int32 [262144], P(('dp', 'rep')), may hold values from 0 to 127, as said below
- member_order: int32 [262144], P(('dp', 'rep')), may hold values from 0 to 4095, as said below
Outputs:
- earlier_max: float32 [262144], P(('dp', 'rep'))
Inputs may be any that keep to these rules, and one draw needn't show every extreme that they name: `cluster_ids`: clusters come in groups of 2 consecutive ids. In the rows of one device (aligned blocks of 1024 rows) at most 32 rows name clusters of one group; one group, the same in every block, is named by exactly 32 rows of every block. A cluster has at most 4096 rows, and the clusters of that group have exactly 4096; a cluster may have none. `member_order`: within every cluster the rows carry the orders 0 to its size - 1, each once.
All inputs are finite; a program needn't handle non-finite values.
Results may differ from a plain program's by a relative error of at most 0.00074.
Values may be sent and summed in bfloat16 or wider, within the bound.
No kernel may reach another device: no remote copies, remote signals or barrier semaphores. Data moves between devices by JAX's collectives and lax.ppermute only.
A program may use at most 128 MiB of HBM per device.

v0:
```python
import jax
import jax.numpy as jnp
from jax import lax
from jax.sharding import PartitionSpec as P

CL_OWN = 2


def normalize(embeddings):
    wide_rows = embeddings.astype(jnp.float32)
    return (
        wide_rows / jnp.sqrt(jnp.sum(wide_rows * wide_rows, axis=1, keepdims=True) + 1e-06)
    ).astype(jnp.bfloat16)


def local(embeddings, cluster_ids, member_order):
    row_dev, feature_count = embeddings.shape
    dp_count = lax.axis_size("dp")
    rep_count = lax.axis_size("rep")
    capacity = 2 * row_dev // dp_count
    slot_count = 2 * rep_count * row_dev // CL_OWN
    held_slots = CL_OWN * slot_count
    rep_here = lax.axis_index("rep")
    unit_rows = normalize(embeddings)
    owner_index = cluster_ids // CL_OWN
    slot_place = cluster_ids % CL_OWN * slot_count + member_order
    onehot = (owner_index[:, None] == jnp.arange(dp_count, dtype=jnp.int32)[None, :]).astype(
        jnp.int32
    )
    before_me = jnp.sum((jnp.cumsum(onehot, axis=0) - onehot) * onehot, axis=1)
    target = owner_index * capacity + before_me
    outbox = jnp.zeros((dp_count * capacity, feature_count), jnp.bfloat16).at[target].set(unit_rows)
    out_place = jnp.full((dp_count * capacity,), held_slots, jnp.int32).at[target].set(slot_place)
    received, received_place = (
        lax.all_to_all(outbox, "dp", split_axis=0, concat_axis=0, tiled=True),
        lax.all_to_all(out_place, "dp", split_axis=0, concat_axis=0, tiled=True),
    )
    all_rows, all_place = (
        lax.all_gather(received[None], "rep", axis=0, tiled=True),
        lax.all_gather(received_place[None], "rep", axis=0, tiled=True),
    )
    members = (
        jnp.zeros((held_slots, feature_count), jnp.bfloat16)
        .at[all_place.reshape(-1)]
        .set(all_rows.reshape(-1, feature_count), mode="drop")
    )
    clusters = members.reshape(CL_OWN, slot_count, feature_count)
    position = jnp.arange(slot_count, dtype=jnp.int32)
    quarter = slot_count // rep_count
    key_rows = lax.dynamic_slice_in_dim(clusters, rep_here * quarter, quarter, 1)
    similar = jnp.einsum("csd,ckd->csk", clusters, key_rows, preferred_element_type=jnp.float32)
    key_pos = rep_here * quarter + jnp.arange(quarter, dtype=jnp.int32)
    earlier_mask = key_pos[None, :] < position[:, None]
    partial_max = jnp.max(jnp.where(earlier_mask[None], similar, -1.0), axis=2)
    merged = lax.pmax(partial_max.reshape(-1), "rep")
    answers = merged[jnp.minimum(received_place, held_slots - 1)]
    returned = lax.all_to_all(answers, "dp", split_axis=0, concat_axis=0, tiled=True)
    return returned[target]


def solution(mesh):
    return jax.shard_map(
        local,
        mesh=mesh,
        in_specs=(P(("dp", "rep"), None), P(("dp", "rep")), P(("dp", "rep"))),
        out_specs=P(("dp", "rep")),
        check_vma=False,
    )
```

profile of v0, /device:TPU:1, one launch (start us, length us, event | category | flops | bytes accessed | tf_op | source)
XLA Modules:
  0.0 369.9 jit_solution(7168944072356704308)
XLA Ops:
  6.5 0.0 all-gather.3.cloned.1.call-start
  6.5 1.8 fusion.2
  8.3 0.7 fusion.14
  9.1 18.0 %reduce-window.6 = s32[64,8,128]{2,1,0:T(8,128)S(1)} reduce-window(s32[64,8,128]{2,1,0:T(8,128)S(1)} %fusion.12, s32[]{:T(128)} %constant.27.clone.1), window={size=1x1x128 pad=0_0x0_0x127_0}, to_apply=%region_0.0 | reduce-window | flops 8323072 | bytes 524292 | tf_op jit(solution)/shard_map/reduce-window
  27.1 0.1 slice.12
  27.2 0.1 copy.6
  27.4 0.1 copy.7
  27.5 0.1 broadcast_add_fusion
  27.6 0.1 fusion.11
  27.7 7.2 %scatter_custom_fusion.1 = bf16[2048,768]{1,0:T(8,128)(2,1)S(1)} fusion(s32[1024]{0:T(1024)S(1)} %get-tuple-element.8, bf16[1024,768]{1,0:T(8,128)(2,1)} %param.3, f32[1024]{0:T(1024)S(1)} %add_sqrt_fusion, bf16[]{:T(256)} %constant.22.clone.1), kind=kCustom, calls=%fused_computation.14 | custom fusion | flops 2359296 | bytes 4722690 | tf_op jit(solution)/shard_map/scatter | solution.py:32
  34.9 86.6 %all_to_all.30 = bf16[64,32,768]{2,1,0:T(8,128)(2,1)} all-to-all(bf16[64,32,768]{2,1,0:T(8,128)(2,1)S(1)} %bitcast.38), channel_id=1, replica_groups=mesh['dp'=64,'rep'=4] {'dp'}, dimensions={0} | all-to-all | bytes 6291456 | tf_op jit(solution)/shard_map/all_to_all | solution.py:35
  121.5 0.0 all-gather.3.cloned.1.call-update
  121.5 4.3 %scatter_custom_fusion = s32[2048]{0:T(1024)S(1)} fusion(s32[1024]{0:T(1024)S(1)} %get-tuple-element.8, s32[1024]{0:T(1024)S(1)} %get-tuple-element.9, s32[]{:T(128)} %constant.25.clone.1), kind=kCustom, calls=%fused_computation.39 | custom fusion | bytes 8196 | tf_op jit(solution)/shard_map/scatter | solution.py:33
  125.8 0.7 all_to_all.20
  126.5 6.2 %all-to-all-start = ((s32[64,32,1]{1,2,0:T(1,128)}), s32[64,32,1]{1,2,0:T(1,128)S(1)}, u32[]{:S(2)}, u32[]{:S(2)}) async-start(s32[64,32,1]{1,2,0:T(1,128)} %bitcast.3), calls=%async_computation | async-start | bytes 65536 | tf_op jit(solution)/shard_map/all_to_all | solution.py:36
  132.7 5.0 %iota_compare_fusion = pred[4096,1024]{0,1:T(8,128)(4,1)} fusion(s32[1024]{0:T(1024)S(1)} %iota_add_fusion), kind=kLoop, calls=%fused_computation.6 | loop fusion | flops 4194304 | bytes 4198400 | tf_op jit(solution)/shard_map/lt | solution.py:53
  137.7 4.3 %all-to-all-done = s32[64,32,1]{1,2,0:T(1,128)S(1)} async-done(((s32[64,32,1]{1,2,0:T(1,128)}), s32[64,32,1]{1,2,0:T(1,128)S(1)}, u32[]{:S(2)}, u32[]{:S(2)}) %all-to-all-start) | async-done | bytes 8224 | tf_op jit(solution)/shard_map/all_to_all | solution.py:36
  142.0 0.5 broadcast.126
  142.5 0.8 minimum_reduce_fusion
  143.3 0.1 min.18
  143.4 0.1 reshape.163
  143.5 10.7 %all-gather = s32[4,1,2048]{2,1,0:T(1,128)S(1)} all-gather(s32[1,1,2048]{2,1,0:T(1,128)S(1)} %reshape.163), channel_id=1, replica_groups=mesh['dp'=64,'rep'=4] {'rep'}, dimensions={0}, use_global_device_ids=true | all-gather | bytes 40960 | tf_op jit(solution)/shard_map/all_gather | solution.py:40
  154.3 85.7 %all-gather.3.cloned.1.call-done = bf16[4,2048,768]{2,1,0:T(8,128)(2,1)} async-done(((bf16[1,2048,768]{2,1,0:T(8,128)(2,1)}), bf16[4,2048,768]{2,1,0:T(8,128)(2,1)}) %all-gather.3.cloned.1.call-update) | async-done | bytes 12582928 | tf_op jit(solution)/shard_map/all_gather | solution.py:39
  239.9 43.6 %scatter_custom_fusion.2 = bf16[8192,768]{1,0:T(8,128)(2,1)} fusion(s32[8192]{0:T(1024)S(1)} %bitcast.44, bf16[8192,768]{1,0:T(8,128)(2,1)} %bitcast.48, bf16[]{:T(256)} %constant.22.clone.1), kind=kCustom, calls=%fused_computation.7 | custom fusion | bytes 12583424 | tf_op jit(solution)/shard_map/scatter | solution.py:45
  283.5 19.9 %select_reduce_fusion = f32[2,4096]{1,0:T(2,128)S(1)} fusion(pred[4096,1024]{0,1:T(8,128)(4,1)} %iota_compare_fusion, bf16[2,4096,768]{2,1,0:T(8,128)(2,1)} %bitcast.36, s32[]{:T(128)S(6)} %select_n.48), kind=kOutput, calls=%fused_computation.5 | convolution fusion | flops 12901670912 | bytes 19955716 | tf_op jit(solution)/shard_map/csd,ckd->csk/dot_general | solution.py:51
  303.4 12.0 %pmax.7 = f32[8192]{0:T(1024)S(1)} all-reduce(f32[8192]{0:T(1024)S(1)} %bitcast.42), channel_id=1, replica_groups=mesh['dp'=64,'rep'=4] {'rep'}, use_global_device_ids=true, to_apply=%region_8.9 | all-reduce | flops 8192 | bytes 65536 | tf_op jit(solution)/shard_map/pmax | solution.py:55
  315.5 11.8 %gather_fusion = f32[2048]{0:T(1024)S(1)} fusion(f32[8192]{0:T(1024)S(1)} %pmax.7, s32[2048]{0:T(1024)S(1)} %broadcast_clamp_fusion), kind=kCustom, calls=%fused_computation | custom fusion | bytes 24576 | tf_op jit(solution)/shard_map/gather | solution.py:56
  327.3 0.1 all_to_all.24
  327.3 23.8 %all_to_all.31 = f32[64,32,1]{1,2,0:T(1,128)S(1)} all-to-all(f32[64,32,1]{1,2,0:T(1,128)S(1)} %bitcast.41), channel_id=1, replica_groups=mesh['dp'=64,'rep'=4] {'dp'}, dimensions={0} | all-to-all | bytes 16384 | tf_op jit(solution)/shard_map/all_to_all | solution.py:57
  351.2 0.5 broadcast.127
  351.7 0.7 reduce.11
  352.4 0.1 all_to_all.26
  352.5 10.5 %gather_fusion.1 = f32[1024]{0:T(1024)} fusion(f32[2048]{0:T(1024)S(1)} %all_to_all.26, s32[1024]{0:T(1024)S(1)} %get-tuple-element.7), kind=kCustom, calls=%fused_computation.1 | custom fusion | bytes 12288 | tf_op jit(solution)/shard_map/gather | solution.py:58
  (10 shorter events, 0.1 us)
Async XLA Ops:
  6.5 233.4 %all-gather.3.cloned.1.call-start = ((), (), s32[]{:S(2)}) async-start(), calls=%async_computation.3 | async-start | bytes 15728640 | tf_op jit(solution)/shard_map/all_gather | solution.py:39
  126.5 15.5 %all-to-all-start = ((s32[64,32,1]{1,2,0:T(1,128)}), s32[64,32,1]{1,2,0:T(1,128)S(1)}, u32[]{:S(2)}, u32[]{:S(2)}) async-start(s32[64,32,1]{1,2,0:T(1,128)} %bitcast.3), calls=%async_computation | async-start | bytes 65536 | tf_op jit(solution)/shard_map/all_to_all | solution.py:36
Sparse Core Ops, SparseCore 0:
  121.6 118.2 all-gather.2
where the time goes:
time: 370 us
  blocking collectives  133 us (36%)
  waiting for transfers between devices  89.9 us (24%)
  local copies, waits for them, and re-layouts  72.6 us (20%)
  other arithmetic  34.6 us (9%)
  matrix products  19.9 us (5%)
  between operations  13.6 us (4%)
  starting transfers between devices  6.19 us (2%)
    all_to_all x1, blocking collectives, local(): lax.all_to_all(outbox, 'dp', split_axis=0, concat_axis=0, tiled=True)  86.6 us
    all_gather x1, waiting for transfers between devices, local(): lax.all_gather(received[None], 'rep', axis=0, tiled=True)  85.7 us
    scatter x1, local copies, waits for them, and re-layouts, local(): members = jnp.zeros((held_slots, feature_count), jnp.bfloat16).at[all_pla...  43.6 us
    all_to_all x1, blocking collectives, local(): lax.all_to_all(answers, 'dp', split_axis=0, concat_axis=0, tiled=True)  23.8 us
    dot_general x1, matrix products, local(): jnp.einsum('csd,ckd->csk', clusters, key_rows, preferred_element_type=jnp...  19.9 us
    another operation x3, other arithmetic  18.2 us
    pmax x1, blocking collectives, local(): merged = lax.pmax(partial_max.reshape(-1), 'rep')  12 us
    gather x1, local copies, waits for them, and re-layouts, local(): answers = merged[jnp.minimum(received_place, held_slots - 1)]  11.8 us
  transfers between devices with their start and end apart: 2, of which 2 were waited for; matrix products, arithmetic and copies ran while one was open for 3% of the time, Pallas kernels for 0%

commit v1 on v0

v1 whole, which is shorter than its diff:
```python
import functools

import jax
import jax.numpy as jnp
import numpy as np
from jax import lax
from jax.experimental import pallas as pl
from jax.experimental.pallas import tpu as pltpu
from jax.sharding import PartitionSpec as P

AXES = ("dp", "rep")
NX, NY, NZ = 4, 4, 8
CHIPS = NX * NY * NZ
GROUPS = 64
HALF = GROUPS // 2
SUB = 8
ROWS = 1024
D = 768
KEYS = 128
WIDE = D + KEYS
HALF_ROWS = 512
ORDERS = 4096
VMEM = 56 * 1024 * 1024


def device(x, y, z, core):
    return ((y * NZ + z) * 2 + core) * NX + x


SAME_CORE = [
    [device(x, y, z, core) for y in range(NY) for z in range(NZ) for x in range(NX)] for core in range(2)
]


def ring(step):
    pairs = []
    for y in range(NY):
        for z in range(NZ):
            for x in range(NX):
                pairs.append((device(x, y, z, 0), device((x + step) % NX, y, z, 0)))
                pairs.append((device(x, y, z, 1), device(x, (y + step) % NY, z, 1)))
    return pairs


SIBLING = [(dp * NX + x, (dp ^ 1) * NX + x) for dp in range(NY * NZ * 2) for x in range(NX)]


def exchange(rows):
    return lax.all_to_all(
        rows, AXES, split_axis=0, concat_axis=0, tiled=True, axis_index_groups=SAME_CORE
    )


def send(rows, pairs):
    return lax.ppermute(rows, AXES, pairs)


def cost(flops, size):
    return pl.CostEstimate(flops=flops, bytes_accessed=size, transcendentals=0)


def chip_of(group, place):
    core = (group >= HALF).astype(jnp.int32)
    inner = group - HALF * core
    on_x = inner * NX + place
    on_y = (place * NZ + (inner & (NZ - 1))) * NX + (inner >> 3)
    return jnp.where(core == 0, on_x, on_y), core


def key_rows(ids, order, first):
    key = (ids & 1) * ORDERS + order
    which = lax.broadcasted_iota(jnp.int32, (KEYS, ids.shape[1]), 0)
    high, low = (key >> 7) + 1, key & 127
    return jnp.where(which == first, high, jnp.where(which == first + 1, low, 0)).astype(jnp.float32).astype(
        jnp.bfloat16
    )


def slots_of(info, core, mine):
    group, rank = info[0:1], info[1:2]
    chip, serving = chip_of(group, rank & 3)
    slot = chip * SUB + (rank >> 2)
    return jnp.where((serving == core) if mine else (serving != core), slot, -1)


def onehot(slot):
    rows = lax.broadcasted_iota(jnp.int32, (ROWS, ROWS), 0)
    return jnp.where(rows == slot, 1.0, 0.0).astype(jnp.bfloat16)


def prep_kernel(place_ref, emb_ref, ids_ref, order_ref, unit_ref, box_ref, slab_ref, info_ref):
    ids, order = ids_ref[...], order_ref[...]
    group = ids >> 1
    member = (lax.broadcasted_iota(jnp.int32, (GROUPS, ROWS), 0) == group)
    hot = jnp.where(member, 1.0, 0.0)
    step = 256
    earlier = jnp.where(
        lax.broadcasted_iota(jnp.int32, (step, step), 0) < lax.broadcasted_iota(jnp.int32, (step, step), 1), 1.0, 0.0
    ).astype(jnp.bfloat16)
    before = jnp.zeros((GROUPS, 1), jnp.float32)
    ranks = []
    for part in range(ROWS // step):
        here = hot[:, part * step : (part + 1) * step]
        count = jnp.dot(here.astype(jnp.bfloat16), earlier, preferred_element_type=jnp.float32) + before
        ranks.append(jnp.sum(here * count, axis=0, keepdims=True))
        before = before + jnp.sum(here, axis=1, keepdims=True)
    rank = jnp.concatenate(ranks, axis=1).astype(jnp.int32)
    which = lax.broadcasted_iota(jnp.int32, (8, ROWS), 0)
    info = jnp.where(which == 0, group, jnp.where(which == 1, rank, 0))
    info_ref[...] = info

    wide = emb_ref[...].astype(jnp.float32)
    scale = 1.0 / jnp.sqrt(jnp.sum(wide * wide, axis=1, keepdims=True) + 1e-06)
    unit = (wide * scale).astype(jnp.bfloat16)
    unit_ref[...] = unit

    pick = onehot(slots_of(info, place_ref[0], True))
    box_ref[...] = jnp.dot(pick, unit, preferred_element_type=jnp.float32).astype(jnp.bfloat16)
    slab_ref[...] = lax.dot_general(
        pick, key_rows(ids, order, 2), (((1,), (1,)), ((), ())), preferred_element_type=jnp.float32
    ).astype(jnp.bfloat16)


def prep(place, embeddings, ids, order):
    return pl.pallas_call(
        prep_kernel,
        out_shape=(
            jax.ShapeDtypeStruct((ROWS, D), jnp.bfloat16),
            jax.ShapeDtypeStruct((ROWS, D), jnp.bfloat16),
            jax.ShapeDtypeStruct((ROWS, KEYS), jnp.bfloat16),
            jax.ShapeDtypeStruct((8, ROWS), jnp.int32),
        ),
        in_specs=[pl.BlockSpec(memory_space=pltpu.SMEM)] + [pl.BlockSpec(memory_space=pltpu.VMEM)] * 3,
        out_specs=tuple([pl.BlockSpec(memory_space=pltpu.VMEM)] * 4),
        compiler_params=pltpu.CompilerParams(vmem_limit_bytes=VMEM),
        cost_estimate=cost(2 * ROWS * ROWS * WIDE, 6 * ROWS * D),
        name="prep",
    )(place, embeddings, ids, order)


def hand_kernel(place_ref, unit_ref, info_ref, ids_ref, order_ref, box_ref):
    pick = onehot(slots_of(info_ref[...], place_ref[0], False))
    box_ref[:, :D] = jnp.dot(pick, unit_ref[...], preferred_element_type=jnp.float32).astype(jnp.bfloat16)
    box_ref[:, D:] = lax.dot_general(
        pick,
        key_rows(ids_ref[...], order_ref[...], 0),
        (((1,), (1,)), ((), ())),
        preferred_element_type=jnp.float32,
    ).astype(jnp.bfloat16)


def hand(place, unit, info, ids, order):
    return pl.pallas_call(
        hand_kernel,
        out_shape=jax.ShapeDtypeStruct((ROWS, WIDE), jnp.bfloat16),
        in_specs=[pl.BlockSpec(memory_space=pltpu.SMEM)] + [pl.BlockSpec(memory_space=pltpu.VMEM)] * 4,
        out_specs=pl.BlockSpec(memory_space=pltpu.VMEM),
        compiler_params=pltpu.CompilerParams(vmem_limit_bytes=VMEM),
        cost_estimate=cost(2 * ROWS * ROWS * WIDE, 4 * ROWS * D),
        name="hand",
    )(place, unit, info, ids, order)


def stamp_kernel(box_ref, slab_ref, out_ref):
    out_ref[...] = box_ref[...] + slab_ref[...]


def stamp(box, slab):
    return pl.pallas_call(
        stamp_kernel,
        grid=(1,),
        out_shape=jax.ShapeDtypeStruct(box.shape, box.dtype),
        in_specs=[
            pl.BlockSpec((ROWS, KEYS), lambda i: (0, D // KEYS)),
            pl.BlockSpec((ROWS, KEYS), lambda i: (0, 0)),
        ],
        out_specs=pl.BlockSpec((ROWS, KEYS), lambda i: (0, D // KEYS)),
        input_output_aliases={0: 0},
        compiler_params=pltpu.CompilerParams(vmem_limit_bytes=VMEM),
        cost_estimate=cost(0, 3 * 2 * ROWS * KEYS),
        name="stamp",
    )(box, slab)


BLOCKS = [(part, far, chunk) for far in range(3) for chunk in range(2) for part in "PM"]
SLOT = {block: number for number, block in enumerate(BLOCKS)}


def pair_lists():
    pairs, by_place = [], []

    def all_chunks(one, other):
        for c in range(2):
            for e in range(2):
                pairs.append((one + (c,), other + (e,)))

    for part in "PM":
        pairs.append(((part, 0, 0), (part, 0, 1)))
        all_chunks((part, 0), (part, 1))
        pairs.append(((part, 0, 1), (part, 2, 0)))
        early = ((part, 0, 0), (part, 2, 0))
        late = ((part, 0, 1), (part, 2, 1))
        by_place.append((early, late) if part == "P" else (late, early))
    all_chunks(("P", 0), ("M", 0))
    all_chunks(("P", 0), ("M", 1))
    all_chunks(("P", 1), ("M", 1))
    pairs.append((("P", 1, 0), ("M", 2, 0)))
    pairs.append((("P", 1, 1), ("M", 2, 0)))
    pairs.append((("P", 2, 0), ("M", 1, 1)))
    pairs.append((("P", 1, 1), ("M", 2, 1)))
    return pairs, by_place


def similar_kernel(loads, used, n_self, n_pairs, n_before, *refs):
    n_arrays = 1 + max(load[0] for load in loads)
    selfs_ref, pairs_ref = refs[:2]
    arrays = refs[2 : 2 + n_arrays]
    befores = refs[2 + n_arrays : 2 + n_arrays + n_before]
    out_ref = refs[2 + n_arrays + n_before]
    rows, slabs, kcol, ccol, krow, crow, best_row, best_col, sems = refs[3 + n_arrays + n_before :]

    copies = []
    for number, (array, first, columns, slot) in enumerate(loads):
        source = arrays[array].at[pl.ds(first, HALF_ROWS), pl.ds(columns, KEYS if columns else D)]
        target = slabs.at[slot] if columns else rows.at[slot]
        copy = pltpu.make_async_copy(source, target, sems.at[number])
        copy.start()
        copies.append((copy, bool(columns)))
    for slot in used:
        best_row[slot] = jnp.full((HALF_ROWS, 128), -1.0, jnp.float32)
        best_col[slot] = jnp.full((8, HALF_ROWS), -1.0, jnp.float32)
    for copy, is_key in copies:
        if is_key:
            copy.wait()

    lane_of = lax.broadcasted_iota(jnp.int32, (KEYS, 128), 0)
    row_of = lax.broadcasted_iota(jnp.int32, (8, KEYS), 1)
    for slot in used:
        part, far, chunk = BLOCKS[slot]
        first = 0 if chunk == 1 else 2
        slab = slabs[SLOT[(part, far, 1)]]
        weight = jnp.where(lane_of == first, 128.0, jnp.where(lane_of == first + 1, 1.0, 0.0)).astype(jnp.bfloat16)
        key = jnp.dot(slab, weight, preferred_element_type=jnp.float32)
        kcol[slot] = key
        ccol[slot] = jnp.where(key >= ORDERS + 128, 2.0, jnp.where(key > 0, 1.0, 0.0))
        weight = jnp.where(row_of == first, 128.0, jnp.where(row_of == first + 1, 1.0, 0.0)).astype(jnp.bfloat16)
        key = lax.dot_general(weight, slab, (((1,), (1,)), ((), ())), preferred_element_type=jnp.float32)
        krow[slot] = key
        crow[slot] = jnp.where(key >= ORDERS + 128, 2.0, jnp.where(key > 0, 1.0, 0.0))
    for copy, is_key in copies:
        if not is_key:
            copy.wait()

    width = 256

    def products(a, b, start):
        return lax.dot_general(
            rows[a], rows[b, start : start + width], (((1,), (1,)), ((), ())), preferred_element_type=jnp.float32
        )

    def one_self(number, carry):
        a = selfs_ref[number]
        ka, ca = kcol[a], ccol[a]
        best = best_row[a]
        for start in range(0, HALF_ROWS, width):
            s = products(a, a, start)
            for lane in range(0, width, 128):
                at = start + lane
                kb, cb = krow[a, 0:1, at : at + 128], crow[a, 0:1, at : at + 128]
                best = jnp.maximum(
                    best, jnp.where((ca == cb) & (kb < ka), s[:, lane : lane + 128], -1.0)
                )
        best_row[a] = best
        return carry

    def one_pair(number, carry):
        a, b = pairs_ref[2 * number], pairs_ref[2 * number + 1]
        ka, ca = kcol[a], ccol[a]
        best = best_row[a]
        for start in range(0, HALF_ROWS, width):
            s = products(a, b, start)
            for lane in range(0, width, 128):
                at = start + lane
                kb, cb = krow[b, 0:1, at : at + 128], crow[b, 0:1, at : at + 128]
                same = jnp.where(ca == cb, s[:, lane : lane + 128], -1.0)
                later = kb < ka
                best = jnp.maximum(best, jnp.where(later, same, -1.0))
                other = jnp.where(later, -1.0, same).reshape(HALF_ROWS // 8, 8, 128)
                best_col[b, :, at : at + 128] = jnp.maximum(
                    best_col[b, :, at : at + 128], jnp.max(other, axis=0)
                )
        best_row[a] = best
        return carry

    if n_self:
        lax.fori_loop(0, n_self, one_self, 0)
    lax.fori_loop(0, n_pairs, one_pair, 0)

    halves = {}
    sub = lax.broadcasted_iota(jnp.int32, (HALF_ROWS // SUB, SUB, 128), 1)
    lane = lax.broadcasted_iota(jnp.int32, (HALF_ROWS // SUB, SUB, 128), 2)
    for slot in used:
        part, far, chunk = BLOCKS[slot]
        by_row = jnp.max(best_row[slot], axis=1, keepdims=True)
        by_col = jnp.max(best_col[slot], axis=0, keepdims=True)
        by_col = jnp.transpose(jnp.broadcast_to(by_col, (128, HALF_ROWS)))
        value = jnp.maximum(by_col, by_row).reshape(HALF_ROWS // SUB, SUB, 128)
        value = jnp.max(jnp.where(lane == sub + (far * 16 + chunk * SUB), value, -1.0), axis=1)
        halves[part] = jnp.maximum(halves[part], value) if part in halves else value
    for number, part in enumerate("PM"):
        at = pl.ds(number * (CHIPS // 2), CHIPS // 2)
        value = halves[part]
        for before in befores:
            value = jnp.maximum(value, before[at, :])
        out_ref[at, :] = value


def similar(arrays, loads, selfs, pairs, n_pairs, slots, befores, name):
    n_blocks = len(BLOCKS)
    used = sorted(slots)
    kernel = functools.partial(similar_kernel, loads, used, len(selfs), n_pairs, len(befores))
    return pl.pallas_call(
        kernel,
        out_shape=jax.ShapeDtypeStruct((CHIPS, 128), jnp.float32),
        in_specs=[pl.BlockSpec(memory_space=pltpu.SMEM)] * 2
        + [pl.BlockSpec(memory_space=pl.ANY)] * len(arrays)
        + [pl.BlockSpec(memory_space=pltpu.VMEM)] * len(befores),
        out_specs=pl.BlockSpec(memory_space=pltpu.VMEM),
        scratch_shapes=[
            pltpu.VMEM((n_blocks, HALF_ROWS, D), jnp.bfloat16),
            pltpu.VMEM((n_blocks, HALF_ROWS, KEYS), jnp.bfloat16),
            pltpu.VMEM((n_blocks, HALF_ROWS, 128), jnp.float32),
            pltpu.VMEM((n_blocks, HALF_ROWS, 128), jnp.float32),
            pltpu.VMEM((n_blocks, 8, HALF_ROWS), jnp.float32),
            pltpu.VMEM((n_blocks, 8, HALF_ROWS), jnp.float32),
            pltpu.VMEM((n_blocks, HALF_ROWS, 128), jnp.float32),
            pltpu.VMEM((n_blocks, 8, HALF_ROWS), jnp.float32),
            pltpu.SemaphoreType.DMA((len(loads),)),
        ],
        compiler_params=pltpu.CompilerParams(vmem_limit_bytes=VMEM),
        cost_estimate=cost(
            2 * D * HALF_ROWS * HALF_ROWS * (n_pairs + len(selfs)), 2 * len(loads) * HALF_ROWS * D
        ),
        name=name,
    )(jnp.array(selfs or [0], jnp.int32), pairs, *arrays, *befores)


def answer_kernel(place_ref, info_ref, mine_ref, sibling_ref, out_ref):
    info = info_ref[...]
    group, rank = info[0:1], info[1:2]
    core, step = place_ref[0], place_ref[2]
    values = jnp.concatenate([mine_ref[...], sibling_ref[...]], axis=0)
    device_of = lax.broadcasted_iota(jnp.int32, (2 * CHIPS, ROWS), 0)
    lane_of = lax.broadcasted_iota(jnp.int32, (128, ROWS), 0)
    best = jnp.full((1, ROWS), -1.0, jnp.float32)
    for far in range(3):
        chip, serving = chip_of(group, (rank + far * step) & 3)
        away = (serving != core).astype(jnp.int32)
        pick = jnp.where(device_of == chip + CHIPS * away, 1.0, 0.0)
        found = lax.dot_general(
            values,
            pick,
            (((0,), (0,)), ((), ())),
            preferred_element_type=jnp.float32,
            precision=lax.Precision.HIGHEST,
        )
        wanted = far * 16 + away * SUB + (rank >> 2)
        found = jnp.max(jnp.where(lane_of == wanted, found, -1.0), axis=0, keepdims=True)
        best = jnp.maximum(best, found)
    out_ref[...] = best


def answer(place, info, mine, sibling):
    return pl.pallas_call(
        answer_kernel,
        out_shape=jax.ShapeDtypeStruct((1, ROWS), jnp.float32),
        in_specs=[pl.BlockSpec(memory_space=pltpu.SMEM)] + [pl.BlockSpec(memory_space=pltpu.VMEM)] * 3,
        out_specs=pl.BlockSpec(memory_space=pltpu.VMEM),
        compiler_params=pltpu.CompilerParams(vmem_limit_bytes=VMEM),
        cost_estimate=cost(2 * 3 * 6 * 128 * 256 * ROWS, 3 * 4 * 128 * 128),
        name="answer",
    )(place, info, mine, sibling)


def local(embeddings, cluster_ids, member_order):
    dp, x = lax.axis_index("dp"), lax.axis_index("rep")
    core, z, y = dp % 2, (dp // 2) % NZ, dp // (2 * NZ)
    ring_place = jnp.where(core == 0, x, y)
    step = jnp.where((y * NZ + z) * NX + x < CHIPS // 2, 1, -1)
    place = jnp.stack([core, ring_place, step]).astype(jnp.int32)
    ids, order = cluster_ids.reshape(1, ROWS), member_order.reshape(1, ROWS)

    unit, box, slab, info = prep(place, embeddings, ids, order)
    chunk1 = exchange(box.reshape(CHIPS, SUB, D)).reshape(ROWS, D)
    handed = stamp(send(hand(place, unit, info, ids, order), SIBLING), slab)
    chunk2 = exchange(handed.reshape(CHIPS, SUB, WIDE)).reshape(ROWS, WIDE)

    arrays = {(0, 0): chunk1, (0, 1): chunk2}
    hold = {}
    for chunk, rows in enumerate((chunk1, chunk2)):
        hold["P", 0, chunk], hold["M", 0, chunk] = (rows, 0), (rows, HALF_ROWS)
        near = send(rows[:HALF_ROWS], ring(1)), send(rows[HALF_ROWS:], ring(-1))
        far = send(near[0], ring(1)), send(near[1], ring(-1))
        for part, one, two in zip("PM", near, far):
            hold[part, 1, chunk], hold[part, 2, chunk] = (one, 0), (two, 0)

    pairs, by_place = pair_lists()
    answers = []
    for stage in range(3):
        mine = [pair for pair in pairs if max(pair[0][1], pair[1][1]) == stage]
        table = [jnp.array([SLOT[a], SLOT[b]], jnp.int32) for a, b in mine]
        slots = {SLOT[block] for pair in mine for block in pair}
        if stage == 2:
            for low, high in by_place:
                table.append(
                    jnp.where(
                        ring_place < 2,
                        jnp.array([SLOT[block] for block in low], jnp.int32),
                        jnp.array([SLOT[block] for block in high], jnp.int32),
                    )
                )
                slots |= {SLOT[block] for block in low + high}
        arrays, loads = [], []

        def number_of(array):
            for number, known in enumerate(arrays):
                if known is array:
                    return number
            arrays.append(array)
            return len(arrays) - 1

        for slot in sorted(slots):
            part, far, chunk = BLOCKS[slot]
            array, first = hold[part, far, 1]
            load = (number_of(array), first, D, SLOT[part, far, 1])
            if load not in loads:
                loads.append(load)
        for slot in sorted(slots):
            array, first = hold[BLOCKS[slot]]
            loads.append((number_of(array), first, 0, slot))
        selfs = [SLOT[part, 0, chunk] for part in "PM" for chunk in range(2)] if stage == 0 else []
        answers.append(
            similar(
                arrays,
                loads,
                selfs,
                jnp.concatenate(table),
                len(table),
                slots,
                answers if stage == 2 else [],
                ("own", "near", "far")[stage],
            )
        )
    mine = exchange(answers[2].reshape(CHIPS, 1, 128)).reshape(CHIPS, 128)
    return answer(place, info, mine, send(mine, SIBLING)).reshape(ROWS)


def solution(mesh):
    return jax.shard_map(
        local,
        mesh=mesh,
        in_specs=(P(AXES, None), P(AXES), P(AXES)),
        out_specs=P(AXES),
        check_vma=False,
    )
```

time: 370 us -> 218 us (0.59)
  local copies, waits for them, and re-layouts: 72.6 us -> 7.7 us
  Pallas kernels: 0 us -> 56.7 us
  blocking collectives: 133 us -> 79.2 us
  waiting for transfers between devices: 89.9 us -> 46.7 us
  other arithmetic: 34.6 us -> 0.66 us
  starting transfers between devices: 6.19 us -> 26.1 us
  matrix products: 19.9 us -> 0 us
  between operations: 13.6 us -> 0.44 us
    all_gather x1 -> x0, waiting for transfers between devices: 85.7 us -> none  [local(): lax.all_gather(received[None], 'rep', axis=0, tiled=True)]
    pallas_call x0 -> x7, Pallas kernels: none -> 56.7 us  [the longest x3 40.7 us: similar(): pl.pallas_call(kernel, out_shape=jax.ShapeDtypeStruct((CHIPS, 128), jnp.f...]
    scatter x2 -> x0, local copies, waits for them, and re-layouts: 47.9 us -> none  [the longest x1 43.6 us: local(): members = jnp.zeros((held_slots, feature_count), jnp.bfloat16).at[all_pla...]
    all_to_all x2, blocking collectives: 110 us -> 79.2 us  [exchange(): lax.all_to_all(rows, AXES, split_axis=0, concat_axis=0, tiled=True, axis_...]
    all_to_all x1, waiting for transfers between devices: 4.26 us -> 34.4 us  [exchange(): lax.all_to_all(rows, AXES, split_axis=0, concat_axis=0, tiled=True, axis_...]
    gather x2 -> x0, local copies, waits for them, and re-layouts: 22.3 us -> none  [the longest x1 11.8 us: local(): answers = merged[jnp.minimum(received_place, held_slots - 1)]]
    dot_general x1 -> x0, matrix products: 19.9 us -> none  [local(): jnp.einsum('csd,ckd->csk', clusters, key_rows, preferred_element_type=jnp...]
    another operation x3 -> x4, other arithmetic: 18.2 us -> 0.66 us  [the longest x1 0.65 us: local(): place = jnp.stack([core, ring_place, step]).astype(jnp.int32)]
  transfers between devices with their start and end apart: 2 -> 11, of which waited for: 2 -> 4; matrix products, arithmetic and copies ran while one was open for 3% -> 2% of each run, Pallas kernels for 0% -> 13%
where the time goes in v1:
time: 218 us; the launch traced here: 217 us
  blocking collectives  79.2 us (36%)
  Pallas kernels  56.7 us (26%)
  waiting for transfers between devices  46.7 us (21%)
  starting transfers between devices  26.1 us (12%)
  local copies, waits for them, and re-layouts  7.7 us (4%)
    all_to_all x2, blocking collectives, exchange(): lax.all_to_all(rows, AXES, split_axis=0, concat_axis=0, tiled=True, axis_...  79.2 us
    pallas_call x3, Pallas kernels, similar(): pl.pallas_call(kernel, out_shape=jax.ShapeDtypeStruct((CHIPS, 128), jnp.f...  40.7 us
    all_to_all x1, waiting for transfers between devices, exchange(): lax.all_to_all(rows, AXES, split_axis=0, concat_axis=0, tiled=True, axis_...  34.4 us
    ppermute x10, starting transfers between devices, send(): return lax.ppermute(rows, AXES, pairs)  16.4 us
    ppermute x10, waiting for transfers between devices, send(): return lax.ppermute(rows, AXES, pairs)  12.3 us
    all_to_all x1, starting transfers between devices, exchange(): lax.all_to_all(rows, AXES, split_axis=0, concat_axis=0, tiled=True, axis_...  9.65 us
    pallas_call x1, Pallas kernels, prep(): pl.pallas_call(prep_kernel, out_shape=(jax.ShapeDtypeStruct((ROWS, D), jn...  5.56 us
    pallas_call x1, Pallas kernels, hand(): pl.pallas_call(hand_kernel, out_shape=jax.ShapeDtypeStruct((ROWS, WIDE),...  5.04 us
  transfers between devices with their start and end apart: 11, of which 4 were waited for; matrix products, arithmetic and copies ran while one was open for 2% of the time, Pallas kernels for 13%

profile of v1, /device:TPU:1, one launch (start us, length us, event | category | flops | bytes accessed | tf_op | source)
XLA Modules:
  0.0 217.5 jit_solution(16350548198856110410)
XLA Ops:
  0.0 0.6 pad_add_fusion.place_ref
  0.6 5.6 %prep.1 = (bf16[1024,768]{1,0:T(8,128)(2,1)}, bf16[1024,768]{1,0:T(8,128)(2,1)}, bf16[1024,128]{1,0:T(8,128)(2,1)}, s32[8,1024]{1,0:T(8,128)}) custom-call(s32[3]{0:T(128)} %pad_add_fusion.place_ref, bf16[1024,768]{1,0:T(8,128)(2,1)} %emb_ref.1, s32[1,1024]{1,0:T(1,128)} %bitcast.33, s32[1,1024]{1,0:T(1,128)} %bitcast.35), custom_call_target="tpu_custom_call" | custom-call | flops 1879048192 | bytes 4718592 | tf_op jit(solution)/shard_map/prep/pallas_call | solution.py:125
  6.2 5.0 %hand.1 = bf16[1024,896]{1,0:T(8,128)(2,1)} custom-call(s32[3]{0:T(128)} %pad_add_fusion.place_ref, bf16[1024,768]{1,0:T(8,128)(2,1)} %get-tuple-element.10.unit_ref, s32[8,1024]{1,0:T(8,128)} %get-tuple-element.9.info_ref, s32[1,1024]{1,0:T(1,128)} %bitcast.34, s32[1,1024]{1,0:T(1,128)} %bitcast.36), custom_call_target="tpu_custom_call" | custom-call | flops 1879048192 | bytes 3145728 | tf_op jit(solution)/shard_map/hand/pallas_call | solution.py:153
  11.2 3.2 %collective-permute-start = (bf16[1024,896]{1,0:T(8,128)(2,1)}, bf16[1024,896]{1,0:T(8,128)(2,1)S(1)}, u32[]{:S(2)}, u32[]{:S(2)}) collective-permute-start(bf16[1024,896]{1,0:T(8,128)(2,1)} %hand.1), channel_id=1, source_target_pairs={{0,4},{1,5},{2,6},{3,7},{4,0},{5,1},{6,2},{7,3},{8,12},{9,13},{10,... | collective-permute-start | bytes 5505032 | tf_op jit(solution)/shard_map/ppermute | solution.py:55
  14.5 3.6 %collective-permute-done.box_ref = bf16[1024,896]{1,0:T(8,128)(2,1)S(1)} collective-permute-done((bf16[1024,896]{1,0:T(8,128)(2,1)}, bf16[1024,896]{1,0:T(8,128)(2,1)S(1)}, u32[]{:S(2)}, u32[]{:S(2)}) %collective-permute-start) | collective-permute-done | bytes 1835040 | tf_op jit(solution)/shard_map/ppermute | solution.py:55
  18.1 1.3 copy-done.1
  19.4 1.8 stamp.1
  21.2 57.7 %all_to_all.15 = bf16[128,8,896]{2,1,0:T(8,128)(2,1)S(1)} all-to-all(bf16[128,8,896]{2,1,0:T(8,128)(2,1)} %bitcast.25), channel_id=1, replica_groups={{0,1,2,3,8,9,10,11,16,17,18,19,24,25,26,27,32,33,34,35,40,41,42,43,48,4..., dimensions={0} | all-to-all | bytes 3670016 | tf_op jit(solution)/shard_map/all_to_all | solution.py:49
  78.8 9.7 %all-to-all-start.1 = ((bf16[128,8,768]{2,1,0:T(8,128)(2,1)}), bf16[128,8,768]{2,1,0:T(8,128)(2,1)S(1)}, u32[]{:S(2)}, u32[]{:S(2)}) async-start(bf16[128,8,768]{2,1,0:T(8,128)(2,1)} %bitcast.29), calls=%async_computation.1 | async-start | bytes 3145728 | tf_op jit(solution)/shard_map/all_to_all | solution.py:49
  88.5 1.4 slice_bitcast_fusion
  89.9 0.0 copy-start.25
  89.9 0.0 copy-start.26
  89.9 0.0 copy-start.27
  89.9 0.0 copy-start.16
  90.0 0.0 copy-start.17
  90.0 0.0 copy-start.18
  90.0 0.0 copy-start.19
  90.0 0.0 copy-start.20
  90.0 0.0 copy-start.21
  90.0 0.0 copy-start.4
  90.0 0.0 copy-start.5
  90.0 0.0 copy-start.6
  90.1 0.0 copy-start.7
  90.1 0.0 copy-start.8
  90.1 0.0 copy-start.9
  90.1 0.0 copy-start.10
  90.1 0.0 copy-start.11
  90.1 0.0 copy-start.12
  90.1 0.0 copy-start.13
  90.1 0.0 copy-start.14
  90.2 0.0 copy-start.15
  90.2 2.4 %collective-permute-start.2 = (bf16[512,896]{1,0:T(8,128)(2,1)}, bf16[512,896]{1,0:T(8,128)(2,1)}, u32[]{:S(2)}, u32[]{:S(2)}) collective-permute-start(bf16[512,896]{1,0:T(8,128)(2,1)} %get-tuple-element.13), channel_id=1, source_target_pairs={{0,3},{4,196},{1,0},{5,197},{2,1},{6,198},{3,2},{7,199},{8,11},{12... | collective-permute-start | bytes 2752520 | tf_op jit(solution)/shard_map/ppermute | solution.py:55
  92.6 0.0 collective-permute-start.1
  92.6 34.4 %all-to-all-done.1 = bf16[128,8,768]{2,1,0:T(8,128)(2,1)S(1)} async-done(((bf16[128,8,768]{2,1,0:T(8,128)(2,1)}), bf16[128,8,768]{2,1,0:T(8,128)(2,1)S(1)}, u32[]{:S(2)}, u32[]{:S(2)}) %all-to-all-start.1) | async-done | bytes 1572896 | tf_op jit(solution)/shard_map/all_to_all | solution.py:49
  127.0 0.1 slice_bitcast_fusion.2
  127.1 0.7 collective-permute-start.7
  127.8 0.8 collective-permute-start.5
  128.7 0.6 concatenate.10.refs_1_
  129.3 0.6 concatenate.9.refs_1_
  130.1 0.6 concatenate.11.refs_1_
  130.7 7.7 %collective-permute-done.7.refs_7_ = bf16[512,768]{1,0:T(8,128)(2,1)} collective-permute-done((bf16[512,768]{1,0:T(8,128)(2,1)S(1)}, bf16[512,768]{1,0:T(8,128)(2,1)}, u32[]{:S(2)}, u32[]{:S(2)}) %collective-permute-start.7) | collective-permute-done | bytes 786464 | tf_op jit(solution)/shard_map/ppermute | solution.py:55
  138.4 1.9 collective-permute-start.8
  140.3 0.0 collective-permute-done.5.refs_6_.refs_8_
  140.3 0.0 collective-permute-start.6
  140.3 0.0 collective-permute-done.2.refs_4_
  140.3 2.7 %collective-permute-start.4 = (bf16[512,896]{1,0:T(8,128)(2,1)}, bf16[512,896]{1,0:T(8,128)(2,1)S(1)}, u32[]{:S(2)}, u32[]{:S(2)}) collective-permute-start(bf16[512,896]{1,0:T(8,128)(2,1)} %collective-permute-done.2.refs_4_), channel_id=1, source_target_pairs={{0,3},{4,196},{1,0},{5,197},{2,1},{6,198},{3,2},{7,199},{8,11},{12... | collective-permute-start | bytes 2752520 | tf_op jit(solution)/shard_map/ppermute | solution.py:55
  143.0 0.0 collective-permute-done.1.refs_3_
  143.0 0.0 collective-permute-start.3
  143.0 10.8 %own.1.refs_11_ = f32[128,128]{1,0:T(8,128)} custom-call(s32[4]{0:T(128)} %constant.140.clone.refs_0_, s32[12]{0:T(128)} %concatenate.10.refs_1_, bf16[1024,896]{1,0:T(8,128)(2,1)} %bitcast.22, bf16[1024,768]{1,0:T(8,128)(2,1)} %bitcast.26), custom_call_target="tpu_custom_call" | custom-call | flops 4026531840 | bytes 4718592 | tf_op jit(solution)/shard_map/own/pallas_call | solution.py:322
  153.8 17.0 %near.1.refs_12_ = f32[128,128]{1,0:T(8,128)} custom-call(s32[1]{0:T(128)} %constant.157.clone.refs_0_, s32[32]{0:T(128)} %concatenate.11.refs_1_, bf16[1024,896]{1,0:T(8,128)(2,1)} %bitcast.23, bf16[512,896]{1,0:T(8,128)(2,1)} %collective-permute-done.1.refs_3_, bf16[512,896]{1,0:T(8,128)(2,1)} %collective-permute-done.2.refs_4_, ...), custom_call_target="tpu_custom_call" | custom-call | flops 6442450944 | bytes 9437184 | tf_op jit(solution)/shard_map/near/pallas_call | solution.py:322
  170.9 0.0 collective-permute-done.8.refs_10_
  170.9 0.0 collective-permute-done.6.refs_9_
  170.9 0.0 collective-permute-done.4.refs_6_
  170.9 0.0 collective-permute-done.3.refs_5_
  170.9 0.8 copy-done.30
  171.7 0.4 copy-done.31
  172.1 0.2 copy-done.28
  172.3 0.9 copy-done.29
  173.3 12.8 %far.1 = f32[128,128]{1,0:T(8,128)} custom-call(s32[1]{0:T(128)} %constant.157.clone.refs_0_, s32[16]{0:T(128)} %concatenate.9.refs_1_, bf16[1024,896]{1,0:T(8,128)(2,1)} %bitcast.24, bf16[512,896]{1,0:T(8,128)(2,1)} %collective-permute-done.1.refs_3_, bf16[512,896]{1,0:T(8,128)(2,1)} %collective-permute-done.2.refs_4_, bf16[512,896]{1,0:T(8,128)(2,1)} %copy-done.29, ...), custom_call_target="tpu_custom_call" | custom-call | flops 3221225472 | bytes 13369344 | tf_op jit(solution)/shard_map/far/pallas_call | solution.py:322
  186.1 21.6 %all_to_all.16 = f32[128,1,128]{2,1,0:T(1,128)S(1)} all-to-all(f32[128,1,128]{2,1,0:T(1,128)} %bitcast.30), channel_id=1, replica_groups={{0,1,2,3,8,9,10,11,16,17,18,19,24,25,26,27,32,33,34,35,40,41,42,43,48,4..., dimensions={0} | all-to-all | bytes 131072 | tf_op jit(solution)/shard_map/all_to_all | solution.py:49
  207.7 4.7 %collective-permute-start.9 = (f32[128,128]{1,0:T(8,128)S(1)}, f32[128,128]{1,0:T(8,128)S(1)}, u32[]{:S(2)}, u32[]{:S(2)}) collective-permute-start(f32[128,128]{1,0:T(8,128)S(1)} %bitcast.31), channel_id=1, source_target_pairs={{0,4},{1,5},{2,6},{3,7},{4,0},{5,1},{6,2},{7,3},{8,12},{9,13},{10,... | collective-permute-start | bytes 196616 | tf_op jit(solution)/shard_map/ppermute | solution.py:55
  212.4 0.9 collective-permute-done.9.sibling_ref
  213.3 0.6 copy-done.32
  213.9 3.6 %answer.1 = f32[1,1024]{1,0:T(1,128)} custom-call(s32[3]{0:T(128)} %pad_add_fusion.place_ref, s32[8,1024]{1,0:T(8,128)} %get-tuple-element.9.info_ref, f32[128,128]{1,0:T(8,128)} %bitcast.32, f32[128,128]{1,0:T(8,128)} %copy-done.32), custom_call_target="tpu_custom_call" | custom-call | flops 1207959552 | bytes 196608 | tf_op jit(solution)/shard_map/answer/pallas_call | solution.py:374
  (44 shorter events, 0.1 us)
Async XLA Ops:
  11.2 6.9 %collective-permute-start = (bf16[1024,896]{1,0:T(8,128)(2,1)}, bf16[1024,896]{1,0:T(8,128)(2,1)S(1)}, u32[]{:S(2)}, u32[]{:S(2)}) collective-permute-start(bf16[1024,896]{1,0:T(8,128)(2,1)} %hand.1), channel_id=1, source_target_pairs={{0,4},{1,5},{2,6},{3,7},{4,0},{5,1},{6,2},{7,3},{8,12},{9,13},{10,... | collective-permute-start | bytes 5505032 | tf_op jit(solution)/shard_map/ppermute | solution.py:55
  18.1 1.3 copy-start.1
  78.8 11.1 %copy-start = (bf16[128,8,896]{2,1,0:T(8,128)(2,1)}, bf16[128,8,896]{2,1,0:T(8,128)(2,1)S(1)}, u32[]{:S(2)}) copy-start(bf16[128,8,896]{2,1,0:T(8,128)(2,1)S(1)} %all_to_all.15) | copy-start | bytes 5505028
  78.8 48.1 %all-to-all-start.1 = ((bf16[128,8,768]{2,1,0:T(8,128)(2,1)}), bf16[128,8,768]{2,1,0:T(8,128)(2,1)S(1)}, u32[]{:S(2)}, u32[]{:S(2)}) async-start(bf16[128,8,768]{2,1,0:T(8,128)(2,1)} %bitcast.29), calls=%async_computation.1 | async-start | bytes 3145728 | tf_op jit(solution)/shard_map/all_to_all | solution.py:49
  89.9 38.8 %copy-start.22 = (s32[2]{0:T(128)S(1)}, s32[2]{0:T(128)}, u32[]{:S(2)}) copy-start(s32[2]{0:T(128)} %constant.139.clone) | copy-start | bytes 28
  89.9 38.8 %copy-start.23 = (s32[2]{0:T(128)S(1)}, s32[2]{0:T(128)}, u32[]{:S(2)}) copy-start(s32[2]{0:T(128)} %constant.138.clone) | copy-start | bytes 28
  89.9 38.8 %copy-start.24 = (s32[2]{0:T(128)S(1)}, s32[2]{0:T(128)}, u32[]{:S(2)}) copy-start(s32[2]{0:T(128)} %constant.136.clone) | copy-start | bytes 28
  89.9 39.4 %copy-start.25 = (s32[2]{0:T(128)S(1)}, s32[2]{0:T(128)}, u32[]{:S(2)}) copy-start(s32[2]{0:T(128)} %constant.167.clone) | copy-start | bytes 28
  89.9 39.4 %copy-start.26 = (s32[2]{0:T(128)S(1)}, s32[2]{0:T(128)}, u32[]{:S(2)}) copy-start(s32[2]{0:T(128)} %constant.166.clone) | copy-start | bytes 28
  89.9 39.3 %copy-start.27 = (s32[2]{0:T(128)S(1)}, s32[2]{0:T(128)}, u32[]{:S(2)}) copy-start(s32[2]{0:T(128)} %constant.165.clone) | copy-start | bytes 28
  89.9 39.3 %copy-start.16 = (s32[2]{0:T(128)S(1)}, s32[2]{0:T(128)}, u32[]{:S(2)}) copy-start(s32[2]{0:T(128)} %constant.163.clone) | copy-start | bytes 28
  90.0 39.3 %copy-start.17 = (s32[2]{0:T(128)S(1)}, s32[2]{0:T(128)}, u32[]{:S(2)}) copy-start(s32[2]{0:T(128)} %constant.162.clone) | copy-start | bytes 28
  90.0 39.3 %copy-start.18 = (s32[2]{0:T(128)S(1)}, s32[2]{0:T(128)}, u32[]{:S(2)}) copy-start(s32[2]{0:T(128)} %constant.161.clone) | copy-start | bytes 28
  90.0 39.3 %copy-start.19 = (s32[2]{0:T(128)S(1)}, s32[2]{0:T(128)}, u32[]{:S(2)}) copy-start(s32[2]{0:T(128)} %constant.160.clone) | copy-start | bytes 28
  90.0 39.3 %copy-start.20 = (s32[2]{0:T(128)S(1)}, s32[2]{0:T(128)}, u32[]{:S(2)}) copy-start(s32[2]{0:T(128)} %constant.159.clone) | copy-start | bytes 28
  90.0 39.3 %copy-start.21 = (s32[2]{0:T(128)S(1)}, s32[2]{0:T(128)}, u32[]{:S(2)}) copy-start(s32[2]{0:T(128)} %constant.158.clone) | copy-start | bytes 28
  90.0 39.9 %copy-start.4 = (s32[2]{0:T(128)S(1)}, s32[2]{0:T(128)}, u32[]{:S(2)}) copy-start(s32[2]{0:T(128)} %constant.156.clone) | copy-start | bytes 28
  90.0 39.9 %copy-start.5 = (s32[2]{0:T(128)S(1)}, s32[2]{0:T(128)}, u32[]{:S(2)}) copy-start(s32[2]{0:T(128)} %constant.155.clone) | copy-start | bytes 28
  90.0 39.9 %copy-start.6 = (s32[2]{0:T(128)S(1)}, s32[2]{0:T(128)}, u32[]{:S(2)}) copy-start(s32[2]{0:T(128)} %constant.154.clone) | copy-start | bytes 28
  90.1 39.9 %copy-start.7 = (s32[2]{0:T(128)S(1)}, s32[2]{0:T(128)}, u32[]{:S(2)}) copy-start(s32[2]{0:T(128)} %constant.153.clone) | copy-start | bytes 28
  90.1 39.9 %copy-start.8 = (s32[2]{0:T(128)S(1)}, s32[2]{0:T(128)}, u32[]{:S(2)}) copy-start(s32[2]{0:T(128)} %constant.152.clone) | copy-start | bytes 28
  90.1 39.9 %copy-start.9 = (s32[2]{0:T(128)S(1)}, s32[2]{0:T(128)}, u32[]{:S(2)}) copy-start(s32[2]{0:T(128)} %constant.151.clone) | copy-start | bytes 28
  90.1 39.9 %copy-start.10 = (s32[2]{0:T(128)S(1)}, s32[2]{0:T(128)}, u32[]{:S(2)}) copy-start(s32[2]{0:T(128)} %constant.148.clone) | copy-start | bytes 28
  90.1 39.9 %copy-start.11 = (s32[2]{0:T(128)S(1)}, s32[2]{0:T(128)}, u32[]{:S(2)}) copy-start(s32[2]{0:T(128)} %constant.147.clone) | copy-start | bytes 28
  90.1 39.9 %copy-start.12 = (s32[2]{0:T(128)S(1)}, s32[2]{0:T(128)}, u32[]{:S(2)}) copy-start(s32[2]{0:T(128)} %constant.146.clone) | copy-start | bytes 28
  90.1 39.9 %copy-start.13 = (s32[2]{0:T(128)S(1)}, s32[2]{0:T(128)}, u32[]{:S(2)}) copy-start(s32[2]{0:T(128)} %constant.145.clone) | copy-start | bytes 28
  90.1 39.9 %copy-start.14 = (s32[2]{0:T(128)S(1)}, s32[2]{0:T(128)}, u32[]{:S(2)}) copy-start(s32[2]{0:T(128)} %constant.144.clone) | copy-start | bytes 28
  90.2 39.9 %copy-start.15 = (s32[2]{0:T(128)S(1)}, s32[2]{0:T(128)}, u32[]{:S(2)}) copy-start(s32[2]{0:T(128)} %constant.143.clone) | copy-start | bytes 28
  90.2 50.1 %collective-permute-start.2 = (bf16[512,896]{1,0:T(8,128)(2,1)}, bf16[512,896]{1,0:T(8,128)(2,1)}, u32[]{:S(2)}, u32[]{:S(2)}) collective-permute-start(bf16[512,896]{1,0:T(8,128)(2,1)} %get-tuple-element.13), channel_id=1, source_target_pairs={{0,3},{4,196},{1,0},{5,197},{2,1},{6,198},{3,2},{7,199},{8,11},{12... | collective-permute-start | bytes 2752520 | tf_op jit(solution)/shard_map/ppermute | solution.py:55
  92.6 50.4 %collective-permute-start.1 = (bf16[512,896]{1,0:T(8,128)(2,1)}, bf16[512,896]{1,0:T(8,128)(2,1)}, u32[]{:S(2)}, u32[]{:S(2)}) collective-permute-start(bf16[512,896]{1,0:T(8,128)(2,1)} %get-tuple-element.14), channel_id=1, source_target_pairs={{0,1},{4,68},{1,2},{5,69},{2,3},{6,70},{3,0},{7,71},{8,9},{12,76},... | collective-permute-start | bytes 2752520 | tf_op jit(solution)/shard_map/ppermute | solution.py:55
  127.0 16.0 %copy-start.2 = (bf16[128,8,768]{2,1,0:T(8,128)(2,1)}, bf16[128,8,768]{2,1,0:T(8,128)(2,1)S(1)}, u32[]{:S(2)}) copy-start(bf16[128,8,768]{2,1,0:T(8,128)(2,1)S(1)} %all-to-all-done.1) | copy-start | bytes 4718596
  127.1 11.3 %collective-permute-start.7 = (bf16[512,768]{1,0:T(8,128)(2,1)S(1)}, bf16[512,768]{1,0:T(8,128)(2,1)}, u32[]{:S(2)}, u32[]{:S(2)}) collective-permute-start(bf16[512,768]{1,0:T(8,128)(2,1)S(1)} %get-tuple-element.15), channel_id=1, source_target_pairs={{0,3},{4,196},{1,0},{5,197},{2,1},{6,198},{3,2},{7,199},{8,11},{12... | collective-permute-start | bytes 2359304 | tf_op jit(solution)/shard_map/ppermute | solution.py:55
  127.8 12.5 %collective-permute-start.5 = (bf16[512,768]{1,0:T(8,128)(2,1)S(1)}, bf16[512,768]{1,0:T(8,128)(2,1)}, u32[]{:S(2)}, u32[]{:S(2)}) collective-permute-start(bf16[512,768]{1,0:T(8,128)(2,1)S(1)} %get-tuple-element.16), channel_id=1, source_target_pairs={{0,1},{4,68},{1,2},{5,69},{2,3},{6,70},{3,0},{7,71},{8,9},{12,76},... | collective-permute-start | bytes 2359304 | tf_op jit(solution)/shard_map/ppermute | solution.py:55
  138.4 32.5 %collective-permute-start.8 = (bf16[512,768]{1,0:T(8,128)(2,1)}, bf16[512,768]{1,0:T(8,128)(2,1)S(1)}, u32[]{:S(2)}, u32[]{:S(2)}) collective-permute-start(bf16[512,768]{1,0:T(8,128)(2,1)} %collective-permute-done.7.refs_7_), channel_id=1, source_target_pairs={{0,3},{4,196},{1,0},{5,197},{2,1},{6,198},{3,2},{7,199},{8,11},{12... | collective-permute-start | bytes 2359304 | tf_op jit(solution)/shard_map/ppermute | solution.py:55
  140.3 30.6 %collective-permute-start.6 = (bf16[512,768]{1,0:T(8,128)(2,1)}, bf16[512,768]{1,0:T(8,128)(2,1)S(1)}, u32[]{:S(2)}, u32[]{:S(2)}) collective-permute-start(bf16[512,768]{1,0:T(8,128)(2,1)} %collective-permute-done.5.refs_6_.refs_8_), channel_id=1, source_target_pairs={{0,1},{4,68},{1,2},{5,69},{2,3},{6,70},{3,0},{7,71},{8,9},{12,76},... | collective-permute-start | bytes 2359304 | tf_op jit(solution)/shard_map/ppermute | solution.py:55
  140.3 30.6 %collective-permute-start.4 = (bf16[512,896]{1,0:T(8,128)(2,1)}, bf16[512,896]{1,0:T(8,128)(2,1)S(1)}, u32[]{:S(2)}, u32[]{:S(2)}) collective-permute-start(bf16[512,896]{1,0:T(8,128)(2,1)} %collective-permute-done.2.refs_4_), channel_id=1, source_target_pairs={{0,3},{4,196},{1,0},{5,197},{2,1},{6,198},{3,2},{7,199},{8,11},{12... | collective-permute-start | bytes 2752520 | tf_op jit(solution)/shard_map/ppermute | solution.py:55
  143.0 27.9 %collective-permute-start.3 = (bf16[512,896]{1,0:T(8,128)(2,1)}, bf16[512,896]{1,0:T(8,128)(2,1)S(1)}, u32[]{:S(2)}, u32[]{:S(2)}) collective-permute-start(bf16[512,896]{1,0:T(8,128)(2,1)} %collective-permute-done.1.refs_3_), channel_id=1, source_target_pairs={{0,1},{4,68},{1,2},{5,69},{2,3},{6,70},{3,0},{7,71},{8,9},{12,76},... | collective-permute-start | bytes 2752520 | tf_op jit(solution)/shard_map/ppermute | solution.py:55
  170.9 0.9 copy-start.30
  170.9 1.2 copy-start.31
  170.9 1.4 copy-start.28
  172.3 1.0 copy-start.29
  207.7 5.6 %copy-start.3 = (f32[128,1,128]{2,1,0:T(1,128)}, f32[128,1,128]{2,1,0:T(1,128)S(1)}, u32[]{:S(2)}) copy-start(f32[128,1,128]{2,1,0:T(1,128)S(1)} %all_to_all.16) | copy-start | bytes 196612
  207.7 5.6 %collective-permute-start.9 = (f32[128,128]{1,0:T(8,128)S(1)}, f32[128,128]{1,0:T(8,128)S(1)}, u32[]{:S(2)}, u32[]{:S(2)}) collective-permute-start(f32[128,128]{1,0:T(8,128)S(1)} %bitcast.31), channel_id=1, source_target_pairs={{0,4},{1,5},{2,6},{3,7},{4,0},{5,1},{6,2},{7,3},{8,12},{9,13},{10,... | collective-permute-start | bytes 196616 | tf_op jit(solution)/shard_map/ppermute | solution.py:55
  213.3 0.6 copy-start.32

commit v2 on v1

--- a/solution.py
+++ b/solution.py
@@ -20,7 +20,8 @@
 WIDE = D + KEYS
 HALF_ROWS = 512
 ORDERS = 4096
-VMEM = 56 * 1024 * 1024
+VMEM = 24 * 1024 * 1024
+FULL = 56 * 1024 * 1024
 
 
 def device(x, y, z, core):
@@ -132,7 +133,7 @@
         ),
         in_specs=[pl.BlockSpec(memory_space=pltpu.SMEM)] + [pl.BlockSpec(memory_space=pltpu.VMEM)] * 3,
         out_specs=tuple([pl.BlockSpec(memory_space=pltpu.VMEM)] * 4),
-        compiler_params=pltpu.CompilerParams(vmem_limit_bytes=VMEM),
+        compiler_params=pltpu.CompilerParams(vmem_limit_bytes=FULL),
         cost_estimate=cost(2 * ROWS * ROWS * WIDE, 6 * ROWS * D),
         name="prep",
     )(place, embeddings, ids, order)
@@ -183,11 +184,10 @@
 
 
 BLOCKS = [(part, far, chunk) for far in range(3) for chunk in range(2) for part in "PM"]
-SLOT = {block: number for number, block in enumerate(BLOCKS)}
 
 
 def pair_lists():
-    pairs, by_place = [], []
+    pairs = []
 
     def all_chunks(one, other):
         for c in range(2):
@@ -198,9 +198,6 @@
         pairs.append(((part, 0, 0), (part, 0, 1)))
         all_chunks((part, 0), (part, 1))
         pairs.append(((part, 0, 1), (part, 2, 0)))
-        early = ((part, 0, 0), (part, 2, 0))
-        late = ((part, 0, 1), (part, 2, 1))
-        by_place.append((early, late) if part == "P" else (late, early))
     all_chunks(("P", 0), ("M", 0))
     all_chunks(("P", 0), ("M", 1))
     all_chunks(("P", 1), ("M", 1))
@@ -208,25 +205,36 @@
     pairs.append((("P", 1, 1), ("M", 2, 0)))
     pairs.append((("P", 2, 0), ("M", 1, 1)))
     pairs.append((("P", 1, 1), ("M", 2, 1)))
+    by_place = [
+        ((("P", 0, 0), ("P", 2, 0)), (("M", 0, 0), ("M", 2, 0))),
+        ((("M", 0, 1), ("M", 2, 1)), (("P", 0, 1), ("P", 2, 1))),
+    ]
     return pairs, by_place
 
 
-def similar_kernel(loads, used, n_self, n_pairs, n_before, *refs):
+def stage_of(pair):
+    if all(far == 0 for part, far, chunk in pair):
+        return 0
+    return 2 if any(far == 2 and chunk == 1 for part, far, chunk in pair) else 1
+
+
+def similar_kernel(blocks, loads, n_tasks, n_before, *refs):
     n_arrays = 1 + max(load[0] for load in loads)
-    selfs_ref, pairs_ref = refs[:2]
-    arrays = refs[2 : 2 + n_arrays]
-    befores = refs[2 + n_arrays : 2 + n_arrays + n_before]
-    out_ref = refs[2 + n_arrays + n_before]
-    rows, slabs, kcol, ccol, krow, crow, best_row, best_col, sems = refs[3 + n_arrays + n_before :]
+    tasks_ref = refs[0]
+    arrays = refs[1 : 1 + n_arrays]
+    befores = refs[1 + n_arrays : 1 + n_arrays + n_before]
+    out_ref = refs[1 + n_arrays + n_before]
+    rows, slabs, kcol, ccol, krow, crow, best_row, best_col, s0, s1, sems = refs[2 + n_arrays + n_before :]
+    n_blocks = len(blocks)
 
     copies = []
-    for number, (array, first, columns, slot) in enumerate(loads):
-        source = arrays[array].at[pl.ds(first, HALF_ROWS), pl.ds(columns, KEYS if columns else D)]
-        target = slabs.at[slot] if columns else rows.at[slot]
+    for number, (array, first, columns, is_key, slot) in enumerate(loads):
+        source = arrays[array].at[pl.ds(first, HALF_ROWS), pl.ds(columns, KEYS if is_key else D)]
+        target = slabs.at[slot] if is_key else rows.at[slot]
         copy = pltpu.make_async_copy(source, target, sems.at[number])
         copy.start()
-        copies.append((copy, bool(columns)))
-    for slot in used:
+        copies.append((copy, is_key))
+    for slot in range(n_blocks):
         best_row[slot] = jnp.full((HALF_ROWS, 128), -1.0, jnp.float32)
         best_col[slot] = jnp.full((8, HALF_ROWS), -1.0, jnp.float32)
     for copy, is_key in copies:
@@ -235,10 +243,9 @@
 
     lane_of = lax.broadcasted_iota(jnp.int32, (KEYS, 128), 0)
     row_of = lax.broadcasted_iota(jnp.int32, (8, KEYS), 1)
-    for slot in used:
-        part, far, chunk = BLOCKS[slot]
+    for slot, (part, far, chunk) in enumerate(blocks):
         first = 0 if chunk == 1 else 2
-        slab = slabs[SLOT[(part, far, 1)]]
+        slab = slabs[slot]
         weight = jnp.where(lane_of == first, 128.0, jnp.where(lane_of == first + 1, 1.0, 0.0)).astype(jnp.bfloat16)
         key = jnp.dot(slab, weight, preferred_element_type=jnp.float32)
         kcol[slot] = key
@@ -251,98 +258,115 @@
         if not is_key:
             copy.wait()
 
-    width = 256
-
-    def products(a, b, start):
-        return lax.dot_general(
-            rows[a], rows[b, start : start + width], (((1,), (1,)), ((), ())), preferred_element_type=jnp.float32
-        )
-
-    def one_self(number, carry):
-        a = selfs_ref[number]
-        ka, ca = kcol[a], ccol[a]
-        best = best_row[a]
-        for start in range(0, HALF_ROWS, width):
-            s = products(a, a, start)
-            for lane in range(0, width, 128):
-                at = start + lane
-                kb, cb = krow[a, 0:1, at : at + 128], crow[a, 0:1, at : at + 128]
-                best = jnp.maximum(
-                    best, jnp.where((ca == cb) & (kb < ka), s[:, lane : lane + 128], -1.0)
-                )
-        best_row[a] = best
+    def multiply(task, s):
+        a, b = tasks_ref[3 * task], tasks_ref[3 * task + 1]
+        s[...] = lax.dot_general(rows[a], rows[b], (((1,), (1,)), ((), ())), preferred_element_type=jnp.float32)
+
+    step = 16
+
+    def reduce(task, s):
+        a, b, sink = tasks_ref[3 * task], tasks_ref[3 * task + 1], tasks_ref[3 * task + 2]
+        kb, cb = krow[b], crow[b]
+        for row in range(0, HALF_ROWS, step):
+            ka = kcol[a, row : row + step].reshape(step // 8, 8, 128)
+            ca = ccol[a, row : row + step].reshape(step // 8, 8, 128)
+            best = best_row[a, row : row + step]
+            for at in range(0, HALF_ROWS, 128):
+                found = s[row : row + step, at : at + 128].reshape(step // 8, 8, 128)
+                same = jnp.where(ca == cb[None, :, at : at + 128], found, -1.0)
+                later = kb[None, :, at : at + 128] < ka
+                best = jnp.maximum(best, jnp.where(later, same, -1.0).reshape(step, 128))
+                other = jnp.max(jnp.where(later, -1.0, same), axis=0)
+                best_col[sink, :, at : at + 128] = jnp.maximum(best_col[sink, :, at : at + 128], other)
+            best_row[a, row : row + step] = best
+
+    def two(turn, carry):
+        multiply(2 * turn + 1, s1)
+        reduce(2 * turn, s0)
+        multiply(2 * turn + 2, s0)
+        reduce(2 * turn + 1, s1)
         return carry
 
-    def one_pair(number, carry):
-        a, b = pairs_ref[2 * number], pairs_ref[2 * number + 1]
-        ka, ca = kcol[a], ccol[a]
-        best = best_row[a]
-        for start in range(0, HALF_ROWS, width):
-            s = products(a, b, start)
-            for lane in range(0, width, 128):
-                at = start + lane
-                kb, cb = krow[b, 0:1, at : at + 128], crow[b, 0:1, at : at + 128]
-                same = jnp.where(ca == cb, s[:, lane : lane + 128], -1.0)
-                later = kb < ka
-                best = jnp.maximum(best, jnp.where(later, same, -1.0))
-                other = jnp.where(later, -1.0, same).reshape(HALF_ROWS // 8, 8, 128)
-                best_col[b, :, at : at + 128] = jnp.maximum(
-                    best_col[b, :, at : at + 128], jnp.max(other, axis=0)
-                )
-        best_row[a] = best
-        return carry
-
-    if n_self:
-        lax.fori_loop(0, n_self, one_self, 0)
-    lax.fori_loop(0, n_pairs, one_pair, 0)
-
-    halves = {}
-    sub = lax.broadcasted_iota(jnp.int32, (HALF_ROWS // SUB, SUB, 128), 1)
-    lane = lax.broadcasted_iota(jnp.int32, (HALF_ROWS // SUB, SUB, 128), 2)
-    for slot in used:
-        part, far, chunk = BLOCKS[slot]
-        by_row = jnp.max(best_row[slot], axis=1, keepdims=True)
-        by_col = jnp.max(best_col[slot], axis=0, keepdims=True)
-        by_col = jnp.transpose(jnp.broadcast_to(by_col, (128, HALF_ROWS)))
-        value = jnp.maximum(by_col, by_row).reshape(HALF_ROWS // SUB, SUB, 128)
-        value = jnp.max(jnp.where(lane == sub + (far * 16 + chunk * SUB), value, -1.0), axis=1)
-        halves[part] = jnp.maximum(halves[part], value) if part in halves else value
+    multiply(0, s0)
+    if n_tasks > 2:
+        lax.fori_loop(0, n_tasks // 2 - 1, two, 0)
+    multiply(n_tasks - 1, s1)
+    reduce(n_tasks - 2, s0)
+    reduce(n_tasks - 1, s1)
+
+    empty = jnp.full((8, HALF_ROWS), -1.0, jnp.float32)
+    diagonal = lax.broadcasted_iota(jnp.int32, (8, HALF_ROWS), 0) == (
+        lax.broadcasted_iota(jnp.int32, (8, HALF_ROWS), 1) & (SUB - 1)
+    )
     for number, part in enumerate("PM"):
+        tiles = [empty] * 16
+        for slot, (its, far, chunk) in enumerate(blocks):
+            if its == part:
+                by_row = jnp.max(jnp.transpose(best_row[slot]), axis=0, keepdims=True)
+                by_col = jnp.max(best_col[slot], axis=0, keepdims=True)
+                tiles[2 * far + chunk] = jnp.where(diagonal, jnp.maximum(by_row, by_col), -1.0)
+        value = jnp.transpose(jnp.concatenate(tiles, axis=0)).reshape(HALF_ROWS // SUB, SUB, 128)
+        value = jnp.max(value, axis=1)
         at = pl.ds(number * (CHIPS // 2), CHIPS // 2)
-        value = halves[part]
         for before in befores:
             value = jnp.maximum(value, before[at, :])
         out_ref[at, :] = value
 
 
-def similar(arrays, loads, selfs, pairs, n_pairs, slots, befores, name):
-    n_blocks = len(BLOCKS)
-    used = sorted(slots)
-    kernel = functools.partial(similar_kernel, loads, used, len(selfs), n_pairs, len(befores))
+def similar(hold, keys, low, high, ring_place, befores, name):
+    blocks = [block for block in BLOCKS if any(block in pair for pair in low + high)]
+    place = {block: number for number, block in enumerate(blocks)}
+    spare = len(blocks)
+
+    def table(pairs):
+        return np.array(
+            [(place[a], place[b], spare if a == b else place[b]) for a, b in pairs], np.int32
+        ).reshape(-1)
+
+    tasks = jnp.asarray(table(low))
+    if low != high:
+        tasks = jnp.where(ring_place < 2, tasks, jnp.asarray(table(high)))
+    arrays, loads = [], []
+
+    def number_of(array):
+        for number, known in enumerate(arrays):
+            if known is array:
+                return number
+        arrays.append(array)
+        return len(arrays) - 1
+
+    for block in blocks:
+        array, first, column = keys[block[:2]]
+        loads.append((number_of(array), first, column, True, place[block]))
+    for block in blocks:
+        array, first = hold[block]
+        loads.append((number_of(array), first, 0, False, place[block]))
+    n = len(blocks)
+    kernel = functools.partial(similar_kernel, blocks, loads, len(low), len(befores))
     return pl.pallas_call(
         kernel,
         out_shape=jax.ShapeDtypeStruct((CHIPS, 128), jnp.float32),
-        in_specs=[pl.BlockSpec(memory_space=pltpu.SMEM)] * 2
+        in_specs=[pl.BlockSpec(memory_space=pltpu.SMEM)]
         + [pl.BlockSpec(memory_space=pl.ANY)] * len(arrays)
         + [pl.BlockSpec(memory_space=pltpu.VMEM)] * len(befores),
         out_specs=pl.BlockSpec(memory_space=pltpu.VMEM),
         scratch_shapes=[
-            pltpu.VMEM((n_blocks, HALF_ROWS, D), jnp.bfloat16),
-            pltpu.VMEM((n_blocks, HALF_ROWS, KEYS), jnp.bfloat16),
-            pltpu.VMEM((n_blocks, HALF_ROWS, 128), jnp.float32),
-            pltpu.VMEM((n_blocks, HALF_ROWS, 128), jnp.float32),
-            pltpu.VMEM((n_blocks, 8, HALF_ROWS), jnp.float32),
-            pltpu.VMEM((n_blocks, 8, HALF_ROWS), jnp.float32),
-            pltpu.VMEM((n_blocks, HALF_ROWS, 128), jnp.float32),
-            pltpu.VMEM((n_blocks, 8, HALF_ROWS), jnp.float32),
+            pltpu.VMEM((n, HALF_ROWS, D), jnp.bfloat16),
+            pltpu.VMEM((n, HALF_ROWS, KEYS), jnp.bfloat16),
+            pltpu.VMEM((n, HALF_ROWS, 128), jnp.float32),
+            pltpu.VMEM((n, HALF_ROWS, 128), jnp.float32),
+            pltpu.VMEM((n, 8, HALF_ROWS), jnp.float32),
+            pltpu.VMEM((n, 8, HALF_ROWS), jnp.float32),
+            pltpu.VMEM((n, HALF_ROWS, 128), jnp.float32),
+            pltpu.VMEM((n + 1, 8, HALF_ROWS), jnp.float32),
+            pltpu.VMEM((HALF_ROWS, HALF_ROWS), jnp.float32),
+            pltpu.VMEM((HALF_ROWS, HALF_ROWS), jnp.float32),
             pltpu.SemaphoreType.DMA((len(loads),)),
         ],
-        compiler_params=pltpu.CompilerParams(vmem_limit_bytes=VMEM),
-        cost_estimate=cost(
-            2 * D * HALF_ROWS * HALF_ROWS * (n_pairs + len(selfs)), 2 * len(loads) * HALF_ROWS * D
-        ),
+        compiler_params=pltpu.CompilerParams(vmem_limit_bytes=32 * 1024 * 1024),
+        cost_estimate=cost(2 * D * HALF_ROWS * HALF_ROWS * len(low), 2 * len(loads) * HALF_ROWS * D),
         name=name,
-    )(jnp.array(selfs or [0], jnp.int32), pairs, *arrays, *befores)
+    )(tasks, *arrays, *befores)
 
 
 def answer_kernel(place_ref, info_ref, mine_ref, sibling_ref, out_ref):
@@ -353,16 +377,21 @@
     device_of = lax.broadcasted_iota(jnp.int32, (2 * CHIPS, ROWS), 0)
     lane_of = lax.broadcasted_iota(jnp.int32, (128, ROWS), 0)
     best = jnp.full((1, ROWS), -1.0, jnp.float32)
+    parts = []
+    rest = values
+    for piece in range(3):
+        parts.append(rest.astype(jnp.bfloat16))
+        rest = rest - parts[-1].astype(jnp.float32)
+    parts = jnp.concatenate(parts, axis=0)
     for far in range(3):
         chip, serving = chip_of(group, (rank + far * step) & 3)
         away = (serving != core).astype(jnp.int32)
-        pick = jnp.where(device_of == chip + CHIPS * away, 1.0, 0.0)
+        pick = jnp.where(device_of == chip + CHIPS * away, 1.0, 0.0).astype(jnp.bfloat16)
         found = lax.dot_general(
-            values,
-            pick,
+            parts,
+            jnp.concatenate([pick] * 3, axis=0),
             (((0,), (0,)), ((), ())),
             preferred_element_type=jnp.float32,
-            precision=lax.Precision.HIGHEST,
         )
         wanted = far * 16 + away * SUB + (rank >> 2)
         found = jnp.max(jnp.where(lane_of == wanted, found, -1.0), axis=0, keepdims=True)
@@ -393,64 +422,41 @@
     unit, box, slab, info = prep(place, embeddings, ids, order)
     chunk1 = exchange(box.reshape(CHIPS, SUB, D)).reshape(ROWS, D)
     handed = stamp(send(hand(place, unit, info, ids, order), SIBLING), slab)
+    chunk1, handed = lax.optimization_barrier((chunk1, handed))
     chunk2 = exchange(handed.reshape(CHIPS, SUB, WIDE)).reshape(ROWS, WIDE)
-
-    arrays = {(0, 0): chunk1, (0, 1): chunk2}
-    hold = {}
-    for chunk, rows in enumerate((chunk1, chunk2)):
-        hold["P", 0, chunk], hold["M", 0, chunk] = (rows, 0), (rows, HALF_ROWS)
-        near = send(rows[:HALF_ROWS], ring(1)), send(rows[HALF_ROWS:], ring(-1))
-        far = send(near[0], ring(1)), send(near[1], ring(-1))
-        for part, one, two in zip("PM", near, far):
-            hold[part, 1, chunk], hold[part, 2, chunk] = (one, 0), (two, 0)
+    near1 = send(chunk1[:HALF_ROWS], ring(1)), send(chunk1[HALF_ROWS:], ring(-1))
+    far1 = send(near1[0], ring(1)), send(near1[1], ring(-1))
+    chunk2, near1, far1 = lax.optimization_barrier((chunk2, near1, far1))
+    near2 = send(chunk2[:HALF_ROWS], ring(1)), send(chunk2[HALF_ROWS:], ring(-1))
+    far_keys = send(chunk2[:, D:], ring(2))
+
+    hold, keys = {}, {}
+    for half, part in enumerate("PM"):
+        first = half * HALF_ROWS
+        hold[part, 0, 0], hold[part, 0, 1] = (chunk1, first), (chunk2, first)
+        hold[part, 1, 0], hold[part, 2, 0] = (near1[half], 0), (far1[half], 0)
+        keys[part, 0], keys[part, 2] = (chunk2, first, D), (far_keys, first, 0)
 
     pairs, by_place = pair_lists()
     answers = []
     for stage in range(3):
-        mine = [pair for pair in pairs if max(pair[0][1], pair[1][1]) == stage]
-        table = [jnp.array([SLOT[a], SLOT[b]], jnp.int32) for a, b in mine]
-        slots = {SLOT[block] for pair in mine for block in pair}
-        if stage == 2:
-            for low, high in by_place:
-                table.append(
-                    jnp.where(
-                        ring_place < 2,
-                        jnp.array([SLOT[block] for block in low], jnp.int32),
-                        jnp.array([SLOT[block] for block in high], jnp.int32),
-                    )
-                )
-                slots |= {SLOT[block] for block in low + high}
-        arrays, loads = [], []
-
-        def number_of(array):
-            for number, known in enumerate(arrays):
-                if known is array:
-                    return number
-            arrays.append(array)
-            return len(arrays) - 1
-
-        for slot in sorted(slots):
-            part, far, chunk = BLOCKS[slot]
-            array, first = hold[part, far, 1]
-            load = (number_of(array), first, D, SLOT[part, far, 1])
-            if load not in loads:
-                loads.append(load)
-        for slot in sorted(slots):
-            array, first = hold[BLOCKS[slot]]
-            loads.append((number_of(array), first, 0, slot))
-        selfs = [SLOT[part, 0, chunk] for part in "PM" for chunk in range(2)] if stage == 0 else []
+        low = [pair for pair in pairs if stage_of(pair) == stage]
+        if stage == 0:
+            low += [((part, 0, chunk),) * 2 for part in "PM" for chunk in range(2)]
+        high = list(low)
+        for one, other in by_place:
+            if stage_of(one) == stage:
+                low.append(one)
+                high.append(other)
         answers.append(
-            similar(
-                arrays,
-                loads,
-                selfs,
-                jnp.concatenate(table),
-                len(table),
-                slots,
-                answers if stage == 2 else [],
-                ("own", "near", "far")[stage],
-            )
+            similar(hold, keys, low, high, ring_place, answers if stage == 2 else [], ("own", "near", "far")[stage])
         )
+        if stage == 0:
+            near2, answers[0] = lax.optimization_barrier((near2, answers[0]))
+            far2 = send(near2[0], ring(1)), send(near2[1], ring(-1))
+            for half, part in enumerate("PM"):
+                hold[part, 1, 1], hold[part, 2, 1] = (near2[half], 0), (far2[half], 0)
+                keys[part, 1] = (near2[half], 0, D)
     mine = exchange(answers[2].reshape(CHIPS, 1, 128)).reshape(CHIPS, 128)
     return answer(place, info, mine, send(mine, SIBLING)).reshape(ROWS)
 

time: 218 us -> 186 us (0.85)
  blocking collectives: 79.2 us -> 22 us
  waiting for transfers between devices: 46.7 us -> 75.2 us
  Pallas kernels: 56.7 us -> 38.9 us
  starting transfers between devices: 26.1 us -> 41.6 us
    all_to_all x2 -> x1, blocking collectives: 79.2 us -> 22 us  [exchange(): lax.all_to_all(rows, AXES, split_axis=0, concat_axis=0, tiled=True, axis_...]
    ppermute x10 -> x11, waiting for transfers between devices: 12.3 us -> 43.6 us  [send(): return lax.ppermute(rows, AXES, pairs)]
    all_to_all x1 -> x2, starting transfers between devices: 9.65 us -> 25.4 us  [exchange(): lax.all_to_all(rows, AXES, split_axis=0, concat_axis=0, tiled=True, axis_...]
    pallas_call x3, Pallas kernels: 40.7 us -> 28 us  [similar(): pl.pallas_call(kernel, out_shape=jax.ShapeDtypeStruct((CHIPS, 128), jnp.f...]
    all_to_all x1 -> x2, waiting for transfers between devices: 34.4 us -> 31.6 us  [exchange(): lax.all_to_all(rows, AXES, split_axis=0, concat_axis=0, tiled=True, axis_...]
    unnamed x66 -> x40, local copies, waits for them, and re-layouts: 4.4 us -> 4.88 us
    ppermute x10 -> x11, starting transfers between devices: 16.4 us -> 16.2 us  [send(): return lax.ppermute(rows, AXES, pairs)]
  transfers between devices with their start and end apart: 11 -> 13, of which waited for: 4 -> 7; matrix products, arithmetic and copies ran while one was open for 2% -> 0% of each run, Pallas kernels for 13% -> 15%
where the time goes in v2:
time: 186 us; the launch traced here: 185 us
  waiting for transfers between devices  75.2 us (40%)
  starting transfers between devices  41.6 us (22%)
  Pallas kernels  38.9 us (21%)
  blocking collectives  22 us (12%)
  local copies, waits for them, and re-layouts  6.37 us (3%)
    ppermute x11, waiting for transfers between devices, send(): return lax.ppermute(rows, AXES, pairs)  43.6 us
    all_to_all x2, waiting for transfers between devices, exchange(): lax.all_to_all(rows, AXES, split_axis=0, concat_axis=0, tiled=True, axis_...  31.6 us
    pallas_call x3, Pallas kernels, similar(): pl.pallas_call(kernel, out_shape=jax.ShapeDtypeStruct((CHIPS, 128), jnp.f...  28 us
    all_to_all x2, starting transfers between devices, exchange(): lax.all_to_all(rows, AXES, split_axis=0, concat_axis=0, tiled=True, axis_...  25.4 us
    all_to_all x1, blocking collectives, exchange(): lax.all_to_all(rows, AXES, split_axis=0, concat_axis=0, tiled=True, axis_...  22 us
    ppermute x11, starting transfers between devices, send(): return lax.ppermute(rows, AXES, pairs)  16.2 us
    pallas_call x1, Pallas kernels, prep(): pl.pallas_call(prep_kernel, out_shape=(jax.ShapeDtypeStruct((ROWS, D), jn...  5.52 us
    unnamed x40, local copies, waits for them, and re-layouts  4.88 us
  transfers between devices with their start and end apart: 13, of which 7 were waited for; matrix products, arithmetic and copies ran while one was open for 0% of the time, Pallas kernels for 15%

profile of v2, /device:TPU:1, one launch (start us, length us, event | category | flops | bytes accessed | tf_op | source)
XLA Modules:
  0.0 185.1 jit_solution(3424532429790425409)
XLA Ops:
  0.0 0.7 pad_add_fusion.place_ref
  0.7 5.5 %prep.1 = (bf16[1024,768]{1,0:T(8,128)(2,1)}, bf16[1024,768]{1,0:T(8,128)(2,1)}, bf16[1024,128]{1,0:T(8,128)(2,1)}, s32[8,1024]{1,0:T(8,128)}) custom-call(s32[3]{0:T(128)} %pad_add_fusion.place_ref, bf16[1024,768]{1,0:T(8,128)(2,1)} %emb_ref.1, s32[1,1024]{1,0:T(1,128)} %bitcast.26, s32[1,1024]{1,0:T(1,128)} %bitcast.28), custom_call_target="tpu_custom_call" | custom-call | flops 1879048192 | bytes 4718592 | tf_op jit(solution)/shard_map/prep/pallas_call | solution.py:126
  6.2 0.0 copy-start.14
  6.2 0.0 copy-start.15
  6.2 16.5 %all-to-all-start = ((bf16[128,8,768]{2,1,0:T(8,128)(2,1)}), bf16[128,8,768]{2,1,0:T(8,128)(2,1)S(1)}, u32[]{:S(2)}, u32[]{:S(2)}) async-start(bf16[128,8,768]{2,1,0:T(8,128)(2,1)} %bitcast.30), calls=%async_computation | async-start | bytes 3145728 | tf_op jit(solution)/shard_map/all_to_all | solution.py:50
  22.7 0.0 copy-done.2
  22.7 0.0 copy-done.11
  22.7 0.0 copy-done.12
  22.7 0.0 copy-done.14
  22.7 0.0 copy-done.15
  22.7 0.0 copy-start.1
  22.7 2.9 %hand.1 = bf16[1024,896]{1,0:T(8,128)(2,1)S(1)} custom-call(s32[3]{0:T(128)S(1)} %copy-done.2, bf16[1024,768]{1,0:T(8,128)(2,1)S(1)} %copy-done.14, s32[8,1024]{1,0:T(8,128)S(1)} %copy-done.15, s32[1,1024]{1,0:T(1,128)S(1)} %bitcast.27, s32[1,1024]{1,0:T(1,128)S(1)} %bitcast.29), custom_call_target="tpu_custom_call" | custom-call | flops 1879048192 | bytes 3145728 | tf_op jit(solution)/shard_map/hand/pallas_call | solution.py:154
  25.6 1.0 collective-permute-start
  26.7 3.4 %collective-permute-done.box_ref = bf16[1024,896]{1,0:T(8,128)(2,1)S(1)} collective-permute-done((bf16[1024,896]{1,0:T(8,128)(2,1)S(1)}, bf16[1024,896]{1,0:T(8,128)(2,1)S(1)}, u32[]{:S(2)}, u32[]{:S(2)}) %collective-permute-start) | collective-permute-done | bytes 1835040 | tf_op jit(solution)/shard_map/ppermute | solution.py:56
  30.1 0.0 copy-done.1
  30.1 0.2 stamp.1
  30.2 0.0 copy-start
  30.3 1.2 copy-done
  31.5 30.0 %all-to-all-done = bf16[128,8,768]{2,1,0:T(8,128)(2,1)S(1)} async-done(((bf16[128,8,768]{2,1,0:T(8,128)(2,1)}), bf16[128,8,768]{2,1,0:T(8,128)(2,1)S(1)}, u32[]{:S(2)}, u32[]{:S(2)}) %all-to-all-start) | async-done | bytes 1572896 | tf_op jit(solution)/shard_map/all_to_all | solution.py:50
  61.4 8.9 %all-to-all-start.1 = ((bf16[128,8,896]{2,1,0:T(8,128)(2,1)}), bf16[128,8,896]{2,1,0:T(8,128)(2,1)S(1)}, u32[]{:S(2)}, u32[]{:S(2)}) async-start(bf16[128,8,896]{2,1,0:T(8,128)(2,1)} %bitcast.19), calls=%async_computation.1 | async-start | bytes 3670016 | tf_op jit(solution)/shard_map/all_to_all | solution.py:50
  70.4 0.1 fusion.1
  70.5 0.8 collective-permute-start.1
  71.3 2.0 %collective-permute-start.2 = (bf16[512,768]{1,0:T(8,128)(2,1)S(1)}, bf16[512,768]{1,0:T(8,128)(2,1)S(1)}, u32[]{:S(2)}, u32[]{:S(2)}) collective-permute-start(bf16[512,768]{1,0:T(8,128)(2,1)S(1)} %get-tuple-element.35), channel_id=1, source_target_pairs={{0,3},{4,196},{1,0},{5,197},{2,1},{6,198},{3,2},{7,199},{8,11},{12... | collective-permute-start | bytes 2359304 | tf_op jit(solution)/shard_map/ppermute | solution.py:56
  73.3 18.3 %collective-permute-done.1.refs_6_ = bf16[512,768]{1,0:T(8,128)(2,1)S(1)} collective-permute-done((bf16[512,768]{1,0:T(8,128)(2,1)S(1)}, bf16[512,768]{1,0:T(8,128)(2,1)S(1)}, u32[]{:S(2)}, u32[]{:S(2)}) %collective-permute-start.1) | collective-permute-done | bytes 786464 | tf_op jit(solution)/shard_map/ppermute | solution.py:56
  91.5 0.0 collective-permute-start.3
  91.5 0.9 copy-done.3
  92.4 0.0 collective-permute-done.2.refs_7_
  92.4 2.7 %collective-permute-start.4 = (bf16[512,768]{1,0:T(8,128)(2,1)S(1)}, bf16[512,768]{1,0:T(8,128)(2,1)S(1)}, u32[]{:S(2)}, u32[]{:S(2)}) collective-permute-start(bf16[512,768]{1,0:T(8,128)(2,1)S(1)} %collective-permute-done.2.refs_7_), channel_id=1, source_target_pairs={{0,3},{4,196},{1,0},{5,197},{2,1},{6,198},{3,2},{7,199},{8,11},{12... | collective-permute-start | bytes 2359304 | tf_op jit(solution)/shard_map/ppermute | solution.py:56
  95.1 0.9 copy-done.5
  96.0 14.8 %collective-permute-done.3.refs_8_ = bf16[512,768]{1,0:T(8,128)(2,1)S(1)} collective-permute-done((bf16[512,768]{1,0:T(8,128)(2,1)S(1)}, bf16[512,768]{1,0:T(8,128)(2,1)S(1)}, u32[]{:S(2)}, u32[]{:S(2)}) %collective-permute-start.3) | collective-permute-done | bytes 786464 | tf_op jit(solution)/shard_map/ppermute | solution.py:56
  110.8 0.9 copy-done.7
  111.6 0.0 collective-permute-done.4.refs_9_
  111.6 0.9 copy-done.9
  112.6 1.6 all-to-all-done.1
  114.2 1.4 fusion
  115.6 0.5 collective-permute-start.5
  116.1 2.2 %collective-permute-start.6 = (bf16[512,896]{1,0:T(8,128)(2,1)}, bf16[512,896]{1,0:T(8,128)(2,1)}, u32[]{:S(2)}, u32[]{:S(2)}) collective-permute-start(bf16[512,896]{1,0:T(8,128)(2,1)} %get-tuple-element.33), channel_id=1, source_target_pairs={{0,3},{4,196},{1,0},{5,197},{2,1},{6,198},{3,2},{7,199},{8,11},{12... | collective-permute-start | bytes 2752520 | tf_op jit(solution)/shard_map/ppermute | solution.py:56
  118.2 0.0 copy-done.18
  118.2 0.0 copy-done.19
  118.3 0.0 copy-start.16
  118.3 0.0 copy-start.17
  118.3 0.0 copy-start.4
  118.3 0.0 copy-start.6
  118.3 0.0 copy-start.8
  118.3 0.0 copy-start.10
  118.3 0.1 collective-permute-start.7
  118.4 0.0 copy-done.13
  118.5 7.7 %own.1.refs_6_ = f32[128,128]{1,0:T(8,128)S(1)} custom-call(s32[30]{0:T(128)S(1)} %copy-done.13, bf16[1024,896]{1,0:T(8,128)(2,1)S(1)} %bitcast.16, bf16[1024,768]{1,0:T(8,128)(2,1)S(1)} %bitcast.21), custom_call_target="tpu_custom_call" | custom-call | flops 4026531840 | bytes 6291456 | tf_op jit(solution)/shard_map/own/pallas_call | solution.py:346
  126.2 6.2 %collective-permute-done.5.refs_2_ = bf16[512,896]{1,0:T(8,128)(2,1)} collective-permute-done((bf16[512,896]{1,0:T(8,128)(2,1)}, bf16[512,896]{1,0:T(8,128)(2,1)}, u32[]{:S(2)}, u32[]{:S(2)}) %collective-permute-start.5) | collective-permute-done | bytes 917536 | tf_op jit(solution)/shard_map/ppermute | solution.py:56
  132.4 0.0 collective-permute-done.6.refs_3_
  132.4 0.0 collective-permute-start.8
  132.4 2.7 %collective-permute-start.9 = (bf16[512,896]{1,0:T(8,128)(2,1)}, bf16[512,896]{1,0:T(8,128)(2,1)S(1)}, u32[]{:S(2)}, u32[]{:S(2)}) collective-permute-start(bf16[512,896]{1,0:T(8,128)(2,1)} %collective-permute-done.6.refs_3_), channel_id=1, source_target_pairs={{0,3},{4,196},{1,0},{5,197},{2,1},{6,198},{3,2},{7,199},{8,11},{12... | collective-permute-start | bytes 2752520 | tf_op jit(solution)/shard_map/ppermute | solution.py:56
  135.1 0.0 copy-done.16
  135.1 0.0 copy-done.17
  135.1 0.0 collective-permute-done.7.refs_4_.refs_3_
  135.1 0.0 copy-done.4
  135.2 16.3 %near.1.refs_7_ = f32[128,128]{1,0:T(8,128)S(1)} custom-call(s32[66]{0:T(128)S(1)} %broadcast_select_fusion.refs_0_, bf16[1024,896]{1,0:T(8,128)(2,1)S(1)} %bitcast.17, bf16[512,896]{1,0:T(8,128)(2,1)} %collective-permute-done.5.refs_2_, bf16[512,896]{1,0:T(8,128)(2,1)} %collective-permute-done.6.refs_3_, ...), custom_call_target="tpu_custom_call" | custom-call | flops 8858370048 | bytes 15728640 | tf_op jit(solution)/shard_map/near/pallas_call | solution.py:346
  151.5 0.0 collective-permute-done.8.refs_4_
  151.5 0.0 collective-permute-done.9.refs_5_
  151.5 4.0 %far.1 = f32[128,128]{1,0:T(8,128)S(1)} custom-call(s32[6]{0:T(128)S(1)} %broadcast_select_fusion.1.refs_0_, bf16[1024,896]{1,0:T(8,128)(2,1)S(1)} %bitcast.18, bf16[512,896]{1,0:T(8,128)(2,1)} %collective-permute-done.5.refs_2_, bf16[1024,128]{1,0:T(8,128)(2,1)S(1)} %collective-permute-done.7.refs_4_.refs_3_, ...), custom_call_target="tpu_custom_call" | custom-call | flops 805306368 | bytes 7864320 | tf_op jit(solution)/shard_map/far/pallas_call | solution.py:346
  155.5 22.0 %all_to_all.15 = f32[128,1,128]{2,1,0:T(1,128)S(1)} all-to-all(f32[128,1,128]{2,1,0:T(1,128)S(1)} %bitcast.23), channel_id=1, replica_groups={{0,1,2,3,8,9,10,11,16,17,18,19,24,25,26,27,32,33,34,35,40,41,42,43,48,4..., dimensions={0} | all-to-all | bytes 131072 | tf_op jit(solution)/shard_map/all_to_all | solution.py:50
  177.5 4.3 %collective-permute-start.10 = (f32[128,128]{1,0:T(8,128)S(1)}, f32[128,128]{1,0:T(8,128)S(1)}, u32[]{:S(2)}, u32[]{:S(2)}) collective-permute-start(f32[128,128]{1,0:T(8,128)S(1)} %bitcast.24), channel_id=1, source_target_pairs={{0,4},{1,5},{2,6},{3,7},{4,0},{5,1},{6,2},{7,3},{8,12},{9,13},{10,... | collective-permute-start | bytes 196616 | tf_op jit(solution)/shard_map/ppermute | solution.py:56
  181.8 0.9 collective-permute-done.10.sibling_ref
  182.7 2.4 %answer.1 = f32[1,1024]{1,0:T(1,128)} custom-call(s32[3]{0:T(128)S(1)} %copy-done.2, s32[8,1024]{1,0:T(8,128)S(1)} %copy-done.15, f32[128,128]{1,0:T(8,128)S(1)} %bitcast.25, f32[128,128]{1,0:T(8,128)S(1)} %collective-permute-done.10.sibling_ref), custom_call_target="tpu_custom_call" | custom-call | flops 1207959552 | bytes 196608 | tf_op jit(solution)/shard_map/answer/pallas_call | solution.py:403
  (16 shorter events, 0.0 us)
Async XLA Ops:
  6.2 16.5 %copy-start.2 = (s32[3]{0:T(128)S(1)}, s32[3]{0:T(128)}, u32[]{:S(2)}) copy-start(s32[3]{0:T(128)} %pad_add_fusion.place_ref) | copy-start | bytes 40
  6.2 16.5 %copy-start.11 = (s32[1024]{0:T(1024)S(1)}, s32[1024]{0:T(1024)}, u32[]{:S(2)}) copy-start(s32[1024]{0:T(1024)} %param.9) | copy-start | bytes 12292
  6.2 16.5 %copy-start.12 = (s32[1024]{0:T(1024)S(1)}, s32[1024]{0:T(1024)}, u32[]{:S(2)}) copy-start(s32[1024]{0:T(1024)} %param.10) | copy-start | bytes 12292
  6.2 16.5 %copy-start.14 = (bf16[1024,768]{1,0:T(8,128)(2,1)S(1)}, bf16[1024,768]{1,0:T(8,128)(2,1)}, u32[]{:S(2)}) copy-start(bf16[1024,768]{1,0:T(8,128)(2,1)} %get-tuple-element.21.unit_ref) | copy-start | bytes 4718596
  6.2 16.5 %copy-start.15 = (s32[8,1024]{1,0:T(8,128)S(1)}, s32[8,1024]{1,0:T(8,128)}, u32[]{:S(2)}) copy-start(s32[8,1024]{1,0:T(8,128)} %get-tuple-element.19.info_ref) | copy-start | bytes 98308
  6.2 55.2 %all-to-all-start = ((bf16[128,8,768]{2,1,0:T(8,128)(2,1)}), bf16[128,8,768]{2,1,0:T(8,128)(2,1)S(1)}, u32[]{:S(2)}, u32[]{:S(2)}) async-start(bf16[128,8,768]{2,1,0:T(8,128)(2,1)} %bitcast.30), calls=%async_computation | async-start | bytes 3145728 | tf_op jit(solution)/shard_map/all_to_all | solution.py:50
  22.7 7.3 %copy-start.1 = (bf16[1024,128]{1,0:T(8,128)(2,1)S(1)}, bf16[1024,128]{1,0:T(8,128)(2,1)}, u32[]{:S(2)}) copy-start(bf16[1024,128]{1,0:T(8,128)(2,1)} %get-tuple-element.22.slab_ref) | copy-start | bytes 786436
  25.6 4.5 %collective-permute-start = (bf16[1024,896]{1,0:T(8,128)(2,1)S(1)}, bf16[1024,896]{1,0:T(8,128)(2,1)S(1)}, u32[]{:S(2)}, u32[]{:S(2)}) collective-permute-start(bf16[1024,896]{1,0:T(8,128)(2,1)S(1)} %hand.1), channel_id=1, source_target_pairs={{0,4},{1,5},{2,6},{3,7},{4,0},{5,1},{6,2},{7,3},{8,12},{9,13},{10,... | collective-permute-start | bytes 5505032 | tf_op jit(solution)/shard_map/ppermute | solution.py:56
  30.2 1.2 copy-start
  61.4 52.8 %all-to-all-start.1 = ((bf16[128,8,896]{2,1,0:T(8,128)(2,1)}), bf16[128,8,896]{2,1,0:T(8,128)(2,1)S(1)}, u32[]{:S(2)}, u32[]{:S(2)}) async-start(bf16[128,8,896]{2,1,0:T(8,128)(2,1)} %bitcast.19), calls=%async_computation.1 | async-start | bytes 3670016 | tf_op jit(solution)/shard_map/all_to_all | solution.py:50
  70.5 21.0 %collective-permute-start.1 = (bf16[512,768]{1,0:T(8,128)(2,1)S(1)}, bf16[512,768]{1,0:T(8,128)(2,1)S(1)}, u32[]{:S(2)}, u32[]{:S(2)}) collective-permute-start(bf16[512,768]{1,0:T(8,128)(2,1)S(1)} %get-tuple-element.36), channel_id=1, source_target_pairs={{0,1},{4,68},{1,2},{5,69},{2,3},{6,70},{3,0},{7,71},{8,9},{12,76},... | collective-permute-start | bytes 2359304 | tf_op jit(solution)/shard_map/ppermute | solution.py:56
  71.3 21.2 %collective-permute-start.2 = (bf16[512,768]{1,0:T(8,128)(2,1)S(1)}, bf16[512,768]{1,0:T(8,128)(2,1)S(1)}, u32[]{:S(2)}, u32[]{:S(2)}) collective-permute-start(bf16[512,768]{1,0:T(8,128)(2,1)S(1)} %get-tuple-element.35), channel_id=1, source_target_pairs={{0,3},{4,196},{1,0},{5,197},{2,1},{6,198},{3,2},{7,199},{8,11},{12... | collective-permute-start | bytes 2359304 | tf_op jit(solution)/shard_map/ppermute | solution.py:56
  91.5 19.2 %collective-permute-start.3 = (bf16[512,768]{1,0:T(8,128)(2,1)S(1)}, bf16[512,768]{1,0:T(8,128)(2,1)S(1)}, u32[]{:S(2)}, u32[]{:S(2)}) collective-permute-start(bf16[512,768]{1,0:T(8,128)(2,1)S(1)} %collective-permute-done.1.refs_6_), channel_id=1, source_target_pairs={{0,1},{4,68},{1,2},{5,69},{2,3},{6,70},{3,0},{7,71},{8,9},{12,76},... | collective-permute-start | bytes 2359304 | tf_op jit(solution)/shard_map/ppermute | solution.py:56
  91.5 0.9 copy-start.3
  92.4 19.2 %collective-permute-start.4 = (bf16[512,768]{1,0:T(8,128)(2,1)S(1)}, bf16[512,768]{1,0:T(8,128)(2,1)S(1)}, u32[]{:S(2)}, u32[]{:S(2)}) collective-permute-start(bf16[512,768]{1,0:T(8,128)(2,1)S(1)} %collective-permute-done.2.refs_7_), channel_id=1, source_target_pairs={{0,3},{4,196},{1,0},{5,197},{2,1},{6,198},{3,2},{7,199},{8,11},{12... | collective-permute-start | bytes 2359304 | tf_op jit(solution)/shard_map/ppermute | solution.py:56
  95.1 0.9 copy-start.5
  110.8 0.9 copy-start.7
  111.6 0.9 copy-start.9
  114.2 4.0 %copy-start.18 = (s32[66]{0:T(128)S(1)}, s32[66]{0:T(128)}, u32[]{:S(2)}) copy-start(s32[66]{0:T(128)} %constant.71.clone) | copy-start | bytes 796
  114.2 4.0 %copy-start.19 = (s32[66]{0:T(128)S(1)}, s32[66]{0:T(128)}, u32[]{:S(2)}) copy-start(s32[66]{0:T(128)} %constant.72.clone) | copy-start | bytes 796
  114.2 4.2 %copy-start.13 = (s32[30]{0:T(128)S(1)}, s32[30]{0:T(128)}, u32[]{:S(2)}) copy-start(s32[30]{0:T(128)} %constant.70.clone.refs_0_) | copy-start | bytes 364
  115.6 16.9 %collective-permute-start.5 = (bf16[512,896]{1,0:T(8,128)(2,1)}, bf16[512,896]{1,0:T(8,128)(2,1)}, u32[]{:S(2)}, u32[]{:S(2)}) collective-permute-start(bf16[512,896]{1,0:T(8,128)(2,1)} %get-tuple-element.34), channel_id=1, source_target_pairs={{0,1},{4,68},{1,2},{5,69},{2,3},{6,70},{3,0},{7,71},{8,9},{12,76},... | collective-permute-start | bytes 2752520 | tf_op jit(solution)/shard_map/ppermute | solution.py:56
  116.1 16.4 %collective-permute-start.6 = (bf16[512,896]{1,0:T(8,128)(2,1)}, bf16[512,896]{1,0:T(8,128)(2,1)}, u32[]{:S(2)}, u32[]{:S(2)}) collective-permute-start(bf16[512,896]{1,0:T(8,128)(2,1)} %get-tuple-element.33), channel_id=1, source_target_pairs={{0,3},{4,196},{1,0},{5,197},{2,1},{6,198},{3,2},{7,199},{8,11},{12... | collective-permute-start | bytes 2752520 | tf_op jit(solution)/shard_map/ppermute | solution.py:56
  118.3 16.8 %copy-start.16 = (s32[6]{0:T(128)S(1)}, s32[6]{0:T(128)}, u32[]{:S(2)}) copy-start(s32[6]{0:T(128)} %constant.73.clone) | copy-start | bytes 76
  118.3 16.8 %copy-start.17 = (s32[6]{0:T(128)S(1)}, s32[6]{0:T(128)}, u32[]{:S(2)}) copy-start(s32[6]{0:T(128)} %constant.74.clone) | copy-start | bytes 76
  118.3 16.8 %copy-start.4 = (bf16[512,768]{1,0:T(8,128)(2,1)S(1)}, bf16[512,768]{1,0:T(8,128)(2,1)}, u32[]{:S(2)}) copy-start(bf16[512,768]{1,0:T(8,128)(2,1)} %copy-done.3) | copy-start | bytes 2359300
  118.3 16.8 %copy-start.6 = (bf16[512,768]{1,0:T(8,128)(2,1)S(1)}, bf16[512,768]{1,0:T(8,128)(2,1)}, u32[]{:S(2)}) copy-start(bf16[512,768]{1,0:T(8,128)(2,1)} %copy-done.5) | copy-start | bytes 2359300
  118.3 16.8 %copy-start.8 = (bf16[512,768]{1,0:T(8,128)(2,1)S(1)}, bf16[512,768]{1,0:T(8,128)(2,1)}, u32[]{:S(2)}) copy-start(bf16[512,768]{1,0:T(8,128)(2,1)} %copy-done.7) | copy-start | bytes 2359300
  118.3 16.8 %copy-start.10 = (bf16[512,768]{1,0:T(8,128)(2,1)S(1)}, bf16[512,768]{1,0:T(8,128)(2,1)}, u32[]{:S(2)}) copy-start(bf16[512,768]{1,0:T(8,128)(2,1)} %copy-done.9) | copy-start | bytes 2359300
  118.3 16.8 %collective-permute-start.7 = (bf16[1024,128]{1,0:T(8,128)(2,1)S(1)}, bf16[1024,128]{1,0:T(8,128)(2,1)S(1)}, u32[]{:S(2)}, u32[]{:S(2)}) collective-permute-start(bf16[1024,128]{1,0:T(8,128)(2,1)S(1)} %slice.19), channel_id=1, source_target_pairs={{0,2},{4,132},{1,3},{5,133},{2,0},{6,134},{3,1},{7,135},{8,10},{12... | collective-permute-start | bytes 786440 | tf_op jit(solution)/shard_map/ppermute | solution.py:56
  132.4 19.1 %collective-permute-start.8 = (bf16[512,896]{1,0:T(8,128)(2,1)}, bf16[512,896]{1,0:T(8,128)(2,1)S(1)}, u32[]{:S(2)}, u32[]{:S(2)}) collective-permute-start(bf16[512,896]{1,0:T(8,128)(2,1)} %collective-permute-done.5.refs_2_), channel_id=1, source_target_pairs={{0,1},{4,68},{1,2},{5,69},{2,3},{6,70},{3,0},{7,71},{8,9},{12,76},... | collective-permute-start | bytes 2752520 | tf_op jit(solution)/shard_map/ppermute | solution.py:56
  132.4 19.1 %collective-permute-start.9 = (bf16[512,896]{1,0:T(8,128)(2,1)}, bf16[512,896]{1,0:T(8,128)(2,1)S(1)}, u32[]{:S(2)}, u32[]{:S(2)}) collective-permute-start(bf16[512,896]{1,0:T(8,128)(2,1)} %collective-permute-done.6.refs_3_), channel_id=1, source_target_pairs={{0,3},{4,196},{1,0},{5,197},{2,1},{6,198},{3,2},{7,199},{8,11},{12... | collective-permute-start | bytes 2752520 | tf_op jit(solution)/shard_map/ppermute | solution.py:56
  177.5 5.2 %collective-permute-start.10 = (f32[128,128]{1,0:T(8,128)S(1)}, f32[128,128]{1,0:T(8,128)S(1)}, u32[]{:S(2)}, u32[]{:S(2)}) collective-permute-start(f32[128,128]{1,0:T(8,128)S(1)} %bitcast.24), channel_id=1, source_target_pairs={{0,4},{1,5},{2,6},{3,7},{4,0},{5,1},{6,2},{7,3},{8,12},{9,13},{10,... | collective-permute-start | bytes 196616 | tf_op jit(solution)/shard_map/ppermute | solution.py:56

commit v3 on v2

--- a/solution.py
+++ b/solution.py
@@ -77,6 +77,11 @@
     )
 
 
+def where_am_i():
+    dp = lax.axis_index("dp")
+    return lax.axis_index("rep"), dp >> 4, (dp >> 1) & (NZ - 1), dp & 1
+
+
 def slots_of(info, core, mine):
     group, rank = info[0:1], info[1:2]
     chip, serving = chip_of(group, rank & 3)
@@ -84,24 +89,42 @@
     return jnp.where((serving == core) if mine else (serving != core), slot, -1)
 
 
-def onehot(slot):
-    rows = lax.broadcasted_iota(jnp.int32, (ROWS, ROWS), 0)
+def onehot(slot, first, count):
+    rows = lax.broadcasted_iota(jnp.int32, (count, ROWS), 0) + first
     return jnp.where(rows == slot, 1.0, 0.0).astype(jnp.bfloat16)
 
 
-def prep_kernel(place_ref, emb_ref, ids_ref, order_ref, unit_ref, box_ref, slab_ref, info_ref):
-    ids, order = ids_ref[...], order_ref[...]
-    group = ids >> 1
-    member = (lax.broadcasted_iota(jnp.int32, (GROUPS, ROWS), 0) == group)
+def normalize(rows):
+    wide = rows.astype(jnp.float32)
+    scale = 1.0 / jnp.sqrt(jnp.sum(wide * wide, axis=1, keepdims=True) + 1e-06)
+    return (wide * scale).astype(jnp.bfloat16)
+
+
+PIECE = 256
+PIECES = ROWS // PIECE
+
+
+def prep_kernel(emb_ref, ids_ref, box_ref, info_ref, rows, unit, out, in_sems, out_sems):
+    def piece(number):
+        return pl.ds(number * PIECE, PIECE)
+
+    loads = [
+        pltpu.make_async_copy(emb_ref.at[piece(n)], rows.at[piece(n)], in_sems.at[n]) for n in range(PIECES)
+    ]
+    for load in loads:
+        load.start()
+    group = ids_ref[...] >> 1
+    member = lax.broadcasted_iota(jnp.int32, (GROUPS, ROWS), 0) == group
     hot = jnp.where(member, 1.0, 0.0)
-    step = 256
     earlier = jnp.where(
-        lax.broadcasted_iota(jnp.int32, (step, step), 0) < lax.broadcasted_iota(jnp.int32, (step, step), 1), 1.0, 0.0
+        lax.broadcasted_iota(jnp.int32, (PIECE, PIECE), 0) < lax.broadcasted_iota(jnp.int32, (PIECE, PIECE), 1),
+        1.0,
+        0.0,
     ).astype(jnp.bfloat16)
     before = jnp.zeros((GROUPS, 1), jnp.float32)
     ranks = []
-    for part in range(ROWS // step):
-        here = hot[:, part * step : (part + 1) * step]
+    for n in range(PIECES):
+        here = hot[:, n * PIECE : (n + 1) * PIECE]
         count = jnp.dot(here.astype(jnp.bfloat16), earlier, preferred_element_type=jnp.float32) + before
         ranks.append(jnp.sum(here * count, axis=0, keepdims=True))
         before = before + jnp.sum(here, axis=1, keepdims=True)
@@ -109,57 +132,71 @@
     which = lax.broadcasted_iota(jnp.int32, (8, ROWS), 0)
     info = jnp.where(which == 0, group, jnp.where(which == 1, rank, 0))
     info_ref[...] = info
-
-    wide = emb_ref[...].astype(jnp.float32)
-    scale = 1.0 / jnp.sqrt(jnp.sum(wide * wide, axis=1, keepdims=True) + 1e-06)
-    unit = (wide * scale).astype(jnp.bfloat16)
-    unit_ref[...] = unit
-
-    pick = onehot(slots_of(info, place_ref[0], True))
-    box_ref[...] = jnp.dot(pick, unit, preferred_element_type=jnp.float32).astype(jnp.bfloat16)
-    slab_ref[...] = lax.dot_general(
-        pick, key_rows(ids, order, 2), (((1,), (1,)), ((), ())), preferred_element_type=jnp.float32
-    ).astype(jnp.bfloat16)
-
-
-def prep(place, embeddings, ids, order):
+    slot = slots_of(info, where_am_i()[3], True)
+
+    for n in range(PIECES):
+        loads[n].wait()
+        unit[piece(n)] = normalize(rows[piece(n)])
+    stores = []
+    for n in range(PIECES):
+        pick = onehot(slot, n * PIECE, PIECE)
+        out[piece(n)] = jnp.dot(pick, unit[...], preferred_element_type=jnp.float32).astype(jnp.bfloat16)
+        stores.append(pltpu.make_async_copy(out.at[piece(n)], box_ref.at[piece(n)], out_sems.at[n]))
+        stores[-1].start()
+    for store in stores:
+        store.wait()
+
+
+def prep(embeddings, ids):
     return pl.pallas_call(
         prep_kernel,
         out_shape=(
             jax.ShapeDtypeStruct((ROWS, D), jnp.bfloat16),
-            jax.ShapeDtypeStruct((ROWS, D), jnp.bfloat16),
-            jax.ShapeDtypeStruct((ROWS, KEYS), jnp.bfloat16),
             jax.ShapeDtypeStruct((8, ROWS), jnp.int32),
         ),
-        in_specs=[pl.BlockSpec(memory_space=pltpu.SMEM)] + [pl.BlockSpec(memory_space=pltpu.VMEM)] * 3,
-        out_specs=tuple([pl.BlockSpec(memory_space=pltpu.VMEM)] * 4),
+        in_specs=[pl.BlockSpec(memory_space=pl.ANY), pl.BlockSpec(memory_space=pltpu.VMEM)],
+        out_specs=(pl.BlockSpec(memory_space=pl.ANY), pl.BlockSpec(memory_space=pltpu.VMEM)),
+        scratch_shapes=[
+            pltpu.VMEM((ROWS, D), jnp.bfloat16),
+            pltpu.VMEM((ROWS, D), jnp.bfloat16),
+            pltpu.VMEM((ROWS, D), jnp.bfloat16),
+            pltpu.SemaphoreType.DMA((PIECES,)),
+            pltpu.SemaphoreType.DMA((PIECES,)),
+        ],
         compiler_params=pltpu.CompilerParams(vmem_limit_bytes=FULL),
-        cost_estimate=cost(2 * ROWS * ROWS * WIDE, 6 * ROWS * D),
+        cost_estimate=cost(2 * ROWS * ROWS * D, 4 * ROWS * D),
         name="prep",
-    )(place, embeddings, ids, order)
-
-
-def hand_kernel(place_ref, unit_ref, info_ref, ids_ref, order_ref, box_ref):
-    pick = onehot(slots_of(info_ref[...], place_ref[0], False))
-    box_ref[:, :D] = jnp.dot(pick, unit_ref[...], preferred_element_type=jnp.float32).astype(jnp.bfloat16)
-    box_ref[:, D:] = lax.dot_general(
-        pick,
-        key_rows(ids_ref[...], order_ref[...], 0),
-        (((1,), (1,)), ((), ())),
-        preferred_element_type=jnp.float32,
-    ).astype(jnp.bfloat16)
-
-
-def hand(place, unit, info, ids, order):
+    )(embeddings, ids)
+
+
+def hand_kernel(emb_ref, info_ref, ids_ref, order_ref, box_ref, slab_ref):
+    info, core = info_ref[...], where_am_i()[3]
+    ids, order = ids_ref[...], order_ref[...]
+
+    def keys(pick, first):
+        return lax.dot_general(
+            pick, key_rows(ids, order, first), (((1,), (1,)), ((), ())), preferred_element_type=jnp.float32
+        ).astype(jnp.bfloat16)
+
+    pick = onehot(slots_of(info, core, False), 0, ROWS)
+    box_ref[:, :D] = jnp.dot(pick, normalize(emb_ref[...]), preferred_element_type=jnp.float32).astype(jnp.bfloat16)
+    box_ref[:, D:] = keys(pick, 0)
+    slab_ref[...] = keys(onehot(slots_of(info, core, True), 0, ROWS), 2)
+
+
+def hand(embeddings, info, ids, order):
     return pl.pallas_call(
         hand_kernel,
-        out_shape=jax.ShapeDtypeStruct((ROWS, WIDE), jnp.bfloat16),
-        in_specs=[pl.BlockSpec(memory_space=pltpu.SMEM)] + [pl.BlockSpec(memory_space=pltpu.VMEM)] * 4,
-        out_specs=pl.BlockSpec(memory_space=pltpu.VMEM),
+        out_shape=(
+            jax.ShapeDtypeStruct((ROWS, WIDE), jnp.bfloat16),
+            jax.ShapeDtypeStruct((ROWS, KEYS), jnp.bfloat16),
+        ),
+        in_specs=[pl.BlockSpec(memory_space=pltpu.VMEM)] * 4,
+        out_specs=tuple([pl.BlockSpec(memory_space=pltpu.VMEM)] * 2),
         compiler_params=pltpu.CompilerParams(vmem_limit_bytes=VMEM),
         cost_estimate=cost(2 * ROWS * ROWS * WIDE, 4 * ROWS * D),
         name="hand",
-    )(place, unit, info, ids, order)
+    )(embeddings, info, ids, order)
 
 
 def stamp_kernel(box_ref, slab_ref, out_ref):
@@ -181,6 +218,34 @@
         cost_estimate=cost(0, 3 * 2 * ROWS * KEYS),
         name="stamp",
     )(box, slab)
+
+
+def split_kernel(both_ref, p_ref, m_ref, key_ref):
+    p_ref[...] = both_ref[:HALF_ROWS, :D]
+    m_ref[...] = both_ref[HALF_ROWS:, :D]
+    row = lax.broadcasted_iota(jnp.int32, (8, KEYS), 0)
+    lane = lax.broadcasted_iota(jnp.int32, (8, KEYS), 1)
+    first = jnp.where(row == 0, 2, jnp.where(row == 1, 0, KEYS))
+    weight = jnp.where(lane == first, 128.0, jnp.where(lane == first + 1, 1.0, 0.0)).astype(jnp.bfloat16)
+    key_ref[...] = lax.dot_general(
+        weight, both_ref[:, D:], (((1,), (1,)), ((), ())), preferred_element_type=jnp.float32
+    )
+
+
+def split(both):
+    return pl.pallas_call(
+        split_kernel,
+        out_shape=(
+            jax.ShapeDtypeStruct((HALF_ROWS, D), jnp.bfloat16),
+            jax.ShapeDtypeStruct((HALF_ROWS, D), jnp.bfloat16),
+            jax.ShapeDtypeStruct((8, ROWS), jnp.float32),
+        ),
+        in_specs=[pl.BlockSpec(memory_space=pltpu.VMEM)],
+        out_specs=tuple([pl.BlockSpec(memory_space=pltpu.VMEM)] * 3),
+        compiler_params=pltpu.CompilerParams(vmem_limit_bytes=VMEM),
+        cost_estimate=cost(0, 4 * ROWS * WIDE),
+        name="split",
+    )(both)
 
 
 BLOCKS = [(part, far, chunk) for far in range(3) for chunk in range(2) for part in "PM"]
@@ -218,45 +283,40 @@
     return 2 if any(far == 2 and chunk == 1 for part, far, chunk in pair) else 1
 
 
-def similar_kernel(blocks, loads, n_tasks, n_before, *refs):
+def similar_kernel(blocks, loads, n_tasks, n_keys, n_before, *refs):
     n_arrays = 1 + max(load[0] for load in loads)
-    tasks_ref = refs[0]
-    arrays = refs[1 : 1 + n_arrays]
-    befores = refs[1 + n_arrays : 1 + n_arrays + n_before]
-    out_ref = refs[1 + n_arrays + n_before]
-    rows, slabs, kcol, ccol, krow, crow, best_row, best_col, s0, s1, sems = refs[2 + n_arrays + n_before :]
+    tasks_ref, refs = refs[0], refs[1:]
+    arrays, refs = refs[:n_arrays], refs[n_arrays:]
+    key_refs, refs = refs[:n_keys], refs[n_keys:]
+    befores, refs = refs[:n_before], refs[n_before:]
+    out_ref, rows, kcol, ccol, krow, crow, best_row, best_col, s0, s1, sems = refs
     n_blocks = len(blocks)
 
     copies = []
-    for number, (array, first, columns, is_key, slot) in enumerate(loads):
-        source = arrays[array].at[pl.ds(first, HALF_ROWS), pl.ds(columns, KEYS if is_key else D)]
-        target = slabs.at[slot] if is_key else rows.at[slot]
-        copy = pltpu.make_async_copy(source, target, sems.at[number])
+    for number, (array, first, slot, task) in enumerate(loads):
+        copy = pltpu.make_async_copy(arrays[array].at[pl.ds(first, HALF_ROWS)], rows.at[slot], sems.at[number])
         copy.start()
-        copies.append((copy, is_key))
+        copies.append((copy, task))
     for slot in range(n_blocks):
         best_row[slot] = jnp.full((HALF_ROWS, 128), -1.0, jnp.float32)
         best_col[slot] = jnp.full((8, HALF_ROWS), -1.0, jnp.float32)
-    for copy, is_key in copies:
-        if is_key:
-            copy.wait()
-
-    lane_of = lax.broadcasted_iota(jnp.int32, (KEYS, 128), 0)
-    row_of = lax.broadcasted_iota(jnp.int32, (8, KEYS), 1)
-    for slot, (part, far, chunk) in enumerate(blocks):
-        first = 0 if chunk == 1 else 2
-        slab = slabs[slot]
-        weight = jnp.where(lane_of == first, 128.0, jnp.where(lane_of == first + 1, 1.0, 0.0)).astype(jnp.bfloat16)
-        key = jnp.dot(slab, weight, preferred_element_type=jnp.float32)
+
+    def cluster(key):
+        return jnp.where(key >= ORDERS + 128, 2.0, jnp.where(key > 0, 1.0, 0.0))
+
+    for slot, (part, far, chunk, source) in enumerate(blocks):
+        first = 0 if part == "P" else HALF_ROWS
+        key = key_refs[source][chunk : chunk + 1, first : first + HALF_ROWS]
+        krow[slot] = jnp.broadcast_to(key, (8, HALF_ROWS))
+        crow[slot] = cluster(krow[slot])
+        key = jnp.transpose(jnp.broadcast_to(key, (128, HALF_ROWS)))
         kcol[slot] = key
-        ccol[slot] = jnp.where(key >= ORDERS + 128, 2.0, jnp.where(key > 0, 1.0, 0.0))
-        weight = jnp.where(row_of == first, 128.0, jnp.where(row_of == first + 1, 1.0, 0.0)).astype(jnp.bfloat16)
-        key = lax.dot_general(weight, slab, (((1,), (1,)), ((), ())), preferred_element_type=jnp.float32)
-        krow[slot] = key
-        crow[slot] = jnp.where(key >= ORDERS + 128, 2.0, jnp.where(key > 0, 1.0, 0.0))
-    for copy, is_key in copies:
-        if not is_key:
-            copy.wait()
+        ccol[slot] = cluster(key)
+
+    def arrive(low, high):
+        for copy, task in copies:
+            if low <= task < high:
+                copy.wait()
 
     def multiply(task, s):
         a, b = tasks_ref[3 * task], tasks_ref[3 * task + 1]
@@ -281,15 +341,24 @@
             best_row[a, row : row + step] = best
 
     def two(turn, carry):
+        for t in range(n_tasks // 2 - 1):
+            if any(2 * t + 1 <= task < 2 * t + 3 for copy, task in copies):
+
+                @pl.when(turn == t)
+                def _():
+                    arrive(2 * t + 1, 2 * t + 3)
+
         multiply(2 * turn + 1, s1)
         reduce(2 * turn, s0)
         multiply(2 * turn + 2, s0)
         reduce(2 * turn + 1, s1)
         return carry
 
+    arrive(0, 1)
     multiply(0, s0)
     if n_tasks > 2:
         lax.fori_loop(0, n_tasks // 2 - 1, two, 0)
+    arrive(n_tasks - 1, n_tasks)
     multiply(n_tasks - 1, s1)
     reduce(n_tasks - 2, s0)
     reduce(n_tasks - 1, s1)
@@ -300,7 +369,7 @@
     )
     for number, part in enumerate("PM"):
         tiles = [empty] * 16
-        for slot, (its, far, chunk) in enumerate(blocks):
+        for slot, (its, far, chunk, source) in enumerate(blocks):
             if its == part:
                 by_row = jnp.max(jnp.transpose(best_row[slot]), axis=0, keepdims=True)
                 by_col = jnp.max(best_col[slot], axis=0, keepdims=True)
@@ -326,33 +395,32 @@
     tasks = jnp.asarray(table(low))
     if low != high:
         tasks = jnp.where(ring_place < 2, tasks, jnp.asarray(table(high)))
-    arrays, loads = [], []
-
-    def number_of(array):
+
+    def number_of(array, arrays):
         for number, known in enumerate(arrays):
             if known is array:
                 return number
         arrays.append(array)
         return len(arrays) - 1
 
-    for block in blocks:
-        array, first, column = keys[block[:2]]
-        loads.append((number_of(array), first, column, True, place[block]))
+    arrays, key_arrays, loads, full = [], [], [], []
     for block in blocks:
         array, first = hold[block]
-        loads.append((number_of(array), first, 0, False, place[block]))
+        task = min(n for n, pairs in enumerate(zip(low, high)) if any(block in pair for pair in pairs))
+        loads.append((number_of(array, arrays), first, place[block], task))
+        full.append(block + (number_of(keys[block[:2]], key_arrays),))
+    loads.sort(key=lambda load: load[3])
     n = len(blocks)
-    kernel = functools.partial(similar_kernel, blocks, loads, len(low), len(befores))
+    kernel = functools.partial(similar_kernel, full, loads, len(low), len(key_arrays), len(befores))
     return pl.pallas_call(
         kernel,
         out_shape=jax.ShapeDtypeStruct((CHIPS, 128), jnp.float32),
         in_specs=[pl.BlockSpec(memory_space=pltpu.SMEM)]
         + [pl.BlockSpec(memory_space=pl.ANY)] * len(arrays)
-        + [pl.BlockSpec(memory_space=pltpu.VMEM)] * len(befores),
+        + [pl.BlockSpec(memory_space=pltpu.VMEM)] * (len(key_arrays) + len(befores)),
         out_specs=pl.BlockSpec(memory_space=pltpu.VMEM),
         scratch_shapes=[
             pltpu.VMEM((n, HALF_ROWS, D), jnp.bfloat16),
-            pltpu.VMEM((n, HALF_ROWS, KEYS), jnp.bfloat16),
             pltpu.VMEM((n, HALF_ROWS, 128), jnp.float32),
             pltpu.VMEM((n, HALF_ROWS, 128), jnp.float32),
             pltpu.VMEM((n, 8, HALF_ROWS), jnp.float32),
@@ -366,13 +434,14 @@
         compiler_params=pltpu.CompilerParams(vmem_limit_bytes=32 * 1024 * 1024),
         cost_estimate=cost(2 * D * HALF_ROWS * HALF_ROWS * len(low), 2 * len(loads) * HALF_ROWS * D),
         name=name,
-    )(tasks, *arrays, *befores)
-
-
-def answer_kernel(place_ref, info_ref, mine_ref, sibling_ref, out_ref):
+    )(tasks, *arrays, *key_arrays, *befores)
+
+
+def answer_kernel(info_ref, mine_ref, sibling_ref, out_ref):
     info = info_ref[...]
     group, rank = info[0:1], info[1:2]
-    core, step = place_ref[0], place_ref[2]
+    x, y, z, core = where_am_i()
+    step = jnp.where((y * NZ + z) * NX + x < CHIPS // 2, 1, -1)
     values = jnp.concatenate([mine_ref[...], sibling_ref[...]], axis=0)
     device_of = lax.broadcasted_iota(jnp.int32, (2 * CHIPS, ROWS), 0)
     lane_of = lax.broadcasted_iota(jnp.int32, (128, ROWS), 0)
@@ -399,43 +468,42 @@
     out_ref[...] = best
 
 
-def answer(place, info, mine, sibling):
+def answer(info, mine, sibling):
     return pl.pallas_call(
         answer_kernel,
         out_shape=jax.ShapeDtypeStruct((1, ROWS), jnp.float32),
-        in_specs=[pl.BlockSpec(memory_space=pltpu.SMEM)] + [pl.BlockSpec(memory_space=pltpu.VMEM)] * 3,
+        in_specs=[pl.BlockSpec(memory_space=pltpu.VMEM)] * 3,
         out_specs=pl.BlockSpec(memory_space=pltpu.VMEM),
         compiler_params=pltpu.CompilerParams(vmem_limit_bytes=VMEM),
         cost_estimate=cost(2 * 3 * 6 * 128 * 256 * ROWS, 3 * 4 * 128 * 128),
         name="answer",
-    )(place, info, mine, sibling)
+    )(info, mine, sibling)
 
 
 def local(embeddings, cluster_ids, member_order):
-    dp, x = lax.axis_index("dp"), lax.axis_index("rep")
-    core, z, y = dp % 2, (dp // 2) % NZ, dp // (2 * NZ)
+    x, y, z, core = where_am_i()
     ring_place = jnp.where(core == 0, x, y)
-    step = jnp.where((y * NZ + z) * NX + x < CHIPS // 2, 1, -1)
-    place = jnp.stack([core, ring_place, step]).astype(jnp.int32)
     ids, order = cluster_ids.reshape(1, ROWS), member_order.reshape(1, ROWS)
 
-    unit, box, slab, info = prep(place, embeddings, ids, order)
+    box, info = prep(embeddings, ids)
     chunk1 = exchange(box.reshape(CHIPS, SUB, D)).reshape(ROWS, D)
-    handed = stamp(send(hand(place, unit, info, ids, order), SIBLING), slab)
+    handed, slab = hand(embeddings, info, ids, order)
+    handed = stamp(send(handed, SIBLING), slab)
     chunk1, handed = lax.optimization_barrier((chunk1, handed))
     chunk2 = exchange(handed.reshape(CHIPS, SUB, WIDE)).reshape(ROWS, WIDE)
     near1 = send(chunk1[:HALF_ROWS], ring(1)), send(chunk1[HALF_ROWS:], ring(-1))
     far1 = send(near1[0], ring(1)), send(near1[1], ring(-1))
     chunk2, near1, far1 = lax.optimization_barrier((chunk2, near1, far1))
-    near2 = send(chunk2[:HALF_ROWS], ring(1)), send(chunk2[HALF_ROWS:], ring(-1))
-    far_keys = send(chunk2[:, D:], ring(2))
-
-    hold, keys = {}, {}
+    own2_p, own2_m, key = split(chunk2)
+    own2 = own2_p, own2_m
+    near2 = send(own2_p, ring(1)), send(own2_m, ring(-1))
+    keys = {("P", 0): key, ("M", 0): key, ("P", 1): send(key, ring(1)), ("M", 1): send(key, ring(-1))}
+    keys["P", 2] = keys["M", 2] = send(key, ring(2))
+
+    hold = {}
     for half, part in enumerate("PM"):
-        first = half * HALF_ROWS
-        hold[part, 0, 0], hold[part, 0, 1] = (chunk1, first), (chunk2, first)
+        hold[part, 0, 0], hold[part, 0, 1] = (chunk1, half * HALF_ROWS), (own2[half], 0)
         hold[part, 1, 0], hold[part, 2, 0] = (near1[half], 0), (far1[half], 0)
-        keys[part, 0], keys[part, 2] = (chunk2, first, D), (far_keys, first, 0)
 
     pairs, by_place = pair_lists()
     answers = []
@@ -456,9 +524,8 @@
             far2 = send(near2[0], ring(1)), send(near2[1], ring(-1))
             for half, part in enumerate("PM"):
                 hold[part, 1, 1], hold[part, 2, 1] = (near2[half], 0), (far2[half], 0)
-                keys[part, 1] = (near2[half], 0, D)
     mine = exchange(answers[2].reshape(CHIPS, 1, 128)).reshape(CHIPS, 128)
-    return answer(place, info, mine, send(mine, SIBLING)).reshape(ROWS)
+    return answer(info, mine, send(mine, SIBLING)).reshape(ROWS)
 
 
 def solution(mesh):

time: 186 us -> 179 us (0.962)
  waiting for transfers between devices: 75.2 us -> 71.1 us
  local copies, waits for them, and re-layouts: 6.37 us -> 2.81 us
    all_to_all x2, waiting for transfers between devices: 31.6 us -> 28.7 us  [exchange(): lax.all_to_all(rows, AXES, split_axis=0, concat_axis=0, tiled=True, axis_...]
    unnamed x40 -> x20, local copies, waits for them, and re-layouts: 4.88 us -> 2.71 us
    ppermute x11 -> x13, starting transfers between devices: 16.2 us -> 18 us  [send(): return lax.ppermute(rows, AXES, pairs)]
    ppermute x11 -> x13, waiting for transfers between devices: 43.6 us -> 42.5 us  [send(): return lax.ppermute(rows, AXES, pairs)]
  transfers between devices with their start and end apart: 13 -> 15, of which waited for: 7 -> 9; matrix products, arithmetic and copies ran while one was open for 0% -> 0% of each run, Pallas kernels for 15% -> 16%
where the time goes in v3:
time: 179 us
  waiting for transfers between devices  71.1 us (40%)
  starting transfers between devices  43.4 us (24%)
  Pallas kernels  38.8 us (22%)
  blocking collectives  22.2 us (12%)
  local copies, waits for them, and re-layouts  2.81 us (2%)
    ppermute x13, waiting for transfers between devices, send(): return lax.ppermute(rows, AXES, pairs)  42.5 us
    all_to_all x2, waiting for transfers between devices, exchange(): lax.all_to_all(rows, AXES, split_axis=0, concat_axis=0, tiled=True, axis_...  28.7 us
    pallas_call x3, Pallas kernels, similar(): pl.pallas_call(kernel, out_shape=jax.ShapeDtypeStruct((CHIPS, 128), jnp.f...  27.6 us
    all_to_all x2, starting transfers between devices, exchange(): lax.all_to_all(rows, AXES, split_axis=0, concat_axis=0, tiled=True, axis_...  25.4 us
    all_to_all x1, blocking collectives, exchange(): lax.all_to_all(rows, AXES, split_axis=0, concat_axis=0, tiled=True, axis_...  22.2 us
    ppermute x13, starting transfers between devices, send(): return lax.ppermute(rows, AXES, pairs)  18 us
    pallas_call x1, Pallas kernels, prep(): pl.pallas_call(prep_kernel, out_shape=(jax.ShapeDtypeStruct((ROWS, D), jn...  5.54 us
  transfers between devices with their start and end apart: 15, of which 9 were waited for; matrix products, arithmetic and copies ran while one was open for 0% of the time, Pallas kernels for 16%

profile of v3, /device:TPU:1, one launch (start us, length us, event | category | flops | bytes accessed | tf_op | source)
XLA Modules:
  0.0 178.5 jit_solution(6033471783267925308)
XLA Ops:
  0.0 5.5 %prep.1 = (bf16[1024,768]{1,0:T(8,128)(2,1)}, s32[8,1024]{1,0:T(8,128)}) custom-call(bf16[1024,768]{1,0:T(8,128)(2,1)} %emb_ref.3, s32[1,1024]{1,0:T(1,128)} %bitcast.19), custom_call_target="tpu_custom_call" | custom-call | flops 1610612736 | bytes 3145728 | tf_op jit(solution)/shard_map/prep/pallas_call | solution.py:151
  5.6 0.0 copy-start.2
  5.6 0.0 copy-start.3
  5.6 0.0 copy-start.5
  5.6 16.5 %all-to-all-start = ((bf16[128,8,768]{2,1,0:T(8,128)(2,1)}), bf16[128,8,768]{2,1,0:T(8,128)(2,1)S(1)}, u32[]{:S(2)}, u32[]{:S(2)}) async-start(bf16[128,8,768]{2,1,0:T(8,128)(2,1)} %bitcast.22), calls=%async_computation | async-start | bytes 3145728 | tf_op jit(solution)/shard_map/all_to_all | solution.py:50
  22.1 0.0 copy-done.2
  22.1 0.0 copy-done.3
  22.1 0.0 copy-done.5
  22.1 0.0 copy-start.1
  22.1 1.4 copy-done.1
  23.5 3.4 %hand.1 = (bf16[1024,896]{1,0:T(8,128)(2,1)S(1)}, bf16[1024,128]{1,0:T(8,128)(2,1)S(1)}) custom-call(bf16[1024,768]{1,0:T(8,128)(2,1)S(1)} %copy-done.1, s32[8,1024]{1,0:T(8,128)S(1)} %copy-done.5, s32[1,1024]{1,0:T(1,128)S(1)} %bitcast.20, s32[1,1024]{1,0:T(1,128)S(1)} %bitcast.21), custom_call_target="tpu_custom_call" | custom-call | flops 1879048192 | bytes 3145728 | tf_op jit(solution)/shard_map/hand/pallas_call | solution.py:188
  26.9 1.0 collective-permute-start
  28.0 3.4 %collective-permute-done.box_ref = bf16[1024,896]{1,0:T(8,128)(2,1)S(1)} collective-permute-done((bf16[1024,896]{1,0:T(8,128)(2,1)S(1)}, bf16[1024,896]{1,0:T(8,128)(2,1)S(1)}, u32[]{:S(2)}, u32[]{:S(2)}) %collective-permute-start) | collective-permute-done | bytes 1835040 | tf_op jit(solution)/shard_map/ppermute | solution.py:56
  31.4 0.2 stamp.1
  31.5 0.0 copy-start
  31.6 1.3 copy-done
  32.8 28.0 %all-to-all-done = bf16[128,8,768]{2,1,0:T(8,128)(2,1)S(1)} async-done(((bf16[128,8,768]{2,1,0:T(8,128)(2,1)}), bf16[128,8,768]{2,1,0:T(8,128)(2,1)S(1)}, u32[]{:S(2)}, u32[]{:S(2)}) %all-to-all-start) | async-done | bytes 1572896 | tf_op jit(solution)/shard_map/all_to_all | solution.py:50
  60.8 8.9 %all-to-all-start.1 = ((bf16[128,8,896]{2,1,0:T(8,128)(2,1)}), bf16[128,8,896]{2,1,0:T(8,128)(2,1)S(1)}, u32[]{:S(2)}, u32[]{:S(2)}) async-start(bf16[128,8,896]{2,1,0:T(8,128)(2,1)} %bitcast.12), calls=%async_computation.1 | async-start | bytes 3670016 | tf_op jit(solution)/shard_map/all_to_all | solution.py:50
  69.8 0.0 copy-start.8
  69.8 0.0 copy-start.9
  69.8 0.0 copy-start.6
  69.8 0.0 copy-start.7
  69.8 0.0 copy-start.4
  69.8 0.1 fusion
  70.0 2.4 %collective-permute-start.2 = (bf16[512,768]{1,0:T(8,128)(2,1)S(1)}, bf16[512,768]{1,0:T(8,128)(2,1)}, u32[]{:S(2)}, u32[]{:S(2)}) collective-permute-start(bf16[512,768]{1,0:T(8,128)(2,1)S(1)} %get-tuple-element.39), channel_id=1, source_target_pairs={{0,3},{4,196},{1,0},{5,197},{2,1},{6,198},{3,2},{7,199},{8,11},{12... | collective-permute-start | bytes 2359304 | tf_op jit(solution)/shard_map/ppermute | solution.py:56
  72.3 0.0 collective-permute-start.1
  72.4 17.7 %collective-permute-done.2.refs_5_ = bf16[512,768]{1,0:T(8,128)(2,1)} collective-permute-done((bf16[512,768]{1,0:T(8,128)(2,1)S(1)}, bf16[512,768]{1,0:T(8,128)(2,1)}, u32[]{:S(2)}, u32[]{:S(2)}) %collective-permute-start.2) | collective-permute-done | bytes 786464 | tf_op jit(solution)/shard_map/ppermute | solution.py:56
  90.1 2.9 %collective-permute-start.4 = (bf16[512,768]{1,0:T(8,128)(2,1)}, bf16[512,768]{1,0:T(8,128)(2,1)}, u32[]{:S(2)}, u32[]{:S(2)}) collective-permute-start(bf16[512,768]{1,0:T(8,128)(2,1)} %collective-permute-done.2.refs_5_), channel_id=1, source_target_pairs={{0,3},{4,196},{1,0},{5,197},{2,1},{6,198},{3,2},{7,199},{8,11},{12... | collective-permute-start | bytes 2359304 | tf_op jit(solution)/shard_map/ppermute | solution.py:56
  93.0 0.3 collective-permute-done.1.refs_4_
  93.3 0.0 collective-permute-start.3
  93.3 15.4 %collective-permute-done.4.refs_9_ = bf16[512,768]{1,0:T(8,128)(2,1)} collective-permute-done((bf16[512,768]{1,0:T(8,128)(2,1)}, bf16[512,768]{1,0:T(8,128)(2,1)}, u32[]{:S(2)}, u32[]{:S(2)}) %collective-permute-start.4) | collective-permute-done | bytes 786464 | tf_op jit(solution)/shard_map/ppermute | solution.py:56
  108.7 4.3 %collective-permute-done.3.refs_8_ = bf16[512,768]{1,0:T(8,128)(2,1)} collective-permute-done((bf16[512,768]{1,0:T(8,128)(2,1)}, bf16[512,768]{1,0:T(8,128)(2,1)}, u32[]{:S(2)}, u32[]{:S(2)}) %collective-permute-start.3) | collective-permute-done | bytes 786464 | tf_op jit(solution)/shard_map/ppermute | solution.py:56
  112.9 0.6 all-to-all-done.1
  113.6 0.3 split.1
  113.8 0.5 collective-permute-start.5
  114.4 2.2 %collective-permute-start.6 = (bf16[512,768]{1,0:T(8,128)(2,1)S(1)}, bf16[512,768]{1,0:T(8,128)(2,1)S(1)}, u32[]{:S(2)}, u32[]{:S(2)}) collective-permute-start(bf16[512,768]{1,0:T(8,128)(2,1)S(1)} %get-tuple-element.30.refs_3_.refs_2_), channel_id=1, source_target_pairs={{0,3},{4,196},{1,0},{5,197},{2,1},{6,198},{3,2},{7,199},{8,11},{12... | collective-permute-start | bytes 2359304 | tf_op jit(solution)/shard_map/ppermute | solution.py:56
  116.5 0.0 copy-done.8
  116.5 0.0 copy-done.9
  116.6 0.0 copy-done.6
  116.6 0.0 copy-done.7
  116.6 0.1 collective-permute-start.11
  116.7 1.1 collective-permute-start.10
  117.7 0.4 collective-permute-start.9
  118.1 0.0 copy-done.4
  118.1 7.9 %own.1.refs_9_ = f32[128,128]{1,0:T(8,128)S(1)} custom-call(s32[30]{0:T(128)S(1)} %copy-done.4, bf16[1024,768]{1,0:T(8,128)(2,1)S(1)} %bitcast.14, bf16[512,768]{1,0:T(8,128)(2,1)S(1)} %get-tuple-element.29.refs_2_.refs_1_, bf16[512,768]{1,0:T(8,128)(2,1)S(1)} %get-tuple-element.30.refs_3_.refs_2_, f32[8,1024]{1,0:T(8,128)S(1)} %get-tuple-element.31.refs_4_.refs_10_.refs_6_), custom_call_target="tpu_custom_call" | custom-call | flops 4026531840 | bytes 3145728 | tf_op jit(solution)/shard_map/own/pallas_call | solution.py:415
  126.1 0.5 collective-permute-done.5.refs_6_.refs_3_
  126.6 0.0 collective-permute-done.6.refs_7_
  126.6 2.7 %collective-permute-start.8 = (bf16[512,768]{1,0:T(8,128)(2,1)S(1)}, bf16[512,768]{1,0:T(8,128)(2,1)S(1)}, u32[]{:S(2)}, u32[]{:S(2)}) collective-permute-start(bf16[512,768]{1,0:T(8,128)(2,1)S(1)} %collective-permute-done.6.refs_7_), channel_id=1, source_target_pairs={{0,3},{4,196},{1,0},{5,197},{2,1},{6,198},{3,2},{7,199},{8,11},{12... | collective-permute-start | bytes 2359304 | tf_op jit(solution)/shard_map/ppermute | solution.py:56
  129.2 0.0 collective-permute-start.7
  129.2 0.0 collective-permute-done.11.refs_12_
  129.2 0.0 collective-permute-done.10.refs_13_.refs_8_
  129.3 0.0 collective-permute-done.9.refs_11_.refs_7_
  129.3 16.3 %near.1.refs_10_ = f32[128,128]{1,0:T(8,128)S(1)} custom-call(s32[66]{0:T(128)S(1)} %broadcast_select_fusion.refs_0_, bf16[1024,768]{1,0:T(8,128)(2,1)S(1)} %bitcast.15, bf16[512,768]{1,0:T(8,128)(2,1)S(1)} %get-tuple-element.29.refs_2_.refs_1_, bf16[512,768]{1,0:T(8,128)(2,1)S(1)} %get-tuple-element.30.refs_3_.refs_2_, ...), custom_call_target="tpu_custom_call" | custom-call | flops 8858370048 | bytes 7864320 | tf_op jit(solution)/shard_map/near/pallas_call | solution.py:415
  145.6 0.0 collective-permute-done.8.refs_5_
  145.6 0.0 collective-permute-done.7.refs_4_
  145.6 3.4 %far.1 = f32[128,128]{1,0:T(8,128)S(1)} custom-call(s32[6]{0:T(128)S(1)} %broadcast_select_fusion.1.refs_0_, bf16[512,768]{1,0:T(8,128)(2,1)S(1)} %get-tuple-element.29.refs_2_.refs_1_, bf16[512,768]{1,0:T(8,128)(2,1)S(1)} %get-tuple-element.30.refs_3_.refs_2_, bf16[512,768]{1,0:T(8,128)(2,1)S(1)} %collective-permute-done.5.refs_6_.refs_3_, ...), custom_call_target="tpu_custom_call" | custom-call | flops 805306368 | bytes 3932160 | tf_op jit(solution)/shard_map/far/pallas_call | solution.py:415
  149.0 22.2 %all_to_all.15 = f32[128,1,128]{2,1,0:T(1,128)S(1)} all-to-all(f32[128,1,128]{2,1,0:T(1,128)S(1)} %bitcast.16), channel_id=1, replica_groups={{0,1,2,3,8,9,10,11,16,17,18,19,24,25,26,27,32,33,34,35,40,41,42,43,48,4..., dimensions={0} | all-to-all | bytes 131072 | tf_op jit(solution)/shard_map/all_to_all | solution.py:50
  171.1 4.7 %collective-permute-start.12 = (f32[128,128]{1,0:T(8,128)S(1)}, f32[128,128]{1,0:T(8,128)S(1)}, u32[]{:S(2)}, u32[]{:S(2)}) collective-permute-start(f32[128,128]{1,0:T(8,128)S(1)} %bitcast.17), channel_id=1, source_target_pairs={{0,4},{1,5},{2,6},{3,7},{4,0},{5,1},{6,2},{7,3},{8,12},{9,13},{10,... | collective-permute-start | bytes 196616 | tf_op jit(solution)/shard_map/ppermute | solution.py:56
  175.8 0.9 collective-permute-done.12.sibling_ref
  176.7 1.8 %answer.1 = f32[1,1024]{1,0:T(1,128)} custom-call(s32[8,1024]{1,0:T(8,128)S(1)} %copy-done.5, f32[128,128]{1,0:T(8,128)S(1)} %bitcast.18, f32[128,128]{1,0:T(8,128)S(1)} %collective-permute-done.12.sibling_ref), custom_call_target="tpu_custom_call" | custom-call | flops 1207959552 | bytes 196608 | tf_op jit(solution)/shard_map/answer/pallas_call | solution.py:472
  (2 shorter events, 0.0 us)
Async XLA Ops:
  5.6 16.5 %copy-start.2 = (s32[1024]{0:T(1024)S(1)}, s32[1024]{0:T(1024)}, u32[]{:S(2)}) copy-start(s32[1024]{0:T(1024)} %param.9) | copy-start | bytes 12292
  5.6 16.5 %copy-start.3 = (s32[1024]{0:T(1024)S(1)}, s32[1024]{0:T(1024)}, u32[]{:S(2)}) copy-start(s32[1024]{0:T(1024)} %param.10) | copy-start | bytes 12292
  5.6 16.5 %copy-start.5 = (s32[8,1024]{1,0:T(8,128)S(1)}, s32[8,1024]{1,0:T(8,128)}, u32[]{:S(2)}) copy-start(s32[8,1024]{1,0:T(8,128)} %get-tuple-element.22.info_ref) | copy-start | bytes 98308
  5.6 55.2 %all-to-all-start = ((bf16[128,8,768]{2,1,0:T(8,128)(2,1)}), bf16[128,8,768]{2,1,0:T(8,128)(2,1)S(1)}, u32[]{:S(2)}, u32[]{:S(2)}) async-start(bf16[128,8,768]{2,1,0:T(8,128)(2,1)} %bitcast.22), calls=%async_computation | async-start | bytes 3145728 | tf_op jit(solution)/shard_map/all_to_all | solution.py:50
  22.1 1.4 copy-start.1
  26.9 4.5 %collective-permute-start = (bf16[1024,896]{1,0:T(8,128)(2,1)S(1)}, bf16[1024,896]{1,0:T(8,128)(2,1)S(1)}, u32[]{:S(2)}, u32[]{:S(2)}) collective-permute-start(bf16[1024,896]{1,0:T(8,128)(2,1)S(1)} %get-tuple-element.24), channel_id=1, source_target_pairs={{0,4},{1,5},{2,6},{3,7},{4,0},{5,1},{6,2},{7,3},{8,12},{9,13},{10,... | collective-permute-start | bytes 5505032 | tf_op jit(solution)/shard_map/ppermute | solution.py:56
  31.5 1.3 copy-start
  60.8 52.7 %all-to-all-start.1 = ((bf16[128,8,896]{2,1,0:T(8,128)(2,1)}), bf16[128,8,896]{2,1,0:T(8,128)(2,1)S(1)}, u32[]{:S(2)}, u32[]{:S(2)}) async-start(bf16[128,8,896]{2,1,0:T(8,128)(2,1)} %bitcast.12), calls=%async_computation.1 | async-start | bytes 3670016 | tf_op jit(solution)/shard_map/all_to_all | solution.py:50
  69.8 46.8 %copy-start.8 = (s32[66]{0:T(128)S(1)}, s32[66]{0:T(128)}, u32[]{:S(2)}) copy-start(s32[66]{0:T(128)} %constant.29.clone) | copy-start | bytes 796
  69.8 46.8 %copy-start.9 = (s32[66]{0:T(128)S(1)}, s32[66]{0:T(128)}, u32[]{:S(2)}) copy-start(s32[66]{0:T(128)} %constant.28.clone) | copy-start | bytes 796
  69.8 46.8 %copy-start.6 = (s32[6]{0:T(128)S(1)}, s32[6]{0:T(128)}, u32[]{:S(2)}) copy-start(s32[6]{0:T(128)} %constant.31.clone) | copy-start | bytes 76
  69.8 46.8 %copy-start.7 = (s32[6]{0:T(128)S(1)}, s32[6]{0:T(128)}, u32[]{:S(2)}) copy-start(s32[6]{0:T(128)} %constant.30.clone) | copy-start | bytes 76
  69.8 48.3 %copy-start.4 = (s32[30]{0:T(128)S(1)}, s32[30]{0:T(128)}, u32[]{:S(2)}) copy-start(s32[30]{0:T(128)} %constant.27.clone.refs_0_) | copy-start | bytes 364
  70.0 20.1 %collective-permute-start.2 = (bf16[512,768]{1,0:T(8,128)(2,1)S(1)}, bf16[512,768]{1,0:T(8,128)(2,1)}, u32[]{:S(2)}, u32[]{:S(2)}) collective-permute-start(bf16[512,768]{1,0:T(8,128)(2,1)S(1)} %get-tuple-element.39), channel_id=1, source_target_pairs={{0,3},{4,196},{1,0},{5,197},{2,1},{6,198},{3,2},{7,199},{8,11},{12... | collective-permute-start | bytes 2359304 | tf_op jit(solution)/shard_map/ppermute | solution.py:56
  72.3 21.0 %collective-permute-start.1 = (bf16[512,768]{1,0:T(8,128)(2,1)S(1)}, bf16[512,768]{1,0:T(8,128)(2,1)}, u32[]{:S(2)}, u32[]{:S(2)}) collective-permute-start(bf16[512,768]{1,0:T(8,128)(2,1)S(1)} %get-tuple-element.40), channel_id=1, source_target_pairs={{0,1},{4,68},{1,2},{5,69},{2,3},{6,70},{3,0},{7,71},{8,9},{12,76},... | collective-permute-start | bytes 2359304 | tf_op jit(solution)/shard_map/ppermute | solution.py:56
  90.1 18.6 %collective-permute-start.4 = (bf16[512,768]{1,0:T(8,128)(2,1)}, bf16[512,768]{1,0:T(8,128)(2,1)}, u32[]{:S(2)}, u32[]{:S(2)}) collective-permute-start(bf16[512,768]{1,0:T(8,128)(2,1)} %collective-permute-done.2.refs_5_), channel_id=1, source_target_pairs={{0,3},{4,196},{1,0},{5,197},{2,1},{6,198},{3,2},{7,199},{8,11},{12... | collective-permute-start | bytes 2359304 | tf_op jit(solution)/shard_map/ppermute | solution.py:56
  93.3 19.6 %collective-permute-start.3 = (bf16[512,768]{1,0:T(8,128)(2,1)}, bf16[512,768]{1,0:T(8,128)(2,1)}, u32[]{:S(2)}, u32[]{:S(2)}) collective-permute-start(bf16[512,768]{1,0:T(8,128)(2,1)} %collective-permute-done.1.refs_4_), channel_id=1, source_target_pairs={{0,1},{4,68},{1,2},{5,69},{2,3},{6,70},{3,0},{7,71},{8,9},{12,76},... | collective-permute-start | bytes 2359304 | tf_op jit(solution)/shard_map/ppermute | solution.py:56
  113.8 12.7 %collective-permute-start.5 = (bf16[512,768]{1,0:T(8,128)(2,1)S(1)}, bf16[512,768]{1,0:T(8,128)(2,1)S(1)}, u32[]{:S(2)}, u32[]{:S(2)}) collective-permute-start(bf16[512,768]{1,0:T(8,128)(2,1)S(1)} %get-tuple-element.29.refs_2_.refs_1_), channel_id=1, source_target_pairs={{0,1},{4,68},{1,2},{5,69},{2,3},{6,70},{3,0},{7,71},{8,9},{12,76},... | collective-permute-start | bytes 2359304 | tf_op jit(solution)/shard_map/ppermute | solution.py:56
  114.4 12.2 %collective-permute-start.6 = (bf16[512,768]{1,0:T(8,128)(2,1)S(1)}, bf16[512,768]{1,0:T(8,128)(2,1)S(1)}, u32[]{:S(2)}, u32[]{:S(2)}) collective-permute-start(bf16[512,768]{1,0:T(8,128)(2,1)S(1)} %get-tuple-element.30.refs_3_.refs_2_), channel_id=1, source_target_pairs={{0,3},{4,196},{1,0},{5,197},{2,1},{6,198},{3,2},{7,199},{8,11},{12... | collective-permute-start | bytes 2359304 | tf_op jit(solution)/shard_map/ppermute | solution.py:56
  116.6 12.7 %collective-permute-start.11 = (f32[8,1024]{1,0:T(8,128)S(1)}, f32[8,1024]{1,0:T(8,128)S(1)}, u32[]{:S(2)}, u32[]{:S(2)}) collective-permute-start(f32[8,1024]{1,0:T(8,128)S(1)} %get-tuple-element.31.refs_4_.refs_10_.refs_6_), channel_id=1, source_target_pairs={{0,3},{4,196},{1,0},{5,197},{2,1},{6,198},{3,2},{7,199},{8,11},{12... | collective-permute-start | bytes 98312 | tf_op jit(solution)/shard_map/ppermute | solution.py:56
  116.7 12.6 %collective-permute-start.10 = (f32[8,1024]{1,0:T(8,128)S(1)}, f32[8,1024]{1,0:T(8,128)S(1)}, u32[]{:S(2)}, u32[]{:S(2)}) collective-permute-start(f32[8,1024]{1,0:T(8,128)S(1)} %get-tuple-element.31.refs_4_.refs_10_.refs_6_), channel_id=1, source_target_pairs={{0,2},{4,132},{1,3},{5,133},{2,0},{6,134},{3,1},{7,135},{8,10},{12... | collective-permute-start | bytes 98312 | tf_op jit(solution)/shard_map/ppermute | solution.py:56
  117.7 11.5 %collective-permute-start.9 = (f32[8,1024]{1,0:T(8,128)S(1)}, f32[8,1024]{1,0:T(8,128)S(1)}, u32[]{:S(2)}, u32[]{:S(2)}) collective-permute-start(f32[8,1024]{1,0:T(8,128)S(1)} %get-tuple-element.31.refs_4_.refs_10_.refs_6_), channel_id=1, source_target_pairs={{0,1},{4,68},{1,2},{5,69},{2,3},{6,70},{3,0},{7,71},{8,9},{12,76},... | collective-permute-start | bytes 98312 | tf_op jit(solution)/shard_map/ppermute | solution.py:56
  126.6 19.0 %collective-permute-start.8 = (bf16[512,768]{1,0:T(8,128)(2,1)S(1)}, bf16[512,768]{1,0:T(8,128)(2,1)S(1)}, u32[]{:S(2)}, u32[]{:S(2)}) collective-permute-start(bf16[512,768]{1,0:T(8,128)(2,1)S(1)} %collective-permute-done.6.refs_7_), channel_id=1, source_target_pairs={{0,3},{4,196},{1,0},{5,197},{2,1},{6,198},{3,2},{7,199},{8,11},{12... | collective-permute-start | bytes 2359304 | tf_op jit(solution)/shard_map/ppermute | solution.py:56
  129.2 16.3 %collective-permute-start.7 = (bf16[512,768]{1,0:T(8,128)(2,1)S(1)}, bf16[512,768]{1,0:T(8,128)(2,1)S(1)}, u32[]{:S(2)}, u32[]{:S(2)}) collective-permute-start(bf16[512,768]{1,0:T(8,128)(2,1)S(1)} %collective-permute-done.5.refs_6_.refs_3_), channel_id=1, source_target_pairs={{0,1},{4,68},{1,2},{5,69},{2,3},{6,70},{3,0},{7,71},{8,9},{12,76},... | collective-permute-start | bytes 2359304 | tf_op jit(solution)/shard_map/ppermute | solution.py:56
  171.1 5.6 %collective-permute-start.12 = (f32[128,128]{1,0:T(8,128)S(1)}, f32[128,128]{1,0:T(8,128)S(1)}, u32[]{:S(2)}, u32[]{:S(2)}) collective-permute-start(f32[128,128]{1,0:T(8,128)S(1)} %bitcast.17), channel_id=1, source_target_pairs={{0,4},{1,5},{2,6},{3,7},{4,0},{5,1},{6,2},{7,3},{8,12},{9,13},{10,... | collective-permute-start | bytes 196616 | tf_op jit(solution)/shard_map/ppermute | solution.py:56

commit v4 on v3

--- a/solution.py
+++ b/solution.py
@@ -18,6 +18,7 @@
 D = 768
 KEYS = 128
 WIDE = D + KEYS
+EXTRA = 16
 HALF_ROWS = 512
 ORDERS = 4096
 VMEM = 24 * 1024 * 1024
@@ -100,31 +101,24 @@
     return (wide * scale).astype(jnp.bfloat16)
 
 
-PIECE = 256
+PIECE = 512
 PIECES = ROWS // PIECE
-
-
-def prep_kernel(emb_ref, ids_ref, box_ref, info_ref, rows, unit, out, in_sems, out_sems):
-    def piece(number):
-        return pl.ds(number * PIECE, PIECE)
-
-    loads = [
-        pltpu.make_async_copy(emb_ref.at[piece(n)], rows.at[piece(n)], in_sems.at[n]) for n in range(PIECES)
-    ]
-    for load in loads:
-        load.start()
+SPAN = 256
+
+
+def prep_kernel(emb_ref, ids_ref, box_ref, info_ref, rows, out, in_sem, out_sems):
+    load = pltpu.make_async_copy(emb_ref, rows, in_sem)
+    load.start()
     group = ids_ref[...] >> 1
     member = lax.broadcasted_iota(jnp.int32, (GROUPS, ROWS), 0) == group
     hot = jnp.where(member, 1.0, 0.0)
     earlier = jnp.where(
-        lax.broadcasted_iota(jnp.int32, (PIECE, PIECE), 0) < lax.broadcasted_iota(jnp.int32, (PIECE, PIECE), 1),
-        1.0,
-        0.0,
+        lax.broadcasted_iota(jnp.int32, (SPAN, SPAN), 0) < lax.broadcasted_iota(jnp.int32, (SPAN, SPAN), 1), 1.0, 0.0
     ).astype(jnp.bfloat16)
     before = jnp.zeros((GROUPS, 1), jnp.float32)
     ranks = []
-    for n in range(PIECES):
-        here = hot[:, n * PIECE : (n + 1) * PIECE]
+    for n in range(ROWS // SPAN):
+        here = hot[:, n * SPAN : (n + 1) * SPAN]
         count = jnp.dot(here.astype(jnp.bfloat16), earlier, preferred_element_type=jnp.float32) + before
         ranks.append(jnp.sum(here * count, axis=0, keepdims=True))
         before = before + jnp.sum(here, axis=1, keepdims=True)
@@ -133,15 +127,13 @@
     info = jnp.where(which == 0, group, jnp.where(which == 1, rank, 0))
     info_ref[...] = info
     slot = slots_of(info, where_am_i()[3], True)
-
-    for n in range(PIECES):
-        loads[n].wait()
-        unit[piece(n)] = normalize(rows[piece(n)])
+    load.wait()
     stores = []
     for n in range(PIECES):
+        piece = pl.ds(n * PIECE, PIECE)
         pick = onehot(slot, n * PIECE, PIECE)
-        out[piece(n)] = jnp.dot(pick, unit[...], preferred_element_type=jnp.float32).astype(jnp.bfloat16)
-        stores.append(pltpu.make_async_copy(out.at[piece(n)], box_ref.at[piece(n)], out_sems.at[n]))
+        out[piece] = jnp.dot(pick, rows[...], preferred_element_type=jnp.float32).astype(jnp.bfloat16)
+        stores.append(pltpu.make_async_copy(out.at[piece], box_ref.at[piece], out_sems.at[n]))
         stores[-1].start()
     for store in stores:
         store.wait()
@@ -159,8 +151,7 @@
         scratch_shapes=[
             pltpu.VMEM((ROWS, D), jnp.bfloat16),
             pltpu.VMEM((ROWS, D), jnp.bfloat16),
-            pltpu.VMEM((ROWS, D), jnp.bfloat16),
-            pltpu.SemaphoreType.DMA((PIECES,)),
+            pltpu.SemaphoreType.DMA,
             pltpu.SemaphoreType.DMA((PIECES,)),
         ],
         compiler_params=pltpu.CompilerParams(vmem_limit_bytes=FULL),
@@ -220,25 +211,45 @@
     )(box, slab)
 
 
+def settle_kernel(rows_ref, p_ref, m_ref):
+    p_ref[...] = normalize(rows_ref[:HALF_ROWS])
+    m_ref[...] = normalize(rows_ref[HALF_ROWS:])
+
+
+def settle(rows):
+    return pl.pallas_call(
+        settle_kernel,
+        out_shape=tuple([jax.ShapeDtypeStruct((HALF_ROWS, D), jnp.bfloat16)] * 2),
+        in_specs=[pl.BlockSpec(memory_space=pltpu.VMEM)],
+        out_specs=tuple([pl.BlockSpec(memory_space=pltpu.VMEM)] * 2),
+        compiler_params=pltpu.CompilerParams(vmem_limit_bytes=VMEM),
+        cost_estimate=cost(0, 4 * ROWS * D),
+        name="settle",
+    )(rows)
+
+
 def split_kernel(both_ref, p_ref, m_ref, key_ref):
-    p_ref[...] = both_ref[:HALF_ROWS, :D]
-    m_ref[...] = both_ref[HALF_ROWS:, :D]
-    row = lax.broadcasted_iota(jnp.int32, (8, KEYS), 0)
-    lane = lax.broadcasted_iota(jnp.int32, (8, KEYS), 1)
-    first = jnp.where(row == 0, 2, jnp.where(row == 1, 0, KEYS))
-    weight = jnp.where(lane == first, 128.0, jnp.where(lane == first + 1, 1.0, 0.0)).astype(jnp.bfloat16)
-    key_ref[...] = lax.dot_general(
-        weight, both_ref[:, D:], (((1,), (1,)), ((), ())), preferred_element_type=jnp.float32
-    )
+    row = lax.broadcasted_iota(jnp.int32, (EXTRA, KEYS), 0)
+    lane = lax.broadcasted_iota(jnp.int32, (EXTRA, KEYS), 1)
+    source = jnp.where(row < 2, row + 2, jnp.where(row < 4, row - 2, KEYS))
+    weight = jnp.where(lane == source, 1.0, 0.0).astype(jnp.bfloat16)
+    parts = lax.dot_general(weight, both_ref[:, D:], (((1,), (1,)), ((), ())), preferred_element_type=jnp.float32)
+    key_ref[...] = parts
+    for out_ref, first in ((p_ref, 0), (m_ref, HALF_ROWS)):
+        out_ref[:HALF_ROWS] = both_ref[first : first + HALF_ROWS, :D]
+        its = parts[:, first : first + HALF_ROWS]
+        out_ref[HALF_ROWS:] = jnp.concatenate([its, jnp.zeros((EXTRA, D - HALF_ROWS), jnp.float32)], axis=1).astype(
+            jnp.bfloat16
+        )
 
 
 def split(both):
     return pl.pallas_call(
         split_kernel,
         out_shape=(
-            jax.ShapeDtypeStruct((HALF_ROWS, D), jnp.bfloat16),
-            jax.ShapeDtypeStruct((HALF_ROWS, D), jnp.bfloat16),
-            jax.ShapeDtypeStruct((8, ROWS), jnp.float32),
+            jax.ShapeDtypeStruct((HALF_ROWS + EXTRA, D), jnp.bfloat16),
+            jax.ShapeDtypeStruct((HALF_ROWS + EXTRA, D), jnp.bfloat16),
+            jax.ShapeDtypeStruct((EXTRA, ROWS), jnp.float32),
         ),
         in_specs=[pl.BlockSpec(memory_space=pltpu.VMEM)],
         out_specs=tuple([pl.BlockSpec(memory_space=pltpu.VMEM)] * 3),
@@ -289,14 +300,21 @@
     arrays, refs = refs[:n_arrays], refs[n_arrays:]
     key_refs, refs = refs[:n_keys], refs[n_keys:]
     befores, refs = refs[:n_before], refs[n_before:]
-    out_ref, rows, kcol, ccol, krow, crow, best_row, best_col, s0, s1, sems = refs
+    out_ref, rows, extra, kcol, ccol, krow, crow, best_row, best_col, s0, s1, sems, key_sems = refs
     n_blocks = len(blocks)
 
-    copies = []
-    for number, (array, first, slot, task) in enumerate(loads):
-        copy = pltpu.make_async_copy(arrays[array].at[pl.ds(first, HALF_ROWS)], rows.at[slot], sems.at[number])
-        copy.start()
-        copies.append((copy, task))
+    copies, key_copies = [], []
+    for slot, (part, far, chunk, source, rides) in enumerate(blocks):
+        if rides:
+            key_copies.append(
+                pltpu.make_async_copy(arrays[source].at[pl.ds(HALF_ROWS, EXTRA)], extra.at[slot], key_sems.at[slot])
+            )
+            key_copies[-1].start()
+    for number, (array, first, slot) in enumerate(loads):
+        copies.append(
+            pltpu.make_async_copy(arrays[array].at[pl.ds(first, HALF_ROWS)], rows.at[slot], sems.at[number])
+        )
+        copies[-1].start()
     for slot in range(n_blocks):
         best_row[slot] = jnp.full((HALF_ROWS, 128), -1.0, jnp.float32)
         best_col[slot] = jnp.full((8, HALF_ROWS), -1.0, jnp.float32)
@@ -304,19 +322,22 @@
     def cluster(key):
         return jnp.where(key >= ORDERS + 128, 2.0, jnp.where(key > 0, 1.0, 0.0))
 
-    for slot, (part, far, chunk, source) in enumerate(blocks):
-        first = 0 if part == "P" else HALF_ROWS
-        key = key_refs[source][chunk : chunk + 1, first : first + HALF_ROWS]
+    for copy in key_copies:
+        copy.wait()
+    for slot, (part, far, chunk, source, rides) in enumerate(blocks):
+        if rides:
+            parts = extra[slot].astype(jnp.float32)[:, :HALF_ROWS]
+        else:
+            first = 0 if part == "P" else HALF_ROWS
+            parts = key_refs[source][:, first : first + HALF_ROWS]
+        key = 128.0 * parts[2 * chunk : 2 * chunk + 1] + parts[2 * chunk + 1 : 2 * chunk + 2]
         krow[slot] = jnp.broadcast_to(key, (8, HALF_ROWS))
         crow[slot] = cluster(krow[slot])
         key = jnp.transpose(jnp.broadcast_to(key, (128, HALF_ROWS)))
         kcol[slot] = key
         ccol[slot] = cluster(key)
-
-    def arrive(low, high):
-        for copy, task in copies:
-            if low <= task < high:
-                copy.wait()
+    for copy in copies:
+        copy.wait()
 
     def multiply(task, s):
         a, b = tasks_ref[3 * task], tasks_ref[3 * task + 1]
@@ -341,24 +362,15 @@
             best_row[a, row : row + step] = best
 
     def two(turn, carry):
-        for t in range(n_tasks // 2 - 1):
-            if any(2 * t + 1 <= task < 2 * t + 3 for copy, task in copies):
-
-                @pl.when(turn == t)
-                def _():
-                    arrive(2 * t + 1, 2 * t + 3)
-
         multiply(2 * turn + 1, s1)
         reduce(2 * turn, s0)
         multiply(2 * turn + 2, s0)
         reduce(2 * turn + 1, s1)
         return carry
 
-    arrive(0, 1)
     multiply(0, s0)
     if n_tasks > 2:
         lax.fori_loop(0, n_tasks // 2 - 1, two, 0)
-    arrive(n_tasks - 1, n_tasks)
     multiply(n_tasks - 1, s1)
     reduce(n_tasks - 2, s0)
     reduce(n_tasks - 1, s1)
@@ -369,7 +381,7 @@
     )
     for number, part in enumerate("PM"):
         tiles = [empty] * 16
-        for slot, (its, far, chunk, source) in enumerate(blocks):
+        for slot, (its, far, chunk, source, rides) in enumerate(blocks):
             if its == part:
                 by_row = jnp.max(jnp.transpose(best_row[slot]), axis=0, keepdims=True)
                 by_col = jnp.max(best_col[slot], axis=0, keepdims=True)
@@ -406,10 +418,10 @@
     arrays, key_arrays, loads, full = [], [], [], []
     for block in blocks:
         array, first = hold[block]
-        task = min(n for n, pairs in enumerate(zip(low, high)) if any(block in pair for pair in pairs))
-        loads.append((number_of(array, arrays), first, place[block], task))
-        full.append(block + (number_of(keys[block[:2]], key_arrays),))
-    loads.sort(key=lambda load: load[3])
+        loads.append((number_of(array, arrays), first, place[block]))
+    for block in blocks:
+        source, rides = keys[block[:2]]
+        full.append(block + (number_of(source, arrays if rides else key_arrays), rides))
     n = len(blocks)
     kernel = functools.partial(similar_kernel, full, loads, len(low), len(key_arrays), len(befores))
     return pl.pallas_call(
@@ -421,6 +433,7 @@
         out_specs=pl.BlockSpec(memory_space=pltpu.VMEM),
         scratch_shapes=[
             pltpu.VMEM((n, HALF_ROWS, D), jnp.bfloat16),
+            pltpu.VMEM((n, EXTRA, D), jnp.bfloat16),
             pltpu.VMEM((n, HALF_ROWS, 128), jnp.float32),
             pltpu.VMEM((n, HALF_ROWS, 128), jnp.float32),
             pltpu.VMEM((n, 8, HALF_ROWS), jnp.float32),
@@ -429,7 +442,8 @@
             pltpu.VMEM((n + 1, 8, HALF_ROWS), jnp.float32),
             pltpu.VMEM((HALF_ROWS, HALF_ROWS), jnp.float32),
             pltpu.VMEM((HALF_ROWS, HALF_ROWS), jnp.float32),
-            pltpu.SemaphoreType.DMA((len(loads),)),
+            pltpu.SemaphoreType.DMA((n,)),
+            pltpu.SemaphoreType.DMA((n,)),
         ],
         compiler_params=pltpu.CompilerParams(vmem_limit_bytes=32 * 1024 * 1024),
         cost_estimate=cost(2 * D * HALF_ROWS * HALF_ROWS * len(low), 2 * len(loads) * HALF_ROWS * D),
@@ -437,47 +451,46 @@
     )(tasks, *arrays, *key_arrays, *befores)
 
 
-def answer_kernel(info_ref, mine_ref, sibling_ref, out_ref):
-    info = info_ref[...]
+def answer_kernel(away, info_ref, values_ref, *refs):
+    info, out_ref = info_ref[...], refs[-1]
     group, rank = info[0:1], info[1:2]
     x, y, z, core = where_am_i()
     step = jnp.where((y * NZ + z) * NX + x < CHIPS // 2, 1, -1)
-    values = jnp.concatenate([mine_ref[...], sibling_ref[...]], axis=0)
-    device_of = lax.broadcasted_iota(jnp.int32, (2 * CHIPS, ROWS), 0)
+    device_of = lax.broadcasted_iota(jnp.int32, (CHIPS, ROWS), 0)
     lane_of = lax.broadcasted_iota(jnp.int32, (128, ROWS), 0)
-    best = jnp.full((1, ROWS), -1.0, jnp.float32)
     parts = []
-    rest = values
+    rest = values_ref[...]
     for piece in range(3):
         parts.append(rest.astype(jnp.bfloat16))
         rest = rest - parts[-1].astype(jnp.float32)
     parts = jnp.concatenate(parts, axis=0)
+    best = refs[0][...] if away else jnp.full((1, ROWS), -1.0, jnp.float32)
     for far in range(3):
         chip, serving = chip_of(group, (rank + far * step) & 3)
-        away = (serving != core).astype(jnp.int32)
-        pick = jnp.where(device_of == chip + CHIPS * away, 1.0, 0.0).astype(jnp.bfloat16)
+        here = (serving != core) if away else (serving == core)
+        pick = jnp.where(device_of == jnp.where(here, chip, -1), 1.0, 0.0).astype(jnp.bfloat16)
         found = lax.dot_general(
             parts,
             jnp.concatenate([pick] * 3, axis=0),
             (((0,), (0,)), ((), ())),
             preferred_element_type=jnp.float32,
         )
-        wanted = far * 16 + away * SUB + (rank >> 2)
+        wanted = jnp.where(here, far * 16 + away * SUB + (rank >> 2), -1)
         found = jnp.max(jnp.where(lane_of == wanted, found, -1.0), axis=0, keepdims=True)
         best = jnp.maximum(best, found)
     out_ref[...] = best
 
 
-def answer(info, mine, sibling):
-    return pl.pallas_call(
-        answer_kernel,
+def answer(away, info, values, *before):
+    return pl.pallas_call(
+        functools.partial(answer_kernel, away),
         out_shape=jax.ShapeDtypeStruct((1, ROWS), jnp.float32),
-        in_specs=[pl.BlockSpec(memory_space=pltpu.VMEM)] * 3,
+        in_specs=[pl.BlockSpec(memory_space=pltpu.VMEM)] * (2 + len(before)),
         out_specs=pl.BlockSpec(memory_space=pltpu.VMEM),
         compiler_params=pltpu.CompilerParams(vmem_limit_bytes=VMEM),
-        cost_estimate=cost(2 * 3 * 6 * 128 * 256 * ROWS, 3 * 4 * 128 * 128),
+        cost_estimate=cost(2 * 3 * 3 * 128 * 128 * ROWS, 4 * 128 * 128),
         name="answer",
-    )(info, mine, sibling)
+    )(info, values, *before)
 
 
 def local(embeddings, cluster_ids, member_order):
@@ -491,19 +504,19 @@
     handed = stamp(send(handed, SIBLING), slab)
     chunk1, handed = lax.optimization_barrier((chunk1, handed))
     chunk2 = exchange(handed.reshape(CHIPS, SUB, WIDE)).reshape(ROWS, WIDE)
-    near1 = send(chunk1[:HALF_ROWS], ring(1)), send(chunk1[HALF_ROWS:], ring(-1))
+    own1 = settle(chunk1)
+    near1 = send(own1[0], ring(1)), send(own1[1], ring(-1))
     far1 = send(near1[0], ring(1)), send(near1[1], ring(-1))
-    chunk2, near1, far1 = lax.optimization_barrier((chunk2, near1, far1))
-    own2_p, own2_m, key = split(chunk2)
-    own2 = own2_p, own2_m
-    near2 = send(own2_p, ring(1)), send(own2_m, ring(-1))
-    keys = {("P", 0): key, ("M", 0): key, ("P", 1): send(key, ring(1)), ("M", 1): send(key, ring(-1))}
-    keys["P", 2] = keys["M", 2] = send(key, ring(2))
-
-    hold = {}
+    chunk2, own1, near1, far1 = lax.optimization_barrier((chunk2, own1, near1, far1))
+    *own2, key = split(chunk2)
+    near2 = send(own2[0], ring(1)), send(own2[1], ring(-1))
+    far_key = send(key, ring(2))
+
+    hold, keys = {}, {}
     for half, part in enumerate("PM"):
-        hold[part, 0, 0], hold[part, 0, 1] = (chunk1, half * HALF_ROWS), (own2[half], 0)
+        hold[part, 0, 0], hold[part, 0, 1] = (own1[half], 0), (own2[half], 0)
         hold[part, 1, 0], hold[part, 2, 0] = (near1[half], 0), (far1[half], 0)
+        keys[part, 0], keys[part, 2] = (key, False), (far_key, False)
 
     pairs, by_place = pair_lists()
     answers = []
@@ -524,8 +537,10 @@
             far2 = send(near2[0], ring(1)), send(near2[1], ring(-1))
             for half, part in enumerate("PM"):
                 hold[part, 1, 1], hold[part, 2, 1] = (near2[half], 0), (far2[half], 0)
+                keys[part, 1] = (near2[half], True)
     mine = exchange(answers[2].reshape(CHIPS, 1, 128)).reshape(CHIPS, 128)
-    return answer(info, mine, send(mine, SIBLING)).reshape(ROWS)
+    best = answer(0, info, mine)
+    return answer(1, info, send(mine, SIBLING), best).reshape(ROWS)
 
 
 def solution(mesh):

time: 179 us -> 178 us (level)
    all_to_all x2, waiting for transfers between devices: 28.7 us -> 32.1 us  [exchange(): lax.all_to_all(rows, AXES, split_axis=0, concat_axis=0, tiled=True, axis_...]
    ppermute x13 -> x11, waiting for transfers between devices: 42.5 us -> 39.2 us  [send(): return lax.ppermute(rows, AXES, pairs)]
    ppermute x13 -> x11, starting transfers between devices: 18 us -> 16.5 us  [send(): return lax.ppermute(rows, AXES, pairs)]
  transfers between devices with their start and end apart: 15 -> 13, of which waited for: 9 -> 7; matrix products, arithmetic and copies ran while one was open for 0% -> 0% of each run, Pallas kernels for 16% -> 16%
where the time goes in v4:
time: 178 us
  waiting for transfers between devices  71.3 us (40%)
  starting transfers between devices  41.9 us (24%)
  Pallas kernels  39 us (22%)
  blocking collectives  21.9 us (12%)
  local copies, waits for them, and re-layouts  3.13 us (2%)
    ppermute x11, waiting for transfers between devices, send(): return lax.ppermute(rows, AXES, pairs)  39.2 us
    all_to_all x2, waiting for transfers between devices, exchange(): lax.all_to_all(rows, AXES, split_axis=0, concat_axis=0, tiled=True, axis_...  32.1 us
    pallas_call x3, Pallas kernels, similar(): pl.pallas_call(kernel, out_shape=jax.ShapeDtypeStruct((CHIPS, 128), jnp.f...  27.1 us
    all_to_all x2, starting transfers between devices, exchange(): lax.all_to_all(rows, AXES, split_axis=0, concat_axis=0, tiled=True, axis_...  25.4 us
    all_to_all x1, blocking collectives, exchange(): lax.all_to_all(rows, AXES, split_axis=0, concat_axis=0, tiled=True, axis_...  21.9 us
    ppermute x11, starting transfers between devices, send(): return lax.ppermute(rows, AXES, pairs)  16.5 us
    pallas_call x1, Pallas kernels, prep(): pl.pallas_call(prep_kernel, out_shape=(jax.ShapeDtypeStruct((ROWS, D), jn...  5.43 us
  transfers between devices with their start and end apart: 13, of which 7 were waited for; matrix products, arithmetic and copies ran while one was open for 0% of the time, Pallas kernels for 16%

profile of v4, /device:TPU:1, one launch (start us, length us, event | category | flops | bytes accessed | tf_op | source)
XLA Modules:
  0.0 177.6 jit_solution(13345349346794390738)
XLA Ops:
  0.0 5.4 %prep.1 = (bf16[1024,768]{1,0:T(8,128)(2,1)}, s32[8,1024]{1,0:T(8,128)}) custom-call(bf16[1024,768]{1,0:T(8,128)(2,1)} %emb_ref.3, s32[1,1024]{1,0:T(1,128)} %bitcast.17), custom_call_target="tpu_custom_call" | custom-call | flops 1610612736 | bytes 3145728 | tf_op jit(solution)/shard_map/prep/pallas_call | solution.py:143
  5.4 0.0 copy-start.1
  5.4 0.0 copy-start.6
  5.5 0.0 copy-start.7
  5.5 0.0 copy-start.9
  5.5 16.5 %all-to-all-start = ((bf16[128,8,768]{2,1,0:T(8,128)(2,1)}), bf16[128,8,768]{2,1,0:T(8,128)(2,1)S(1)}, u32[]{:S(2)}, u32[]{:S(2)}) async-start(bf16[128,8,768]{2,1,0:T(8,128)(2,1)} %bitcast.20), calls=%async_computation | async-start | bytes 3145728 | tf_op jit(solution)/shard_map/all_to_all | solution.py:51
  22.0 0.0 copy-done.1
  22.0 0.0 copy-done.6
  22.0 0.0 copy-done.7
  22.0 0.0 copy-done.9
  22.0 3.4 %hand.1 = (bf16[1024,896]{1,0:T(8,128)(2,1)S(1)}, bf16[1024,128]{1,0:T(8,128)(2,1)S(1)}) custom-call(bf16[1024,768]{1,0:T(8,128)(2,1)S(1)} %copy-done.1, s32[8,1024]{1,0:T(8,128)S(1)} %copy-done.9, s32[1,1024]{1,0:T(1,128)S(1)} %bitcast.18, s32[1,1024]{1,0:T(1,128)S(1)} %bitcast.19), custom_call_target="tpu_custom_call" | custom-call | flops 1879048192 | bytes 3145728 | tf_op jit(solution)/shard_map/hand/pallas_call | solution.py:179
  25.4 1.0 collective-permute-start
  26.5 3.4 %collective-permute-done.box_ref = bf16[1024,896]{1,0:T(8,128)(2,1)S(1)} collective-permute-done((bf16[1024,896]{1,0:T(8,128)(2,1)S(1)}, bf16[1024,896]{1,0:T(8,128)(2,1)S(1)}, u32[]{:S(2)}, u32[]{:S(2)}) %collective-permute-start) | collective-permute-done | bytes 1835040 | tf_op jit(solution)/shard_map/ppermute | solution.py:57
  29.9 0.2 stamp.1
  30.0 0.0 copy-start
  30.0 1.2 copy-done
  31.3 29.4 %all-to-all-done = bf16[128,8,768]{2,1,0:T(8,128)(2,1)S(1)} async-done(((bf16[128,8,768]{2,1,0:T(8,128)(2,1)}), bf16[128,8,768]{2,1,0:T(8,128)(2,1)S(1)}, u32[]{:S(2)}, u32[]{:S(2)}) %all-to-all-start) | async-done | bytes 1572896 | tf_op jit(solution)/shard_map/all_to_all | solution.py:51
  60.7 8.9 %all-to-all-start.1 = ((bf16[128,8,896]{2,1,0:T(8,128)(2,1)}), bf16[128,8,896]{2,1,0:T(8,128)(2,1)S(1)}, u32[]{:S(2)}, u32[]{:S(2)}) async-start(bf16[128,8,896]{2,1,0:T(8,128)(2,1)} %bitcast.12), calls=%async_computation.1 | async-start | bytes 3670016 | tf_op jit(solution)/shard_map/all_to_all | solution.py:51
  69.7 0.0 copy-start.12
  69.7 0.0 copy-start.13
  69.7 0.0 copy-start.10
  69.7 0.0 copy-start.11
  69.7 0.0 copy-start.8
  69.7 0.6 settle.1
  70.4 0.8 collective-permute-start.1
  71.1 0.0 copy-start.2
  71.1 0.9 copy-done.2
  72.1 0.0 copy-start.3
  72.1 2.0 %collective-permute-start.2 = (bf16[512,768]{1,0:T(8,128)(2,1)S(1)}, bf16[512,768]{1,0:T(8,128)(2,1)}, u32[]{:S(2)}, u32[]{:S(2)}) collective-permute-start(bf16[512,768]{1,0:T(8,128)(2,1)S(1)} %get-tuple-element.38.refs_2_), channel_id=1, source_target_pairs={{0,3},{4,196},{1,0},{5,197},{2,1},{6,198},{3,2},{7,199},{8,11},{12... | collective-permute-start | bytes 2359304 | tf_op jit(solution)/shard_map/ppermute | solution.py:57
  74.1 0.0 copy-start.4
  74.1 0.9 copy-done.4
  75.0 16.5 %collective-permute-done.1.refs_5_ = bf16[512,768]{1,0:T(8,128)(2,1)} collective-permute-done((bf16[512,768]{1,0:T(8,128)(2,1)S(1)}, bf16[512,768]{1,0:T(8,128)(2,1)}, u32[]{:S(2)}, u32[]{:S(2)}) %collective-permute-start.1) | collective-permute-done | bytes 786464 | tf_op jit(solution)/shard_map/ppermute | solution.py:57
  91.5 0.5 collective-permute-start.3
  92.0 0.0 collective-permute-done.2.refs_6_
  92.0 2.6 %collective-permute-start.4 = (bf16[512,768]{1,0:T(8,128)(2,1)}, bf16[512,768]{1,0:T(8,128)(2,1)}, u32[]{:S(2)}, u32[]{:S(2)}) collective-permute-start(bf16[512,768]{1,0:T(8,128)(2,1)} %collective-permute-done.2.refs_6_), channel_id=1, source_target_pairs={{0,3},{4,196},{1,0},{5,197},{2,1},{6,198},{3,2},{7,199},{8,11},{12... | collective-permute-start | bytes 2359304 | tf_op jit(solution)/shard_map/ppermute | solution.py:57
  94.5 16.3 %collective-permute-done.3.refs_9_ = bf16[512,768]{1,0:T(8,128)(2,1)} collective-permute-done((bf16[512,768]{1,0:T(8,128)(2,1)}, bf16[512,768]{1,0:T(8,128)(2,1)}, u32[]{:S(2)}, u32[]{:S(2)}) %collective-permute-start.3) | collective-permute-done | bytes 786464 | tf_op jit(solution)/shard_map/ppermute | solution.py:57
  110.8 0.0 collective-permute-done.4.refs_10_
  110.8 2.6 %all-to-all-done.1 = bf16[128,8,896]{2,1,0:T(8,128)(2,1)S(1)} async-done(((bf16[128,8,896]{2,1,0:T(8,128)(2,1)}), bf16[128,8,896]{2,1,0:T(8,128)(2,1)S(1)}, u32[]{:S(2)}, u32[]{:S(2)}) %all-to-all-start.1) | async-done | bytes 1835040 | tf_op jit(solution)/shard_map/all_to_all | solution.py:51
  113.5 0.2 split.1
  113.7 0.5 collective-permute-start.5
  114.2 2.2 %collective-permute-start.6 = (bf16[528,768]{1,0:T(8,128)(2,1)S(1)}, bf16[528,768]{1,0:T(8,128)(2,1)S(1)}, u32[]{:S(2)}, u32[]{:S(2)}) collective-permute-start(bf16[528,768]{1,0:T(8,128)(2,1)S(1)} %get-tuple-element.36.refs_4_.refs_2_), channel_id=1, source_target_pairs={{0,3},{4,196},{1,0},{5,197},{2,1},{6,198},{3,2},{7,199},{8,11},{12... | collective-permute-start | bytes 2433032 | tf_op jit(solution)/shard_map/ppermute | solution.py:57
  116.4 0.0 copy-done.12
  116.4 0.0 copy-done.13
  116.4 0.0 copy-done.10
  116.4 0.0 copy-done.11
  116.4 0.1 collective-permute-start.9
  116.5 0.0 copy-done.8
  116.5 0.0 copy-done.3
  116.5 0.0 copy-done.5
  116.5 7.6 %own.1.refs_8_ = f32[128,128]{1,0:T(8,128)S(1)} custom-call(s32[30]{0:T(128)S(1)} %copy-done.8, bf16[512,768]{1,0:T(8,128)(2,1)S(1)} %copy-done.3, bf16[512,768]{1,0:T(8,128)(2,1)S(1)} %copy-done.5, bf16[528,768]{1,0:T(8,128)(2,1)S(1)} %get-tuple-element.35.refs_3_.refs_1_, bf16[528,768]{1,0:T(8,128)(2,1)S(1)} %get-tuple-element.36.refs_4_.refs_2_, ...), custom_call_target="tpu_custom_call" | custom-call | flops 4026531840 | bytes 3145728 | tf_op jit(solution)/shard_map/own/pallas_call | solution.py:427
  124.1 2.9 %collective-permute-done.5.refs_7_.refs_3_ = bf16[528,768]{1,0:T(8,128)(2,1)S(1)} collective-permute-done((bf16[528,768]{1,0:T(8,128)(2,1)S(1)}, bf16[528,768]{1,0:T(8,128)(2,1)S(1)}, u32[]{:S(2)}, u32[]{:S(2)}) %collective-permute-start.5) | collective-permute-done | bytes 811040 | tf_op jit(solution)/shard_map/ppermute | solution.py:57
  127.0 0.0 collective-permute-done.6.refs_8_
  127.0 2.7 %collective-permute-start.8 = (bf16[528,768]{1,0:T(8,128)(2,1)S(1)}, bf16[528,768]{1,0:T(8,128)(2,1)S(1)}, u32[]{:S(2)}, u32[]{:S(2)}) collective-permute-start(bf16[528,768]{1,0:T(8,128)(2,1)S(1)} %collective-permute-done.6.refs_8_), channel_id=1, source_target_pairs={{0,3},{4,196},{1,0},{5,197},{2,1},{6,198},{3,2},{7,199},{8,11},{12... | collective-permute-start | bytes 2433032 | tf_op jit(solution)/shard_map/ppermute | solution.py:57
  129.7 0.0 collective-permute-start.7
  129.7 0.0 collective-permute-done.9.refs_12_.refs_7_
  129.7 16.3 %near.1.refs_9_ = f32[128,128]{1,0:T(8,128)S(1)} custom-call(s32[66]{0:T(128)S(1)} %broadcast_select_fusion.refs_0_, bf16[512,768]{1,0:T(8,128)(2,1)S(1)} %copy-done.3, bf16[512,768]{1,0:T(8,128)(2,1)S(1)} %copy-done.5, bf16[528,768]{1,0:T(8,128)(2,1)S(1)} %get-tuple-element.35.refs_3_.refs_1_, bf16[528,768]{1,0:T(8,128)(2,1)S(1)} %get-tuple-element.36.refs_4_.refs_2_, ...), custom_call_target="tpu_custom_call" | custom-call | flops 8858370048 | bytes 7864320 | tf_op jit(solution)/shard_map/near/pallas_call | solution.py:427
  146.0 0.0 collective-permute-done.8.refs_5_
  146.0 0.0 collective-permute-done.7.refs_4_
  146.0 3.2 %far.1 = f32[128,128]{1,0:T(8,128)S(1)} custom-call(s32[6]{0:T(128)S(1)} %broadcast_select_fusion.1.refs_0_, bf16[528,768]{1,0:T(8,128)(2,1)S(1)} %get-tuple-element.35.refs_3_.refs_1_, bf16[528,768]{1,0:T(8,128)(2,1)S(1)} %get-tuple-element.36.refs_4_.refs_2_, bf16[528,768]{1,0:T(8,128)(2,1)S(1)} %collective-permute-done.5.refs_7_.refs_3_, ...), custom_call_target="tpu_custom_call" | custom-call | flops 805306368 | bytes 3932160 | tf_op jit(solution)/shard_map/far/pallas_call | solution.py:427
  149.2 21.9 %all_to_all.15 = f32[128,1,128]{2,1,0:T(1,128)S(1)} all-to-all(f32[128,1,128]{2,1,0:T(1,128)S(1)} %bitcast.14), channel_id=1, replica_groups={{0,1,2,3,8,9,10,11,16,17,18,19,24,25,26,27,32,33,34,35,40,41,42,43,48,4..., dimensions={0} | all-to-all | bytes 131072 | tf_op jit(solution)/shard_map/all_to_all | solution.py:51
  171.1 4.2 %collective-permute-start.10 = (f32[128,128]{1,0:T(8,128)S(1)}, f32[128,128]{1,0:T(8,128)S(1)}, u32[]{:S(2)}, u32[]{:S(2)}) collective-permute-start(f32[128,128]{1,0:T(8,128)S(1)} %bitcast.15), channel_id=1, source_target_pairs={{0,4},{1,5},{2,6},{3,7},{4,0},{5,1},{6,2},{7,3},{8,12},{9,13},{10,... | collective-permute-start | bytes 196616 | tf_op jit(solution)/shard_map/ppermute | solution.py:57
  175.3 0.8 answer.2.refs_0_
  176.1 0.1 collective-permute-done.10.values_ref
  176.2 1.4 answer.3
  (3 shorter events, 0.0 us)
Async XLA Ops:
  5.4 16.5 %copy-start.1 = (bf16[1024,768]{1,0:T(8,128)(2,1)S(1)}, bf16[1024,768]{1,0:T(8,128)(2,1)}, u32[]{:S(2)}) copy-start(bf16[1024,768]{1,0:T(8,128)(2,1)} %emb_ref.3) | copy-start | bytes 4718596
  5.4 16.5 %copy-start.6 = (s32[1024]{0:T(1024)S(1)}, s32[1024]{0:T(1024)}, u32[]{:S(2)}) copy-start(s32[1024]{0:T(1024)} %param.9) | copy-start | bytes 12292
  5.5 16.5 %copy-start.7 = (s32[1024]{0:T(1024)S(1)}, s32[1024]{0:T(1024)}, u32[]{:S(2)}) copy-start(s32[1024]{0:T(1024)} %param.10) | copy-start | bytes 12292
  5.5 16.5 %copy-start.9 = (s32[8,1024]{1,0:T(8,128)S(1)}, s32[8,1024]{1,0:T(8,128)}, u32[]{:S(2)}) copy-start(s32[8,1024]{1,0:T(8,128)} %get-tuple-element.26.info_ref) | copy-start | bytes 98308
  5.5 55.2 %all-to-all-start = ((bf16[128,8,768]{2,1,0:T(8,128)(2,1)}), bf16[128,8,768]{2,1,0:T(8,128)(2,1)S(1)}, u32[]{:S(2)}, u32[]{:S(2)}) async-start(bf16[128,8,768]{2,1,0:T(8,128)(2,1)} %bitcast.20), calls=%async_computation | async-start | bytes 3145728 | tf_op jit(solution)/shard_map/all_to_all | solution.py:51
  25.4 4.5 %collective-permute-start = (bf16[1024,896]{1,0:T(8,128)(2,1)S(1)}, bf16[1024,896]{1,0:T(8,128)(2,1)S(1)}, u32[]{:S(2)}, u32[]{:S(2)}) collective-permute-start(bf16[1024,896]{1,0:T(8,128)(2,1)S(1)} %get-tuple-element.28), channel_id=1, source_target_pairs={{0,4},{1,5},{2,6},{3,7},{4,0},{5,1},{6,2},{7,3},{8,12},{9,13},{10,... | collective-permute-start | bytes 5505032 | tf_op jit(solution)/shard_map/ppermute | solution.py:57
  30.0 1.3 copy-start
  60.7 52.8 %all-to-all-start.1 = ((bf16[128,8,896]{2,1,0:T(8,128)(2,1)}), bf16[128,8,896]{2,1,0:T(8,128)(2,1)S(1)}, u32[]{:S(2)}, u32[]{:S(2)}) async-start(bf16[128,8,896]{2,1,0:T(8,128)(2,1)} %bitcast.12), calls=%async_computation.1 | async-start | bytes 3670016 | tf_op jit(solution)/shard_map/all_to_all | solution.py:51
  69.7 46.7 %copy-start.12 = (s32[66]{0:T(128)S(1)}, s32[66]{0:T(128)}, u32[]{:S(2)}) copy-start(s32[66]{0:T(128)} %constant.29.clone) | copy-start | bytes 796
  69.7 46.7 %copy-start.13 = (s32[66]{0:T(128)S(1)}, s32[66]{0:T(128)}, u32[]{:S(2)}) copy-start(s32[66]{0:T(128)} %constant.28.clone) | copy-start | bytes 796
  69.7 46.7 %copy-start.10 = (s32[6]{0:T(128)S(1)}, s32[6]{0:T(128)}, u32[]{:S(2)}) copy-start(s32[6]{0:T(128)} %constant.31.clone) | copy-start | bytes 76
  69.7 46.7 %copy-start.11 = (s32[6]{0:T(128)S(1)}, s32[6]{0:T(128)}, u32[]{:S(2)}) copy-start(s32[6]{0:T(128)} %constant.30.clone) | copy-start | bytes 76
  69.7 46.8 %copy-start.8 = (s32[30]{0:T(128)S(1)}, s32[30]{0:T(128)}, u32[]{:S(2)}) copy-start(s32[30]{0:T(128)} %constant.27.clone.refs_0_) | copy-start | bytes 364
  70.4 21.1 %collective-permute-start.1 = (bf16[512,768]{1,0:T(8,128)(2,1)S(1)}, bf16[512,768]{1,0:T(8,128)(2,1)}, u32[]{:S(2)}, u32[]{:S(2)}) collective-permute-start(bf16[512,768]{1,0:T(8,128)(2,1)S(1)} %get-tuple-element.37.refs_1_), channel_id=1, source_target_pairs={{0,1},{4,68},{1,2},{5,69},{2,3},{6,70},{3,0},{7,71},{8,9},{12,76},... | collective-permute-start | bytes 2359304 | tf_op jit(solution)/shard_map/ppermute | solution.py:57
  71.1 0.9 copy-start.2
  72.1 44.5 %copy-start.3 = (bf16[512,768]{1,0:T(8,128)(2,1)S(1)}, bf16[512,768]{1,0:T(8,128)(2,1)}, u32[]{:S(2)}) copy-start(bf16[512,768]{1,0:T(8,128)(2,1)} %copy-done.2) | copy-start | bytes 2359300
  72.1 19.9 %collective-permute-start.2 = (bf16[512,768]{1,0:T(8,128)(2,1)S(1)}, bf16[512,768]{1,0:T(8,128)(2,1)}, u32[]{:S(2)}, u32[]{:S(2)}) collective-permute-start(bf16[512,768]{1,0:T(8,128)(2,1)S(1)} %get-tuple-element.38.refs_2_), channel_id=1, source_target_pairs={{0,3},{4,196},{1,0},{5,197},{2,1},{6,198},{3,2},{7,199},{8,11},{12... | collective-permute-start | bytes 2359304 | tf_op jit(solution)/shard_map/ppermute | solution.py:57
  74.1 0.9 copy-start.4
  91.5 25.1 %copy-start.5 = (bf16[512,768]{1,0:T(8,128)(2,1)S(1)}, bf16[512,768]{1,0:T(8,128)(2,1)}, u32[]{:S(2)}) copy-start(bf16[512,768]{1,0:T(8,128)(2,1)} %copy-done.4) | copy-start | bytes 2359300
  91.5 19.4 %collective-permute-start.3 = (bf16[512,768]{1,0:T(8,128)(2,1)}, bf16[512,768]{1,0:T(8,128)(2,1)}, u32[]{:S(2)}, u32[]{:S(2)}) collective-permute-start(bf16[512,768]{1,0:T(8,128)(2,1)} %collective-permute-done.1.refs_5_), channel_id=1, source_target_pairs={{0,1},{4,68},{1,2},{5,69},{2,3},{6,70},{3,0},{7,71},{8,9},{12,76},... | collective-permute-start | bytes 2359304 | tf_op jit(solution)/shard_map/ppermute | solution.py:57
  92.0 18.9 %collective-permute-start.4 = (bf16[512,768]{1,0:T(8,128)(2,1)}, bf16[512,768]{1,0:T(8,128)(2,1)}, u32[]{:S(2)}, u32[]{:S(2)}) collective-permute-start(bf16[512,768]{1,0:T(8,128)(2,1)} %collective-permute-done.2.refs_6_), channel_id=1, source_target_pairs={{0,3},{4,196},{1,0},{5,197},{2,1},{6,198},{3,2},{7,199},{8,11},{12... | collective-permute-start | bytes 2359304 | tf_op jit(solution)/shard_map/ppermute | solution.py:57
  113.7 13.3 %collective-permute-start.5 = (bf16[528,768]{1,0:T(8,128)(2,1)S(1)}, bf16[528,768]{1,0:T(8,128)(2,1)S(1)}, u32[]{:S(2)}, u32[]{:S(2)}) collective-permute-start(bf16[528,768]{1,0:T(8,128)(2,1)S(1)} %get-tuple-element.35.refs_3_.refs_1_), channel_id=1, source_target_pairs={{0,1},{4,68},{1,2},{5,69},{2,3},{6,70},{3,0},{7,71},{8,9},{12,76},... | collective-permute-start | bytes 2433032 | tf_op jit(solution)/shard_map/ppermute | solution.py:57
  114.2 12.8 %collective-permute-start.6 = (bf16[528,768]{1,0:T(8,128)(2,1)S(1)}, bf16[528,768]{1,0:T(8,128)(2,1)S(1)}, u32[]{:S(2)}, u32[]{:S(2)}) collective-permute-start(bf16[528,768]{1,0:T(8,128)(2,1)S(1)} %get-tuple-element.36.refs_4_.refs_2_), channel_id=1, source_target_pairs={{0,3},{4,196},{1,0},{5,197},{2,1},{6,198},{3,2},{7,199},{8,11},{12... | collective-permute-start | bytes 2433032 | tf_op jit(solution)/shard_map/ppermute | solution.py:57
  116.4 13.3 %collective-permute-start.9 = (f32[16,1024]{1,0:T(8,128)S(1)}, f32[16,1024]{1,0:T(8,128)S(1)}, u32[]{:S(2)}, u32[]{:S(2)}) collective-permute-start(f32[16,1024]{1,0:T(8,128)S(1)} %get-tuple-element.39.refs_5_.refs_11_.refs_6_), channel_id=1, source_target_pairs={{0,2},{4,132},{1,3},{5,133},{2,0},{6,134},{3,1},{7,135},{8,10},{12... | collective-permute-start | bytes 196616 | tf_op jit(solution)/shard_map/ppermute | solution.py:57
  127.0 19.0 %collective-permute-start.8 = (bf16[528,768]{1,0:T(8,128)(2,1)S(1)}, bf16[528,768]{1,0:T(8,128)(2,1)S(1)}, u32[]{:S(2)}, u32[]{:S(2)}) collective-permute-start(bf16[528,768]{1,0:T(8,128)(2,1)S(1)} %collective-permute-done.6.refs_8_), channel_id=1, source_target_pairs={{0,3},{4,196},{1,0},{5,197},{2,1},{6,198},{3,2},{7,199},{8,11},{12... | collective-permute-start | bytes 2433032 | tf_op jit(solution)/shard_map/ppermute | solution.py:57
  129.7 16.3 %collective-permute-start.7 = (bf16[528,768]{1,0:T(8,128)(2,1)S(1)}, bf16[528,768]{1,0:T(8,128)(2,1)S(1)}, u32[]{:S(2)}, u32[]{:S(2)}) collective-permute-start(bf16[528,768]{1,0:T(8,128)(2,1)S(1)} %collective-permute-done.5.refs_7_.refs_3_), channel_id=1, source_target_pairs={{0,1},{4,68},{1,2},{5,69},{2,3},{6,70},{3,0},{7,71},{8,9},{12,76},... | collective-permute-start | bytes 2433032 | tf_op jit(solution)/shard_map/ppermute | solution.py:57
  171.1 5.1 %collective-permute-start.10 = (f32[128,128]{1,0:T(8,128)S(1)}, f32[128,128]{1,0:T(8,128)S(1)}, u32[]{:S(2)}, u32[]{:S(2)}) collective-permute-start(f32[128,128]{1,0:T(8,128)S(1)} %bitcast.15), channel_id=1, source_target_pairs={{0,4},{1,5},{2,6},{3,7},{4,0},{5,1},{6,2},{7,3},{8,12},{9,13},{10,... | collective-permute-start | bytes 196616 | tf_op jit(solution)/shard_map/ppermute | solution.py:57

commit v5 on v4

--- a/solution.py
+++ b/solution.py
@@ -13,7 +13,8 @@
 CHIPS = NX * NY * NZ
 GROUPS = 64
 HALF = GROUPS // 2
-SUB = 8
+SOURCES = 32
+CAP = 32
 ROWS = 1024
 D = 768
 KEYS = 128
@@ -29,8 +30,12 @@
     return ((y * NZ + z) * 2 + core) * NX + x
 
 
-SAME_CORE = [
-    [device(x, y, z, core) for y in range(NY) for z in range(NZ) for x in range(NX)] for core in range(2)
+ROUTES = [[device(x, y, z, 0) for y in range(NY) for z in range(NZ)] for x in range(NX)] + [
+    [device(x, y, z, 1) for x in range(NX) for z in range(NZ)] for y in range(NY)
+]
+RETURNS = [
+    [device(x, y, z, 0) for y in range(NY) for z in range(NZ) for x in range(NX)],
+    [device(x, y, z, 1) for x in range(NX) for z in range(NZ) for y in range(NY)],
 ]
 
 
@@ -47,10 +52,8 @@
 SIBLING = [(dp * NX + x, (dp ^ 1) * NX + x) for dp in range(NY * NZ * 2) for x in range(NX)]
 
 
-def exchange(rows):
-    return lax.all_to_all(
-        rows, AXES, split_axis=0, concat_axis=0, tiled=True, axis_index_groups=SAME_CORE
-    )
+def exchange(rows, groups):
+    return lax.all_to_all(rows, AXES, split_axis=0, concat_axis=0, tiled=True, axis_index_groups=groups)
 
 
 def send(rows, pairs):
@@ -59,14 +62,6 @@
 
 def cost(flops, size):
     return pl.CostEstimate(flops=flops, bytes_accessed=size, transcendentals=0)
-
-
-def chip_of(group, place):
-    core = (group >= HALF).astype(jnp.int32)
-    inner = group - HALF * core
-    on_x = inner * NX + place
-    on_y = (place * NZ + (inner & (NZ - 1))) * NX + (inner >> 3)
-    return jnp.where(core == 0, on_x, on_y), core
 
 
 def key_rows(ids, order, first):
@@ -85,8 +80,8 @@
 
 def slots_of(info, core, mine):
     group, rank = info[0:1], info[1:2]
-    chip, serving = chip_of(group, rank & 3)
-    slot = chip * SUB + (rank >> 2)
+    serving = group >> 5
+    slot = (group & (HALF - 1)) * CAP + rank
     return jnp.where((serving == core) if mine else (serving != core), slot, -1)
 
 
@@ -294,6 +289,14 @@
     return 2 if any(far == 2 and chunk == 1 for part, far, chunk in pair) else 1
 
 
+def three_parts(values):
+    parts = []
+    for piece in range(3):
+        parts.append(values.astype(jnp.bfloat16))
+        values = values - parts[-1].astype(jnp.float32)
+    return parts
+
+
 def similar_kernel(blocks, loads, n_tasks, n_keys, n_before, *refs):
     n_arrays = 1 + max(load[0] for load in loads)
     tasks_ref, refs = refs[0], refs[1:]
@@ -375,23 +378,45 @@
     reduce(n_tasks - 2, s0)
     reduce(n_tasks - 1, s1)
 
-    empty = jnp.full((8, HALF_ROWS), -1.0, jnp.float32)
-    diagonal = lax.broadcasted_iota(jnp.int32, (8, HALF_ROWS), 0) == (
-        lax.broadcasted_iota(jnp.int32, (8, HALF_ROWS), 1) & (SUB - 1)
+    empty = jnp.full((CAP, HALF_ROWS), -1.0, jnp.float32)
+    diagonal = lax.broadcasted_iota(jnp.int32, (CAP, HALF_ROWS), 0) == (
+        lax.broadcasted_iota(jnp.int32, (CAP, HALF_ROWS), 1) & (CAP - 1)
     )
+    values = {}
     for number, part in enumerate("PM"):
-        tiles = [empty] * 16
-        for slot, (its, far, chunk, source, rides) in enumerate(blocks):
-            if its == part:
-                by_row = jnp.max(jnp.transpose(best_row[slot]), axis=0, keepdims=True)
-                by_col = jnp.max(best_col[slot], axis=0, keepdims=True)
-                tiles[2 * far + chunk] = jnp.where(diagonal, jnp.maximum(by_row, by_col), -1.0)
-        value = jnp.transpose(jnp.concatenate(tiles, axis=0)).reshape(HALF_ROWS // SUB, SUB, 128)
-        value = jnp.max(value, axis=1)
-        at = pl.ds(number * (CHIPS // 2), CHIPS // 2)
-        for before in befores:
-            value = jnp.maximum(value, before[at, :])
-        out_ref[at, :] = value
+        for level in range(2):
+            tiles = [empty] * 4
+            for slot, (its, far, chunk, source, rides) in enumerate(blocks):
+                if its == part and far // 2 == level:
+                    by_row = jnp.max(jnp.transpose(best_row[slot]), axis=0, keepdims=True)
+                    by_col = jnp.max(best_col[slot], axis=0, keepdims=True)
+                    tiles[2 * (far & 1) + chunk] = jnp.where(diagonal, jnp.maximum(by_row, by_col), -1.0)
+            if all(tile is empty for tile in tiles):
+                value = jnp.full((HALF_ROWS // CAP, 128), -1.0, jnp.float32)
+            else:
+                value = jnp.transpose(jnp.concatenate(tiles, axis=0)).reshape(HALF_ROWS // CAP, CAP, 128)
+                value = jnp.max(value, axis=1)
+            at = pl.ds(level * SOURCES + number * (SOURCES // 2), SOURCES // 2)
+            for before in befores:
+                value = jnp.maximum(value, before[at, :])
+            values[level, number] = value
+    values = jnp.concatenate([values[level, number] for level in range(2) for number in range(2)], axis=0)
+    if not befores:
+        out_ref[...] = values
+        return
+    x, y, z, core = where_am_i()
+    here = jnp.where(core == 0, x, y)
+    row = lax.broadcasted_iota(jnp.int32, (CHIPS, 2 * SOURCES), 0)
+    column = lax.broadcasted_iota(jnp.int32, (CHIPS, 2 * SOURCES), 1)
+    source, step = row >> 2, jnp.where(row < CHIPS // 2, 1, -1)
+    far = ((here - (row & 3)) * step) & 3
+    wanted = (column == source) & (far < 2) | (column == source + SOURCES) & (far == 2)
+    pick = jnp.where(wanted, 1.0, 0.0).astype(jnp.bfloat16)
+    out_ref[...] = jnp.dot(
+        jnp.concatenate([pick] * 3, axis=1),
+        jnp.concatenate(three_parts(values), axis=0),
+        preferred_element_type=jnp.float32,
+    )
 
 
 def similar(hold, keys, low, high, ring_place, befores, name):
@@ -426,7 +451,7 @@
     kernel = functools.partial(similar_kernel, full, loads, len(low), len(key_arrays), len(befores))
     return pl.pallas_call(
         kernel,
-        out_shape=jax.ShapeDtypeStruct((CHIPS, 128), jnp.float32),
+        out_shape=jax.ShapeDtypeStruct((CHIPS if befores else 2 * SOURCES, 128), jnp.float32),
         in_specs=[pl.BlockSpec(memory_space=pltpu.SMEM)]
         + [pl.BlockSpec(memory_space=pl.ANY)] * len(arrays)
         + [pl.BlockSpec(memory_space=pltpu.VMEM)] * (len(key_arrays) + len(befores)),
@@ -455,27 +480,24 @@
     info, out_ref = info_ref[...], refs[-1]
     group, rank = info[0:1], info[1:2]
     x, y, z, core = where_am_i()
-    step = jnp.where((y * NZ + z) * NX + x < CHIPS // 2, 1, -1)
+    serving = (core + away) & 1
+    here = (group >> 5) == serving
+    ring_place, source = jnp.where(serving == 0, x, y), jnp.where(serving == 0, y, x)
+    step = jnp.where(source < 2, 1, -1)
     device_of = lax.broadcasted_iota(jnp.int32, (CHIPS, ROWS), 0)
     lane_of = lax.broadcasted_iota(jnp.int32, (128, ROWS), 0)
-    parts = []
-    rest = values_ref[...]
-    for piece in range(3):
-        parts.append(rest.astype(jnp.bfloat16))
-        rest = rest - parts[-1].astype(jnp.float32)
-    parts = jnp.concatenate(parts, axis=0)
+    parts = jnp.concatenate(three_parts(values_ref[...]), axis=0)
     best = refs[0][...] if away else jnp.full((1, ROWS), -1.0, jnp.float32)
     for far in range(3):
-        chip, serving = chip_of(group, (rank + far * step) & 3)
-        here = (serving != core) if away else (serving == core)
-        pick = jnp.where(device_of == jnp.where(here, chip, -1), 1.0, 0.0).astype(jnp.bfloat16)
+        holder = (group & (HALF - 1)) * 4 + ((ring_place + far * step) & 3)
+        pick = jnp.where(device_of == jnp.where(here, holder, -1), 1.0, 0.0).astype(jnp.bfloat16)
         found = lax.dot_general(
             parts,
             jnp.concatenate([pick] * 3, axis=0),
             (((0,), (0,)), ((), ())),
             preferred_element_type=jnp.float32,
         )
-        wanted = jnp.where(here, far * 16 + away * SUB + (rank >> 2), -1)
+        wanted = jnp.where(here, (far & 1) * 64 + away * CAP + rank, -1)
         found = jnp.max(jnp.where(lane_of == wanted, found, -1.0), axis=0, keepdims=True)
         best = jnp.maximum(best, found)
     out_ref[...] = best
@@ -499,11 +521,11 @@
     ids, order = cluster_ids.reshape(1, ROWS), member_order.reshape(1, ROWS)
 
     box, info = prep(embeddings, ids)
-    chunk1 = exchange(box.reshape(CHIPS, SUB, D)).reshape(ROWS, D)
+    chunk1 = exchange(box.reshape(SOURCES, CAP, D), ROUTES).reshape(ROWS, D)
     handed, slab = hand(embeddings, info, ids, order)
     handed = stamp(send(handed, SIBLING), slab)
     chunk1, handed = lax.optimization_barrier((chunk1, handed))
-    chunk2 = exchange(handed.reshape(CHIPS, SUB, WIDE)).reshape(ROWS, WIDE)
+    chunk2 = exchange(handed.reshape(SOURCES, CAP, WIDE), ROUTES).reshape(ROWS, WIDE)
     own1 = settle(chunk1)
     near1 = send(own1[0], ring(1)), send(own1[1], ring(-1))
     far1 = send(near1[0], ring(1)), send(near1[1], ring(-1))
@@ -538,7 +560,7 @@
             for half, part in enumerate("PM"):
                 hold[part, 1, 1], hold[part, 2, 1] = (near2[half], 0), (far2[half], 0)
                 keys[part, 1] = (near2[half], True)
-    mine = exchange(answers[2].reshape(CHIPS, 1, 128)).reshape(CHIPS, 128)
+    mine = exchange(answers[2].reshape(CHIPS, 1, 128), RETURNS).reshape(CHIPS, 128)
     best = answer(0, info, mine)
     return answer(1, info, send(mine, SIBLING), best).reshape(ROWS)
 

time: 178 us -> 170 us (0.955)
  waiting for transfers between devices: 71.3 us -> 66.8 us
  starting transfers between devices: 41.9 us -> 38.7 us
    ppermute x11, waiting for transfers between devices: 39.2 us -> 27.3 us  [send(): return lax.ppermute(rows, AXES, pairs)]
    all_to_all x2, waiting for transfers between devices: 32.1 us -> 39.5 us  [exchange(): lax.all_to_all(rows, AXES, split_axis=0, concat_axis=0, tiled=True, axis_...]
    all_to_all x2, starting transfers between devices: 25.4 us -> 19.1 us  [exchange(): lax.all_to_all(rows, AXES, split_axis=0, concat_axis=0, tiled=True, axis_...]
    ppermute x11, starting transfers between devices: 16.5 us -> 19.6 us  [send(): return lax.ppermute(rows, AXES, pairs)]
  transfers between devices with their start and end apart: 13 -> 13, of which waited for: 7 -> 7; matrix products, arithmetic and copies ran while one was open for 0% -> 0% of each run, Pallas kernels for 16% -> 17%
where the time goes in v5:
time: 170 us
  waiting for transfers between devices  66.8 us (39%)
  Pallas kernels  39.6 us (23%)
  starting transfers between devices  38.7 us (23%)
  blocking collectives  21.2 us (12%)
  local copies, waits for them, and re-layouts  3.13 us (2%)
    all_to_all x2, waiting for transfers between devices, exchange(): lax.all_to_all(rows, AXES, split_axis=0, concat_axis=0, tiled=True, axis_...  39.5 us
    pallas_call x3, Pallas kernels, similar(): pl.pallas_call(kernel, out_shape=jax.ShapeDtypeStruct((CHIPS if befores e...  27.5 us
    ppermute x11, waiting for transfers between devices, send(): return lax.ppermute(rows, AXES, pairs)  27.3 us
    all_to_all x1, blocking collectives, exchange(): lax.all_to_all(rows, AXES, split_axis=0, concat_axis=0, tiled=True, axis_...  21.2 us
    ppermute x11, starting transfers between devices, send(): return lax.ppermute(rows, AXES, pairs)  19.6 us
    all_to_all x2, starting transfers between devices, exchange(): lax.all_to_all(rows, AXES, split_axis=0, concat_axis=0, tiled=True, axis_...  19.1 us
    pallas_call x1, Pallas kernels, prep(): pl.pallas_call(prep_kernel, out_shape=(jax.ShapeDtypeStruct((ROWS, D), jn...  5.43 us
  transfers between devices with their start and end apart: 13, of which 7 were waited for; matrix products, arithmetic and copies ran while one was open for 0% of the time, Pallas kernels for 17%

profile of v5, /device:TPU:1, one launch (start us, length us, event | category | flops | bytes accessed | tf_op | source)
XLA Modules:
  0.0 169.7 jit_solution(7942915408155083973)
XLA Ops:
  0.0 5.4 %prep.1 = (bf16[1024,768]{1,0:T(8,128)(2,1)}, s32[8,1024]{1,0:T(8,128)}) custom-call(bf16[1024,768]{1,0:T(8,128)(2,1)} %emb_ref.3, s32[1,1024]{1,0:T(1,128)} %bitcast.17), custom_call_target="tpu_custom_call" | custom-call | flops 1610612736 | bytes 3145728 | tf_op jit(solution)/shard_map/prep/pallas_call | solution.py:138
  5.4 0.0 copy-start.1
  5.5 0.0 copy-start.6
  5.5 0.0 copy-start.7
  5.5 0.0 copy-start.9
  5.5 12.0 %all-to-all-start = ((bf16[32,32,768]{2,1,0:T(8,128)(2,1)}), bf16[32,32,768]{2,1,0:T(8,128)(2,1)S(1)}, u32[]{:S(2)}, u32[]{:S(2)}) async-start(bf16[32,32,768]{2,1,0:T(8,128)(2,1)} %bitcast.20), calls=%async_computation | async-start | bytes 3145728 | tf_op jit(solution)/shard_map/all_to_all | solution.py:56
  17.5 0.0 copy-done.1
  17.5 0.0 copy-done.6
  17.5 0.0 copy-done.7
  17.5 0.0 copy-done.9
  17.5 3.4 %hand.1 = (bf16[1024,896]{1,0:T(8,128)(2,1)S(1)}, bf16[1024,128]{1,0:T(8,128)(2,1)S(1)}) custom-call(bf16[1024,768]{1,0:T(8,128)(2,1)S(1)} %copy-done.1, s32[8,1024]{1,0:T(8,128)S(1)} %copy-done.9, s32[1,1024]{1,0:T(1,128)S(1)} %bitcast.18, s32[1,1024]{1,0:T(1,128)S(1)} %bitcast.19), custom_call_target="tpu_custom_call" | custom-call | flops 1879048192 | bytes 3145728 | tf_op jit(solution)/shard_map/hand/pallas_call | solution.py:174
  20.9 1.2 collective-permute-start
  22.1 3.4 %collective-permute-done.box_ref = bf16[1024,896]{1,0:T(8,128)(2,1)S(1)} collective-permute-done((bf16[1024,896]{1,0:T(8,128)(2,1)S(1)}, bf16[1024,896]{1,0:T(8,128)(2,1)S(1)}, u32[]{:S(2)}, u32[]{:S(2)}) %collective-permute-start) | collective-permute-done | bytes 1835040 | tf_op jit(solution)/shard_map/ppermute | solution.py:60
  25.6 0.2 stamp.1
  25.7 0.0 copy-start
  25.7 1.2 copy-done
  27.0 27.9 %all-to-all-done = bf16[32,32,768]{2,1,0:T(8,128)(2,1)S(1)} async-done(((bf16[32,32,768]{2,1,0:T(8,128)(2,1)}), bf16[32,32,768]{2,1,0:T(8,128)(2,1)S(1)}, u32[]{:S(2)}, u32[]{:S(2)}) %all-to-all-start) | async-done | bytes 1572896 | tf_op jit(solution)/shard_map/all_to_all | solution.py:56
  54.8 7.1 %all-to-all-start.1 = ((bf16[32,32,896]{2,1,0:T(8,128)(2,1)}), bf16[32,32,896]{2,1,0:T(8,128)(2,1)S(1)}, u32[]{:S(2)}, u32[]{:S(2)}) async-start(bf16[32,32,896]{2,1,0:T(8,128)(2,1)} %bitcast.12), calls=%async_computation.1 | async-start | bytes 3670016 | tf_op jit(solution)/shard_map/all_to_all | solution.py:56
  62.0 0.0 copy-start.12
  62.0 0.0 copy-start.13
  62.0 0.0 copy-start.10
  62.0 0.0 copy-start.11
  62.0 0.0 copy-start.8
  62.0 0.6 settle.1
  62.7 1.4 collective-permute-start.1
  64.0 0.0 copy-start.2
  64.0 0.9 copy-done.2
  65.0 0.0 copy-start.3
  65.0 1.5 collective-permute-start.2
  66.4 0.0 copy-start.4
  66.4 0.9 copy-done.4
  67.3 10.6 %collective-permute-done.1.refs_5_ = bf16[512,768]{1,0:T(8,128)(2,1)} collective-permute-done((bf16[512,768]{1,0:T(8,128)(2,1)S(1)}, bf16[512,768]{1,0:T(8,128)(2,1)}, u32[]{:S(2)}, u32[]{:S(2)}) %collective-permute-start.1) | collective-permute-done | bytes 786464 | tf_op jit(solution)/shard_map/ppermute | solution.py:60
  78.0 1.0 collective-permute-start.3
  79.0 0.0 collective-permute-done.2.refs_6_
  79.0 2.2 %collective-permute-start.4 = (bf16[512,768]{1,0:T(8,128)(2,1)}, bf16[512,768]{1,0:T(8,128)(2,1)}, u32[]{:S(2)}, u32[]{:S(2)}) collective-permute-start(bf16[512,768]{1,0:T(8,128)(2,1)} %collective-permute-done.2.refs_6_), channel_id=1, source_target_pairs={{0,3},{4,196},{1,0},{5,197},{2,1},{6,198},{3,2},{7,199},{8,11},{12... | collective-permute-start | bytes 2359304 | tf_op jit(solution)/shard_map/ppermute | solution.py:60
  81.2 12.5 %collective-permute-done.3.refs_9_ = bf16[512,768]{1,0:T(8,128)(2,1)} collective-permute-done((bf16[512,768]{1,0:T(8,128)(2,1)}, bf16[512,768]{1,0:T(8,128)(2,1)}, u32[]{:S(2)}, u32[]{:S(2)}) %collective-permute-start.3) | collective-permute-done | bytes 786464 | tf_op jit(solution)/shard_map/ppermute | solution.py:60
  93.7 0.0 collective-permute-done.4.refs_10_
  93.7 11.7 %all-to-all-done.1 = bf16[32,32,896]{2,1,0:T(8,128)(2,1)S(1)} async-done(((bf16[32,32,896]{2,1,0:T(8,128)(2,1)}), bf16[32,32,896]{2,1,0:T(8,128)(2,1)S(1)}, u32[]{:S(2)}, u32[]{:S(2)}) %all-to-all-start.1) | async-done | bytes 1835040 | tf_op jit(solution)/shard_map/all_to_all | solution.py:56
  105.3 0.2 split.1
  105.5 0.9 collective-permute-start.5
  106.5 1.8 %collective-permute-start.6 = (bf16[528,768]{1,0:T(8,128)(2,1)S(1)}, bf16[528,768]{1,0:T(8,128)(2,1)S(1)}, u32[]{:S(2)}, u32[]{:S(2)}) collective-permute-start(bf16[528,768]{1,0:T(8,128)(2,1)S(1)} %get-tuple-element.36.refs_4_.refs_2_), channel_id=1, source_target_pairs={{0,3},{4,196},{1,0},{5,197},{2,1},{6,198},{3,2},{7,199},{8,11},{12... | collective-permute-start | bytes 2433032 | tf_op jit(solution)/shard_map/ppermute | solution.py:60
  108.2 0.0 copy-done.12
  108.2 0.0 copy-done.13
  108.2 0.0 copy-done.10
  108.2 0.0 copy-done.11
  108.3 1.6 collective-permute-start.9
  109.9 0.0 copy-done.8
  109.9 0.0 copy-done.3
  109.9 0.0 copy-done.5
  109.9 7.6 %own.1.refs_8_ = f32[64,128]{1,0:T(8,128)S(1)} custom-call(s32[30]{0:T(128)S(1)} %copy-done.8, bf16[512,768]{1,0:T(8,128)(2,1)S(1)} %copy-done.3, bf16[512,768]{1,0:T(8,128)(2,1)S(1)} %copy-done.5, bf16[528,768]{1,0:T(8,128)(2,1)S(1)} %get-tuple-element.35.refs_3_.refs_1_, bf16[528,768]{1,0:T(8,128)(2,1)S(1)} %get-tuple-element.36.refs_4_.refs_2_, ...), custom_call_target="tpu_custom_call" | custom-call | flops 4026531840 | bytes 3145728 | tf_op jit(solution)/shard_map/own/pallas_call | solution.py:452
  117.5 0.7 collective-permute-done.5.refs_7_.refs_3_
  118.2 0.0 collective-permute-done.6.refs_8_
  118.2 3.4 %collective-permute-start.8 = (bf16[528,768]{1,0:T(8,128)(2,1)S(1)}, bf16[528,768]{1,0:T(8,128)(2,1)S(1)}, u32[]{:S(2)}, u32[]{:S(2)}) collective-permute-start(bf16[528,768]{1,0:T(8,128)(2,1)S(1)} %collective-permute-done.6.refs_8_), channel_id=1, source_target_pairs={{0,3},{4,196},{1,0},{5,197},{2,1},{6,198},{3,2},{7,199},{8,11},{12... | collective-permute-start | bytes 2433032 | tf_op jit(solution)/shard_map/ppermute | solution.py:60
  121.5 0.0 collective-permute-start.7
  121.5 0.0 collective-permute-done.9.refs_12_.refs_7_
  121.5 16.5 %near.1.refs_9_ = f32[64,128]{1,0:T(8,128)S(1)} custom-call(s32[66]{0:T(128)S(1)} %broadcast_select_fusion.refs_0_, bf16[512,768]{1,0:T(8,128)(2,1)S(1)} %copy-done.3, bf16[512,768]{1,0:T(8,128)(2,1)S(1)} %copy-done.5, bf16[528,768]{1,0:T(8,128)(2,1)S(1)} %get-tuple-element.35.refs_3_.refs_1_, bf16[528,768]{1,0:T(8,128)(2,1)S(1)} %get-tuple-element.36.refs_4_.refs_2_, ...), custom_call_target="tpu_custom_call" | custom-call | flops 8858370048 | bytes 7864320 | tf_op jit(solution)/shard_map/near/pallas_call | solution.py:452
  138.0 0.0 collective-permute-done.8.refs_5_
  138.0 0.0 collective-permute-done.7.refs_4_
  138.1 3.5 %far.1 = f32[128,128]{1,0:T(8,128)S(1)} custom-call(s32[6]{0:T(128)S(1)} %broadcast_select_fusion.1.refs_0_, bf16[528,768]{1,0:T(8,128)(2,1)S(1)} %get-tuple-element.35.refs_3_.refs_1_, bf16[528,768]{1,0:T(8,128)(2,1)S(1)} %get-tuple-element.36.refs_4_.refs_2_, bf16[528,768]{1,0:T(8,128)(2,1)S(1)} %collective-permute-done.5.refs_7_.refs_3_, ...), custom_call_target="tpu_custom_call" | custom-call | flops 805306368 | bytes 3932160 | tf_op jit(solution)/shard_map/far/pallas_call | solution.py:452
  141.5 21.2 %all_to_all.15 = f32[128,1,128]{2,1,0:T(1,128)S(1)} all-to-all(f32[128,1,128]{2,1,0:T(1,128)S(1)} %bitcast.14), channel_id=1, replica_groups={{0,1,2,3,8,9,10,11,16,17,18,19,24,25,26,27,32,33,34,35,40,41,42,43,48,4..., dimensions={0} | all-to-all | bytes 131072 | tf_op jit(solution)/shard_map/all_to_all | solution.py:56
  162.7 4.7 %collective-permute-start.10 = (f32[128,128]{1,0:T(8,128)S(1)}, f32[128,128]{1,0:T(8,128)S(1)}, u32[]{:S(2)}, u32[]{:S(2)}) collective-permute-start(f32[128,128]{1,0:T(8,128)S(1)} %bitcast.15), channel_id=1, source_target_pairs={{0,4},{1,5},{2,6},{3,7},{4,0},{5,1},{6,2},{7,3},{8,12},{9,13},{10,... | collective-permute-start | bytes 196616 | tf_op jit(solution)/shard_map/ppermute | solution.py:60
  167.4 0.8 answer.2.refs_0_
  168.2 0.1 collective-permute-done.10.values_ref
  168.3 1.4 answer.3
  (3 shorter events, 0.0 us)
Async XLA Ops:
  5.4 12.1 %copy-start.1 = (bf16[1024,768]{1,0:T(8,128)(2,1)S(1)}, bf16[1024,768]{1,0:T(8,128)(2,1)}, u32[]{:S(2)}) copy-start(bf16[1024,768]{1,0:T(8,128)(2,1)} %emb_ref.3) | copy-start | bytes 4718596
  5.5 12.1 %copy-start.6 = (s32[1024]{0:T(1024)S(1)}, s32[1024]{0:T(1024)}, u32[]{:S(2)}) copy-start(s32[1024]{0:T(1024)} %param.9) | copy-start | bytes 12292
  5.5 12.1 %copy-start.7 = (s32[1024]{0:T(1024)S(1)}, s32[1024]{0:T(1024)}, u32[]{:S(2)}) copy-start(s32[1024]{0:T(1024)} %param.10) | copy-start | bytes 12292
  5.5 12.1 %copy-start.9 = (s32[8,1024]{1,0:T(8,128)S(1)}, s32[8,1024]{1,0:T(8,128)}, u32[]{:S(2)}) copy-start(s32[8,1024]{1,0:T(8,128)} %get-tuple-element.26.info_ref) | copy-start | bytes 98308
  5.5 49.4 %all-to-all-start = ((bf16[32,32,768]{2,1,0:T(8,128)(2,1)}), bf16[32,32,768]{2,1,0:T(8,128)(2,1)S(1)}, u32[]{:S(2)}, u32[]{:S(2)}) async-start(bf16[32,32,768]{2,1,0:T(8,128)(2,1)} %bitcast.20), calls=%async_computation | async-start | bytes 3145728 | tf_op jit(solution)/shard_map/all_to_all | solution.py:56
  20.9 4.6 %collective-permute-start = (bf16[1024,896]{1,0:T(8,128)(2,1)S(1)}, bf16[1024,896]{1,0:T(8,128)(2,1)S(1)}, u32[]{:S(2)}, u32[]{:S(2)}) collective-permute-start(bf16[1024,896]{1,0:T(8,128)(2,1)S(1)} %get-tuple-element.28), channel_id=1, source_target_pairs={{0,4},{1,5},{2,6},{3,7},{4,0},{5,1},{6,2},{7,3},{8,12},{9,13},{10,... | collective-permute-start | bytes 5505032 | tf_op jit(solution)/shard_map/ppermute | solution.py:60
  25.7 1.3 copy-start
  54.8 50.5 %all-to-all-start.1 = ((bf16[32,32,896]{2,1,0:T(8,128)(2,1)}), bf16[32,32,896]{2,1,0:T(8,128)(2,1)S(1)}, u32[]{:S(2)}, u32[]{:S(2)}) async-start(bf16[32,32,896]{2,1,0:T(8,128)(2,1)} %bitcast.12), calls=%async_computation.1 | async-start | bytes 3670016 | tf_op jit(solution)/shard_map/all_to_all | solution.py:56
  62.0 46.3 %copy-start.12 = (s32[66]{0:T(128)S(1)}, s32[66]{0:T(128)}, u32[]{:S(2)}) copy-start(s32[66]{0:T(128)} %constant.29.clone) | copy-start | bytes 796
  62.0 46.3 %copy-start.13 = (s32[66]{0:T(128)S(1)}, s32[66]{0:T(128)}, u32[]{:S(2)}) copy-start(s32[66]{0:T(128)} %constant.28.clone) | copy-start | bytes 796
  62.0 46.3 %copy-start.10 = (s32[6]{0:T(128)S(1)}, s32[6]{0:T(128)}, u32[]{:S(2)}) copy-start(s32[6]{0:T(128)} %constant.31.clone) | copy-start | bytes 76
  62.0 46.3 %copy-start.11 = (s32[6]{0:T(128)S(1)}, s32[6]{0:T(128)}, u32[]{:S(2)}) copy-start(s32[6]{0:T(128)} %constant.30.clone) | copy-start | bytes 76
  62.0 47.9 %copy-start.8 = (s32[30]{0:T(128)S(1)}, s32[30]{0:T(128)}, u32[]{:S(2)}) copy-start(s32[30]{0:T(128)} %constant.27.clone.refs_0_) | copy-start | bytes 364
  62.7 15.3 %collective-permute-start.1 = (bf16[512,768]{1,0:T(8,128)(2,1)S(1)}, bf16[512,768]{1,0:T(8,128)(2,1)}, u32[]{:S(2)}, u32[]{:S(2)}) collective-permute-start(bf16[512,768]{1,0:T(8,128)(2,1)S(1)} %get-tuple-element.37.refs_1_), channel_id=1, source_target_pairs={{0,1},{4,68},{1,2},{5,69},{2,3},{6,70},{3,0},{7,71},{8,9},{12,76},... | collective-permute-start | bytes 2359304 | tf_op jit(solution)/shard_map/ppermute | solution.py:60
  64.0 0.9 copy-start.2
  65.0 44.9 %copy-start.3 = (bf16[512,768]{1,0:T(8,128)(2,1)S(1)}, bf16[512,768]{1,0:T(8,128)(2,1)}, u32[]{:S(2)}) copy-start(bf16[512,768]{1,0:T(8,128)(2,1)} %copy-done.2) | copy-start | bytes 2359300
  65.0 14.0 %collective-permute-start.2 = (bf16[512,768]{1,0:T(8,128)(2,1)S(1)}, bf16[512,768]{1,0:T(8,128)(2,1)}, u32[]{:S(2)}, u32[]{:S(2)}) collective-permute-start(bf16[512,768]{1,0:T(8,128)(2,1)S(1)} %get-tuple-element.38.refs_2_), channel_id=1, source_target_pairs={{0,3},{4,196},{1,0},{5,197},{2,1},{6,198},{3,2},{7,199},{8,11},{12... | collective-permute-start | bytes 2359304 | tf_op jit(solution)/shard_map/ppermute | solution.py:60
  66.4 0.9 copy-start.4
  78.0 31.9 %copy-start.5 = (bf16[512,768]{1,0:T(8,128)(2,1)S(1)}, bf16[512,768]{1,0:T(8,128)(2,1)}, u32[]{:S(2)}) copy-start(bf16[512,768]{1,0:T(8,128)(2,1)} %copy-done.4) | copy-start | bytes 2359300
  78.0 15.7 %collective-permute-start.3 = (bf16[512,768]{1,0:T(8,128)(2,1)}, bf16[512,768]{1,0:T(8,128)(2,1)}, u32[]{:S(2)}, u32[]{:S(2)}) collective-permute-start(bf16[512,768]{1,0:T(8,128)(2,1)} %collective-permute-done.1.refs_5_), channel_id=1, source_target_pairs={{0,1},{4,68},{1,2},{5,69},{2,3},{6,70},{3,0},{7,71},{8,9},{12,76},... | collective-permute-start | bytes 2359304 | tf_op jit(solution)/shard_map/ppermute | solution.py:60
  79.0 14.7 %collective-permute-start.4 = (bf16[512,768]{1,0:T(8,128)(2,1)}, bf16[512,768]{1,0:T(8,128)(2,1)}, u32[]{:S(2)}, u32[]{:S(2)}) collective-permute-start(bf16[512,768]{1,0:T(8,128)(2,1)} %collective-permute-done.2.refs_6_), channel_id=1, source_target_pairs={{0,3},{4,196},{1,0},{5,197},{2,1},{6,198},{3,2},{7,199},{8,11},{12... | collective-permute-start | bytes 2359304 | tf_op jit(solution)/shard_map/ppermute | solution.py:60
  105.5 12.6 %collective-permute-start.5 = (bf16[528,768]{1,0:T(8,128)(2,1)S(1)}, bf16[528,768]{1,0:T(8,128)(2,1)S(1)}, u32[]{:S(2)}, u32[]{:S(2)}) collective-permute-start(bf16[528,768]{1,0:T(8,128)(2,1)S(1)} %get-tuple-element.35.refs_3_.refs_1_), channel_id=1, source_target_pairs={{0,1},{4,68},{1,2},{5,69},{2,3},{6,70},{3,0},{7,71},{8,9},{12,76},... | collective-permute-start | bytes 2433032 | tf_op jit(solution)/shard_map/ppermute | solution.py:60
  106.5 11.7 %collective-permute-start.6 = (bf16[528,768]{1,0:T(8,128)(2,1)S(1)}, bf16[528,768]{1,0:T(8,128)(2,1)S(1)}, u32[]{:S(2)}, u32[]{:S(2)}) collective-permute-start(bf16[528,768]{1,0:T(8,128)(2,1)S(1)} %get-tuple-element.36.refs_4_.refs_2_), channel_id=1, source_target_pairs={{0,3},{4,196},{1,0},{5,197},{2,1},{6,198},{3,2},{7,199},{8,11},{12... | collective-permute-start | bytes 2433032 | tf_op jit(solution)/shard_map/ppermute | solution.py:60
  108.3 13.3 %collective-permute-start.9 = (f32[16,1024]{1,0:T(8,128)S(1)}, f32[16,1024]{1,0:T(8,128)S(1)}, u32[]{:S(2)}, u32[]{:S(2)}) collective-permute-start(f32[16,1024]{1,0:T(8,128)S(1)} %get-tuple-element.39.refs_5_.refs_11_.refs_6_), channel_id=1, source_target_pairs={{0,2},{4,132},{1,3},{5,133},{2,0},{6,134},{3,1},{7,135},{8,10},{12... | collective-permute-start | bytes 196616 | tf_op jit(solution)/shard_map/ppermute | solution.py:60
  118.2 19.9 %collective-permute-start.8 = (bf16[528,768]{1,0:T(8,128)(2,1)S(1)}, bf16[528,768]{1,0:T(8,128)(2,1)S(1)}, u32[]{:S(2)}, u32[]{:S(2)}) collective-permute-start(bf16[528,768]{1,0:T(8,128)(2,1)S(1)} %collective-permute-done.6.refs_8_), channel_id=1, source_target_pairs={{0,3},{4,196},{1,0},{5,197},{2,1},{6,198},{3,2},{7,199},{8,11},{12... | collective-permute-start | bytes 2433032 | tf_op jit(solution)/shard_map/ppermute | solution.py:60
  121.5 16.5 %collective-permute-start.7 = (bf16[528,768]{1,0:T(8,128)(2,1)S(1)}, bf16[528,768]{1,0:T(8,128)(2,1)S(1)}, u32[]{:S(2)}, u32[]{:S(2)}) collective-permute-start(bf16[528,768]{1,0:T(8,128)(2,1)S(1)} %collective-permute-done.5.refs_7_.refs_3_), channel_id=1, source_target_pairs={{0,1},{4,68},{1,2},{5,69},{2,3},{6,70},{3,0},{7,71},{8,9},{12,76},... | collective-permute-start | bytes 2433032 | tf_op jit(solution)/shard_map/ppermute | solution.py:60
  162.7 5.6 %collective-permute-start.10 = (f32[128,128]{1,0:T(8,128)S(1)}, f32[128,128]{1,0:T(8,128)S(1)}, u32[]{:S(2)}, u32[]{:S(2)}) collective-permute-start(f32[128,128]{1,0:T(8,128)S(1)} %bitcast.15), channel_id=1, source_target_pairs={{0,4},{1,5},{2,6},{3,7},{4,0},{5,1},{6,2},{7,3},{8,12},{9,13},{10,... | collective-permute-start | bytes 196616 | tf_op jit(solution)/shard_map/ppermute | solution.py:60

commit v6 on v5

v6 whole, which is shorter than its diff:
```python
import functools

import jax
import jax.numpy as jnp
import numpy as np
from jax import lax
from jax.experimental import pallas as pl
from jax.experimental.pallas import tpu as pltpu
from jax.sharding import PartitionSpec as P

AXES = ("dp", "rep")
NX, NY, NZ = 4, 4, 8
CHIPS = NX * NY * NZ
GROUPS = 64
HALF = GROUPS // 2
SOURCES = 32
CAP = 32
ROWS = 1024
D = 768
EXTRA = 16
COLUMNS = D // 128
CELL = COLUMNS * 32 + 8
HALF_ROWS = 512
ORDERS = 4096
VMEM = 24 * 1024 * 1024
FULL = 56 * 1024 * 1024


def device(x, y, z, core):
    return ((y * NZ + z) * 2 + core) * NX + x


ROUTES = [[device(x, y, z, 0) for y in range(NY) for z in range(NZ)] for x in range(NX)] + [
    [device(x, y, z, 1) for x in range(NX) for z in range(NZ)] for y in range(NY)
]
RETURNS = [
    [device(x, y, z, 0) for x in range(NX) for y in range(NY) for z in range(NZ)],
    [device(x, y, z, 1) for y in range(NY) for x in range(NX) for z in range(NZ)],
]


def ring(step):
    pairs = []
    for y in range(NY):
        for z in range(NZ):
            for x in range(NX):
                pairs.append((device(x, y, z, 0), device((x + step) % NX, y, z, 0)))
                pairs.append((device(x, y, z, 1), device(x, (y + step) % NY, z, 1)))
    return pairs


SIBLING = [(dp * NX + x, (dp ^ 1) * NX + x) for dp in range(NY * NZ * 2) for x in range(NX)]


def exchange(rows, groups):
    return lax.all_to_all(rows, AXES, split_axis=0, concat_axis=0, tiled=True, axis_index_groups=groups)


def send(rows, pairs):
    return lax.ppermute(rows, AXES, pairs)


def cost(flops, size):
    return pl.CostEstimate(flops=flops, bytes_accessed=size, transcendentals=0)


def across(one, other):
    return lax.dot_general(one, other, (((1,), (1,)), ((), ())), preferred_element_type=jnp.float32)


def key_tables(info, ids, order, core, mine):
    group, rank = info[0:1], info[1:2]
    key = (ids & 1) * ORDERS + order
    serving = group >> 5
    here = jnp.where((serving == core) if mine else (serving != core), group & (HALF - 1), -1)
    here = lax.broadcasted_iota(jnp.int32, (SOURCES, ROWS), 0) == here
    lanes = lax.broadcasted_iota(jnp.int32, (128, ROWS), 0) == rank
    lanes = jnp.where(lanes, 1.0, 0.0).astype(jnp.bfloat16)
    parts = ((key >> 7) + 1).astype(jnp.float32), (key & 127).astype(jnp.float32)
    return [across(jnp.where(here, part, 0.0).astype(jnp.bfloat16), lanes) for part in parts]


def fill_cells(out, first, count, rows, high, low):
    for column in range(COLUMNS):
        out[first : first + count, column * CAP : (column + 1) * CAP, :] = (
            rows[:, column * 128 : (column + 1) * 128].reshape(count, CAP, 128).astype(jnp.bfloat16)
        )
    sub = lax.broadcasted_iota(jnp.int32, (count, 8, 128), 1)
    high, low = high[first : first + count][:, None, :], low[first : first + count][:, None, :]
    tile = jnp.where(sub == 0, high, jnp.where(sub == 1, low, 0.0))
    out[first : first + count, COLUMNS * CAP :, :] = tile.astype(jnp.bfloat16)


def where_am_i():
    dp = lax.axis_index("dp")
    return lax.axis_index("rep"), dp >> 4, (dp >> 1) & (NZ - 1), dp & 1


def slots_of(info, core, mine):
    group, rank = info[0:1], info[1:2]
    serving = group >> 5
    slot = (group & (HALF - 1)) * CAP + rank
    return jnp.where((serving == core) if mine else (serving != core), slot, -1)


def onehot(slot, first, count):
    rows = lax.broadcasted_iota(jnp.int32, (count, ROWS), 0) + first
    return jnp.where(rows == slot, 1.0, 0.0).astype(jnp.bfloat16)


def normalize(rows):
    wide = rows.astype(jnp.float32)
    scale = 1.0 / jnp.sqrt(jnp.sum(wide * wide, axis=1, keepdims=True) + 1e-06)
    return (wide * scale).astype(jnp.bfloat16)


PIECE = 512
PIECES = ROWS // PIECE
SPAN = 256


def prep_kernel(emb_ref, ids_ref, order_ref, box_ref, info_ref, rows, out, in_sem, out_sems):
    load = pltpu.make_async_copy(emb_ref, rows, in_sem)
    load.start()
    group = ids_ref[...] >> 1
    member = lax.broadcasted_iota(jnp.int32, (GROUPS, ROWS), 0) == group
    hot = jnp.where(member, 1.0, 0.0)
    earlier = jnp.where(
        lax.broadcasted_iota(jnp.int32, (SPAN, SPAN), 0) < lax.broadcasted_iota(jnp.int32, (SPAN, SPAN), 1), 1.0, 0.0
    ).astype(jnp.bfloat16)
    before = jnp.zeros((GROUPS, 1), jnp.float32)
    ranks = []
    for n in range(ROWS // SPAN):
        here = hot[:, n * SPAN : (n + 1) * SPAN]
        count = jnp.dot(here.astype(jnp.bfloat16), earlier, preferred_element_type=jnp.float32) + before
        ranks.append(jnp.sum(here * count, axis=0, keepdims=True))
        before = before + jnp.sum(here, axis=1, keepdims=True)
    rank = jnp.concatenate(ranks, axis=1).astype(jnp.int32)
    which = lax.broadcasted_iota(jnp.int32, (8, ROWS), 0)
    info = jnp.where(which == 0, group, jnp.where(which == 1, rank, 0))
    info_ref[...] = info
    core = where_am_i()[3]
    slot = slots_of(info, core, True)
    high, low = key_tables(info, ids_ref[...], order_ref[...], core, True)
    load.wait()
    stores = []
    for n in range(PIECES):
        count = PIECE // CAP
        pick = onehot(slot, n * PIECE, PIECE)
        found = jnp.dot(pick, rows[...], preferred_element_type=jnp.float32)
        fill_cells(out, n * count, count, found, high, low)
        cells = pl.ds(n * count, count)
        stores.append(pltpu.make_async_copy(out.at[cells], box_ref.at[cells], out_sems.at[n]))
        stores[-1].start()
    for store in stores:
        store.wait()


def prep(embeddings, ids, order):
    return pl.pallas_call(
        prep_kernel,
        out_shape=(
            jax.ShapeDtypeStruct((SOURCES, CELL, 128), jnp.bfloat16),
            jax.ShapeDtypeStruct((8, ROWS), jnp.int32),
        ),
        in_specs=[pl.BlockSpec(memory_space=pl.ANY)] + [pl.BlockSpec(memory_space=pltpu.VMEM)] * 2,
        out_specs=(pl.BlockSpec(memory_space=pl.ANY), pl.BlockSpec(memory_space=pltpu.VMEM)),
        scratch_shapes=[
            pltpu.VMEM((ROWS, D), jnp.bfloat16),
            pltpu.VMEM((SOURCES, CELL, 128), jnp.bfloat16),
            pltpu.SemaphoreType.DMA,
            pltpu.SemaphoreType.DMA((PIECES,)),
        ],
        compiler_params=pltpu.CompilerParams(vmem_limit_bytes=FULL),
        cost_estimate=cost(2 * ROWS * ROWS * D, 4 * ROWS * D),
        name="prep",
    )(embeddings, ids, order)


def hand_kernel(emb_ref, info_ref, ids_ref, order_ref, box_ref):
    info, core = info_ref[...], where_am_i()[3]
    pick = onehot(slots_of(info, core, False), 0, ROWS)
    found = jnp.dot(pick, normalize(emb_ref[...]), preferred_element_type=jnp.float32)
    high, low = key_tables(info, ids_ref[...], order_ref[...], core, False)
    fill_cells(box_ref, 0, SOURCES, found, high, low)


def hand(embeddings, info, ids, order):
    return pl.pallas_call(
        hand_kernel,
        out_shape=jax.ShapeDtypeStruct((SOURCES, CELL, 128), jnp.bfloat16),
        in_specs=[pl.BlockSpec(memory_space=pltpu.VMEM)] * 4,
        out_specs=pl.BlockSpec(memory_space=pltpu.VMEM),
        compiler_params=pltpu.CompilerParams(vmem_limit_bytes=VMEM),
        cost_estimate=cost(2 * ROWS * ROWS * D, 4 * ROWS * D),
        name="hand",
    )(embeddings, info, ids, order)


def open_kernel(raw, cells_ref, p_ref, m_ref):
    count = SOURCES // 2
    sub = lax.broadcasted_iota(jnp.int32, (count, 8, 128), 1)
    slot = lax.broadcasted_iota(jnp.int32, (count, CAP, 128), 1) == lax.broadcasted_iota(
        jnp.int32, (count, CAP, 128), 2
    )
    row = lax.broadcasted_iota(jnp.int32, (EXTRA, 128), 0)
    for number, out_ref in enumerate((p_ref, m_ref)):
        first = number * count
        columns = [
            cells_ref[first : first + count, column * CAP : (column + 1) * CAP, :].reshape(HALF_ROWS, 128)
            for column in range(COLUMNS)
        ]
        if raw:
            wide = [column.astype(jnp.float32) for column in columns]
            total = sum(column * column for column in wide)
            scale = 1.0 / jnp.sqrt(jnp.sum(total, axis=1, keepdims=True) + 1e-06)
            columns = [(column * scale).astype(jnp.bfloat16) for column in wide]
        for column in range(COLUMNS):
            out_ref[:HALF_ROWS, column * 128 : (column + 1) * 128] = columns[column]
        tile = cells_ref[first : first + count, COLUMNS * CAP :, :].astype(jnp.float32)
        keys = jnp.zeros((EXTRA, HALF_ROWS), jnp.float32)
        for part in range(2):
            its = jnp.sum(jnp.where(sub == part, tile, 0.0), axis=1)
            its = jnp.where(slot, its[:, None, :], 0.0).reshape(HALF_ROWS, 128).astype(jnp.bfloat16)
            keys += across(jnp.where(row == part, 1.0, 0.0).astype(jnp.bfloat16), its)
        out_ref[HALF_ROWS:] = jnp.concatenate(
            [keys, jnp.zeros((EXTRA, D - HALF_ROWS), jnp.float32)], axis=1
        ).astype(jnp.bfloat16)


def open_cells(cells, raw):
    return pl.pallas_call(
        functools.partial(open_kernel, raw),
        out_shape=tuple([jax.ShapeDtypeStruct((HALF_ROWS + EXTRA, D), jnp.bfloat16)] * 2),
        in_specs=[pl.BlockSpec(memory_space=pltpu.VMEM)],
        out_specs=tuple([pl.BlockSpec(memory_space=pltpu.VMEM)] * 2),
        compiler_params=pltpu.CompilerParams(vmem_limit_bytes=VMEM),
        cost_estimate=cost(0, 4 * ROWS * D),
        name="settle" if raw else "split",
    )(cells)


BLOCKS = [(part, far, chunk) for far in range(3) for chunk in range(2) for part in "PM"]


def pair_lists():
    pairs = []

    def all_chunks(one, other):
        for c in range(2):
            for e in range(2):
                pairs.append((one + (c,), other + (e,)))

    for part in "PM":
        pairs.append(((part, 0, 0), (part, 0, 1)))
        all_chunks((part, 0), (part, 1))
        pairs.append(((part, 0, 1), (part, 2, 0)))
    all_chunks(("P", 0), ("M", 0))
    all_chunks(("P", 0), ("M", 1))
    all_chunks(("P", 1), ("M", 1))
    pairs.append((("P", 1, 0), ("M", 2, 0)))
    pairs.append((("P", 1, 1), ("M", 2, 0)))
    pairs.append((("P", 2, 0), ("M", 1, 1)))
    pairs.append((("P", 1, 1), ("M", 2, 1)))
    by_place = [
        ((("P", 0, 0), ("P", 2, 0)), (("M", 0, 0), ("M", 2, 0))),
        ((("M", 0, 1), ("M", 2, 1)), (("P", 0, 1), ("P", 2, 1))),
    ]
    return pairs, by_place


def stage_of(pair):
    if all(chunk == 0 and far < 2 for part, far, chunk in pair):
        return 0
    return 1 + max([far for part, far, chunk in pair if chunk == 1] + [0])


def three_parts(values):
    parts = []
    for piece in range(3):
        parts.append(values.astype(jnp.bfloat16))
        values = values - parts[-1].astype(jnp.float32)
    return parts


def similar_kernel(blocks, n_tasks, n_before, *refs):
    n_blocks = len(blocks)
    tasks_ref, refs = refs[0], refs[1:]
    arrays, refs = refs[:n_blocks], refs[n_blocks:]
    befores, refs = refs[:n_before], refs[n_before:]
    out_ref, rows, kcol, ccol, krow, crow, best_row, best_col, s0, s1, sems = refs

    copies = [pltpu.make_async_copy(array, rows.at[slot], sems.at[slot]) for slot, array in enumerate(arrays)]
    for copy in copies:
        copy.start()
    for slot in range(n_blocks):
        best_row[slot] = jnp.full((HALF_ROWS, 128), -1.0, jnp.float32)
        best_col[slot] = jnp.full((8, HALF_ROWS), -1.0, jnp.float32)

    def cluster(key):
        return jnp.where(key >= ORDERS + 128, 2.0, jnp.where(key > 0, 1.0, 0.0))

    for slot, copy in enumerate(copies):
        copy.wait()
        parts = rows[slot, HALF_ROWS:, :HALF_ROWS].astype(jnp.float32)
        key = 128.0 * parts[0:1] + parts[1:2]
        krow[slot] = jnp.broadcast_to(key, (8, HALF_ROWS))
        crow[slot] = cluster(krow[slot])
        key = jnp.transpose(jnp.broadcast_to(key, (128, HALF_ROWS)))
        kcol[slot] = key
        ccol[slot] = cluster(key)

    def multiply(task, s):
        a, b = tasks_ref[3 * task], tasks_ref[3 * task + 1]
        s[...] = across(rows[a, :HALF_ROWS], rows[b, :HALF_ROWS])

    step = 16

    def reduce(task, s):
        a, b, sink = tasks_ref[3 * task], tasks_ref[3 * task + 1], tasks_ref[3 * task + 2]
        kb, cb = krow[b], crow[b]
        for row in range(0, HALF_ROWS, step):
            ka = kcol[a, row : row + step].reshape(step // 8, 8, 128)
            ca = ccol[a, row : row + step].reshape(step // 8, 8, 128)
            best = best_row[a, row : row + step]
            for at in range(0, HALF_ROWS, 128):
                found = s[row : row + step, at : at + 128].reshape(step // 8, 8, 128)
                same = jnp.where(ca == cb[None, :, at : at + 128], found, -1.0)
                later = kb[None, :, at : at + 128] < ka
                best = jnp.maximum(best, jnp.where(later, same, -1.0).reshape(step, 128))
                other = jnp.max(jnp.where(later, -1.0, same), axis=0)
                best_col[sink, :, at : at + 128] = jnp.maximum(best_col[sink, :, at : at + 128], other)
            best_row[a, row : row + step] = best

    def two(turn, carry):
        multiply(2 * turn + 1, s1)
        reduce(2 * turn, s0)
        multiply(2 * turn + 2, s0)
        reduce(2 * turn + 1, s1)
        return carry

    turns = (n_tasks - 1) // 2
    multiply(0, s0)
    if turns:
        lax.fori_loop(0, turns, two, 0)
    if n_tasks % 2 == 0:
        multiply(n_tasks - 1, s1)
    reduce(2 * turns, s0)
    if n_tasks % 2 == 0:
        reduce(n_tasks - 1, s1)

    empty = jnp.full((CAP, HALF_ROWS), -1.0, jnp.float32)
    diagonal = lax.broadcasted_iota(jnp.int32, (CAP, HALF_ROWS), 0) == (
        lax.broadcasted_iota(jnp.int32, (CAP, HALF_ROWS), 1) & (CAP - 1)
    )
    values = {}
    for number, part in enumerate("PM"):
        for level in range(2):
            tiles = [empty] * 4
            for slot, (its, far, chunk) in enumerate(blocks):
                if its == part and far // 2 == level:
                    by_row = jnp.max(jnp.transpose(best_row[slot]), axis=0, keepdims=True)
                    by_col = jnp.max(best_col[slot], axis=0, keepdims=True)
                    tiles[2 * (far & 1) + chunk] = jnp.where(diagonal, jnp.maximum(by_row, by_col), -1.0)
            if all(tile is empty for tile in tiles):
                value = jnp.full((HALF_ROWS // CAP, 128), -1.0, jnp.float32)
            else:
                value = jnp.transpose(jnp.concatenate(tiles, axis=0)).reshape(HALF_ROWS // CAP, CAP, 128)
                value = jnp.max(value, axis=1)
            at = pl.ds(level * SOURCES + number * (SOURCES // 2), SOURCES // 2)
            for before in befores:
                value = jnp.maximum(value, before[at, :])
            values[level, number] = value
    values = jnp.concatenate([values[level, number] for level in range(2) for number in range(2)], axis=0)
    if not befores:
        out_ref[...] = values
        return
    x, y, z, core = where_am_i()
    here = jnp.where(core == 0, x, y)
    row = lax.broadcasted_iota(jnp.int32, (CHIPS, 2 * SOURCES), 0)
    column = lax.broadcasted_iota(jnp.int32, (CHIPS, 2 * SOURCES), 1)
    source = row & (SOURCES - 1)
    far = (here - (row >> 5)) * jnp.where(source < SOURCES // 2, 1, -1) & 3
    wanted = (column == source) & (far < 2) | (column == source + SOURCES) & (far == 2)
    pick = jnp.where(wanted, 1.0, 0.0).astype(jnp.bfloat16)
    out_ref[...] = jnp.dot(
        jnp.concatenate([pick] * 3, axis=1),
        jnp.concatenate(three_parts(values), axis=0),
        preferred_element_type=jnp.float32,
    )


def similar(hold, low, high, ring_place, befores, name):
    blocks = [block for block in BLOCKS if any(block in pair for pair in low + high)]
    place = {block: number for number, block in enumerate(blocks)}
    spare = n = len(blocks)

    def table(pairs):
        return np.array(
            [(place[a], place[b], spare if a == b else place[b]) for a, b in pairs], np.int32
        ).reshape(-1)

    tasks = jnp.asarray(table(low))
    if low != high:
        tasks = jnp.where(ring_place < 2, tasks, jnp.asarray(table(high)))
    return pl.pallas_call(
        functools.partial(similar_kernel, blocks, len(low), len(befores)),
        out_shape=jax.ShapeDtypeStruct((CHIPS if befores else 2 * SOURCES, 128), jnp.float32),
        in_specs=[pl.BlockSpec(memory_space=pltpu.SMEM)]
        + [pl.BlockSpec(memory_space=pl.ANY)] * n
        + [pl.BlockSpec(memory_space=pltpu.VMEM)] * len(befores),
        out_specs=pl.BlockSpec(memory_space=pltpu.VMEM),
        scratch_shapes=[
            pltpu.VMEM((n, HALF_ROWS + EXTRA, D), jnp.bfloat16),
            pltpu.VMEM((n, HALF_ROWS, 128), jnp.float32),
            pltpu.VMEM((n, HALF_ROWS, 128), jnp.float32),
            pltpu.VMEM((n, 8, HALF_ROWS), jnp.float32),
            pltpu.VMEM((n, 8, HALF_ROWS), jnp.float32),
            pltpu.VMEM((n, HALF_ROWS, 128), jnp.float32),
            pltpu.VMEM((n + 1, 8, HALF_ROWS), jnp.float32),
            pltpu.VMEM((HALF_ROWS, HALF_ROWS), jnp.float32),
            pltpu.VMEM((HALF_ROWS, HALF_ROWS), jnp.float32),
            pltpu.SemaphoreType.DMA((n,)),
        ],
        compiler_params=pltpu.CompilerParams(vmem_limit_bytes=32 * 1024 * 1024),
        cost_estimate=cost(2 * D * HALF_ROWS * HALF_ROWS * len(low), 2 * n * HALF_ROWS * D),
        name=name,
    )(tasks, *[hold[block] for block in blocks], *befores)


def answer_kernel(away, info_ref, values_ref, *refs):
    info, out_ref = info_ref[...], refs[-1]
    group, rank = info[0:1], info[1:2]
    x, y, z, core = where_am_i()
    serving = (core + away) & 1
    here = (group >> 5) == serving
    ring_place, source = jnp.where(serving == 0, x, y), jnp.where(serving == 0, y, x)
    step = jnp.where(source < 2, 1, -1)
    place_of = lax.broadcasted_iota(jnp.int32, (SOURCES, ROWS), 0)
    pick = jnp.where(place_of == jnp.where(here, group & (HALF - 1), -1), 1.0, 0.0).astype(jnp.bfloat16)
    pick = jnp.concatenate([pick] * 3, axis=0)
    lane_of = lax.broadcasted_iota(jnp.int32, (128, ROWS), 0)
    best = refs[0][...] if away else jnp.full((1, ROWS), -1.0, jnp.float32)
    for far in range(3):
        holder = pl.multiple_of(((ring_place + far * step) & 3) * SOURCES, SOURCES)
        parts = jnp.concatenate(three_parts(values_ref[pl.ds(holder, SOURCES), :]), axis=0)
        found = lax.dot_general(parts, pick, (((0,), (0,)), ((), ())), preferred_element_type=jnp.float32)
        wanted = jnp.where(here, (far & 1) * 64 + away * CAP + rank, -1)
        found = jnp.max(jnp.where(lane_of == wanted, found, -1.0), axis=0, keepdims=True)
        best = jnp.maximum(best, found)
    out_ref[...] = best


def answer(away, info, values, *before):
    return pl.pallas_call(
        functools.partial(answer_kernel, away),
        out_shape=jax.ShapeDtypeStruct((1, ROWS), jnp.float32),
        in_specs=[pl.BlockSpec(memory_space=pltpu.VMEM)] * (2 + len(before)),
        out_specs=pl.BlockSpec(memory_space=pltpu.VMEM),
        compiler_params=pltpu.CompilerParams(vmem_limit_bytes=VMEM),
        cost_estimate=cost(2 * 3 * 3 * 128 * 128 * ROWS, 4 * 128 * 128),
        name="answer",
    )(info, values, *before)


def local(embeddings, cluster_ids, member_order):
    x, y, z, core = where_am_i()
    ring_place = jnp.where(core == 0, x, y)
    ids, order = cluster_ids.reshape(1, ROWS), member_order.reshape(1, ROWS)

    box, info = prep(embeddings, ids, order)
    chunk1 = exchange(box, ROUTES)
    handed = send(hand(embeddings, info, ids, order), SIBLING)
    chunk1, handed = lax.optimization_barrier((chunk1, handed))
    chunk2 = exchange(handed, ROUTES)

    hold = {}

    def ring_blocks(far, chunk, blocks):
        hold["P", far, chunk], hold["M", far, chunk] = blocks
        return blocks

    def onward(blocks):
        return send(blocks[0], ring(1)), send(blocks[1], ring(-1))

    pairs, by_place = pair_lists()
    pairs += [((part, 0, chunk),) * 2 for part in "PM" for chunk in range(2)]

    def run(stage, name, befores=()):
        low = [pair for pair in pairs if stage_of(pair) == stage]
        high = list(low)
        for one, other in by_place:
            if stage_of(one) == stage:
                low.append(one)
                high.append(other)
        return similar(hold, low, high, ring_place, befores, name)

    own1 = ring_blocks(0, 0, open_cells(chunk1, True))
    near1 = ring_blocks(1, 0, onward(own1))
    far1 = onward(near1)
    first = run(0, "first")
    chunk2, own1, near1, far1, first = lax.optimization_barrier((chunk2, own1, near1, far1, first))
    for far, blocks in enumerate((own1, near1, far1)):
        ring_blocks(far, 0, blocks)
    own2 = ring_blocks(0, 1, open_cells(chunk2, False))
    near2 = onward(own2)
    own = run(1, "own")
    near2, own = lax.optimization_barrier((near2, own))
    ring_blocks(1, 1, near2)
    ring_blocks(2, 1, onward(near2))
    near = run(2, "near")
    last = run(3, "far", (first, own, near))
    mine = exchange(last.reshape(CHIPS, 1, 128), RETURNS).reshape(CHIPS, 128)
    best = answer(0, info, mine)
    return answer(1, info, send(mine, SIBLING), best).reshape(ROWS)


def solution(mesh):
    return jax.shard_map(
        local,
        mesh=mesh,
        in_specs=(P(AXES, None), P(AXES), P(AXES)),
        out_specs=P(AXES),
        check_vma=False,
    )
```

time: 170 us -> 168 us (0.988)
  waiting for transfers between devices: 66.8 us -> 61.1 us
  local copies, waits for them, and re-layouts: 3.13 us -> 8.7 us
  starting transfers between devices: 38.7 us -> 34 us
  Pallas kernels: 39.6 us -> 42.7 us
    unnamed x28 -> x50, local copies, waits for them, and re-layouts: 3.13 us -> 8.7 us
    ppermute x11 -> x10, starting transfers between devices: 19.6 us -> 14.9 us  [send(): return lax.ppermute(rows, AXES, pairs)]
    pallas_call x8, Pallas kernels: 37.3 us -> 41.2 us  [the longest x4 32.1 us: similar(): pl.pallas_call(functools.partial(similar_kernel, blocks, len(low), len(be...]
    ppermute x11 -> x10, waiting for transfers between devices: 27.3 us -> 24.3 us  [send(): return lax.ppermute(rows, AXES, pairs)]
    all_to_all x2, waiting for transfers between devices: 39.5 us -> 36.8 us  [exchange(): lax.all_to_all(rows, AXES, split_axis=0, concat_axis=0, tiled=True, axis_...]
  transfers between devices with their start and end apart: 13 -> 12, of which waited for: 7 -> 7; matrix products, arithmetic and copies ran while one was open for 0% -> 0% of each run, Pallas kernels for 17% -> 19%
where the time goes in v6:
time: 168 us; the launch traced here: 167 us
  waiting for transfers between devices  61.1 us (36%)
  Pallas kernels  42.7 us (25%)
  starting transfers between devices  34 us (20%)
  blocking collectives  20.5 us (12%)
  local copies, waits for them, and re-layouts  8.7 us (5%)
    all_to_all x2, waiting for transfers between devices, exchange(): lax.all_to_all(rows, AXES, split_axis=0, concat_axis=0, tiled=True, axis_...  36.8 us
    pallas_call x4, Pallas kernels, similar(): pl.pallas_call(functools.partial(similar_kernel, blocks, len(low), len(be...  32.1 us
    ppermute x10, waiting for transfers between devices, send(): return lax.ppermute(rows, AXES, pairs)  24.3 us
    all_to_all x1, blocking collectives, exchange(): lax.all_to_all(rows, AXES, split_axis=0, concat_axis=0, tiled=True, axis_...  20.5 us
    all_to_all x2, starting transfers between devices, exchange(): lax.all_to_all(rows, AXES, split_axis=0, concat_axis=0, tiled=True, axis_...  19.1 us
    ppermute x10, starting transfers between devices, send(): return lax.ppermute(rows, AXES, pairs)  14.9 us
    unnamed x50, local copies, waits for them, and re-layouts  8.7 us
    pallas_call x1, Pallas kernels, prep(): pl.pallas_call(prep_kernel, out_shape=(jax.ShapeDtypeStruct((SOURCES, CEL...  5.46 us
  transfers between devices with their start and end apart: 12, of which 7 were waited for; matrix products, arithmetic and copies ran while one was open for 0% of the time, Pallas kernels for 19%

profile of v6, /device:TPU:1, one launch (start us, length us, event | category | flops | bytes accessed | tf_op | source)
XLA Modules:
  0.0 167.3 jit_solution(13983705868776101999)
XLA Ops:
  0.0 5.5 %prep.1 = (bf16[32,200,128]{2,1,0:T(8,128)(2,1)}, s32[8,1024]{1,0:T(8,128)}) custom-call(bf16[1024,768]{1,0:T(8,128)(2,1)} %emb_ref.3, s32[1,1024]{1,0:T(1,128)} %bitcast.10, s32[1,1024]{1,0:T(1,128)} %bitcast.12), custom_call_target="tpu_custom_call" | custom-call | flops 1610612736 | bytes 3145728 | tf_op jit(solution)/shard_map/prep/pallas_call | solution.py:160
  5.5 0.0 copy-start
  5.5 0.0 copy-start.16
  5.5 0.0 copy-start.17
  5.5 0.0 copy-start.20
  5.5 12.0 %all-to-all-start = ((bf16[32,200,128]{2,1,0:T(8,128)(2,1)}), bf16[32,200,128]{2,1,0:T(8,128)(2,1)S(1)}, u32[]{:S(2)}, u32[]{:S(2)}) async-start(bf16[32,200,128]{2,1,0:T(8,128)(2,1)} %get-tuple-element.25), calls=%async_computation | async-start | bytes 3276800 | tf_op jit(solution)/shard_map/all_to_all | solution.py:56
  17.5 0.0 copy-done
  17.5 0.0 copy-done.16
  17.6 0.0 copy-done.17
  17.6 0.0 copy-done.20
  17.6 2.4 %hand.1 = bf16[32,200,128]{2,1,0:T(8,128)(2,1)S(1)} custom-call(bf16[1024,768]{1,0:T(8,128)(2,1)S(1)} %copy-done, s32[8,1024]{1,0:T(8,128)S(1)} %copy-done.20, s32[1,1024]{1,0:T(1,128)S(1)} %bitcast.11, s32[1,1024]{1,0:T(1,128)S(1)} %bitcast.13), custom_call_target="tpu_custom_call" | custom-call | flops 1610612736 | bytes 3145728 | tf_op jit(solution)/shard_map/hand/pallas_call | solution.py:189
  20.0 1.2 collective-permute-start
  21.2 3.3 %collective-permute-done = bf16[32,200,128]{2,1,0:T(8,128)(2,1)} collective-permute-done((bf16[32,200,128]{2,1,0:T(8,128)(2,1)S(1)}, bf16[32,200,128]{2,1,0:T(8,128)(2,1)}, u32[]{:S(2)}, u32[]{:S(2)}) %collective-permute-start) | collective-permute-done | bytes 1638432 | tf_op jit(solution)/shard_map/ppermute | solution.py:60
  24.5 31.8 %all-to-all-done.cells_ref = bf16[32,200,128]{2,1,0:T(8,128)(2,1)S(1)} async-done(((bf16[32,200,128]{2,1,0:T(8,128)(2,1)}), bf16[32,200,128]{2,1,0:T(8,128)(2,1)S(1)}, u32[]{:S(2)}, u32[]{:S(2)}) %all-to-all-start) | async-done | bytes 1638432 | tf_op jit(solution)/shard_map/all_to_all | solution.py:56
  56.3 7.1 %all-to-all-start.1 = ((bf16[32,200,128]{2,1,0:T(8,128)(2,1)}), bf16[32,200,128]{2,1,0:T(8,128)(2,1)S(1)}, u32[]{:S(2)}, u32[]{:S(2)}) async-start(bf16[32,200,128]{2,1,0:T(8,128)(2,1)} %collective-permute-done), calls=%async_computation.1 | async-start | bytes 3276800 | tf_op jit(solution)/shard_map/all_to_all | solution.py:56
  63.4 0.0 copy-start.19
  63.4 0.8 settle.1
  64.2 0.0 copy-start.1
  64.2 0.0 copy-start.4
  64.2 1.4 collective-permute-start.1
  65.6 1.5 collective-permute-start.2
  67.1 13.1 %collective-permute-done.1.refs_3_.refs_5_ = bf16[528,768]{1,0:T(8,128)(2,1)S(1)} collective-permute-done((bf16[528,768]{1,0:T(8,128)(2,1)S(1)}, bf16[528,768]{1,0:T(8,128)(2,1)S(1)}, u32[]{:S(2)}, u32[]{:S(2)}) %collective-permute-start.1) | collective-permute-done | bytes 811040 | tf_op jit(solution)/shard_map/ppermute | solution.py:60
  80.2 0.0 collective-permute-start.3
  80.2 0.0 collective-permute-done.2.refs_4_.refs_6_
  80.2 0.0 copy-start.8
  80.2 2.7 %collective-permute-start.4 = (bf16[528,768]{1,0:T(8,128)(2,1)S(1)}, bf16[528,768]{1,0:T(8,128)(2,1)S(1)}, u32[]{:S(2)}, u32[]{:S(2)}) collective-permute-start(bf16[528,768]{1,0:T(8,128)(2,1)S(1)} %collective-permute-done.2.refs_4_.refs_6_), channel_id=1, source_target_pairs={{0,3},{4,196},{1,0},{5,197},{2,1},{6,198},{3,2},{7,199},{8,11},{12... | collective-permute-start | bytes 2433032 | tf_op jit(solution)/shard_map/ppermute | solution.py:60
  82.8 0.0 copy-done.19
  82.8 6.2 %first.1.refs_6_ = f32[64,128]{1,0:T(8,128)S(1)} custom-call(s32[21]{0:T(128)S(1)} %copy-done.19, bf16[528,768]{1,0:T(8,128)(2,1)S(1)} %get-tuple-element.33.refs_1_, bf16[528,768]{1,0:T(8,128)(2,1)S(1)} %get-tuple-element.34.refs_2_, bf16[528,768]{1,0:T(8,128)(2,1)S(1)} %collective-permute-done.1.refs_3_.refs_5_, ...), custom_call_target="tpu_custom_call" | custom-call | flops 2818572288 | bytes 3145728 | tf_op jit(solution)/shard_map/first/pallas_call | solution.py:406
  89.1 0.0 copy-done.1
  89.1 0.0 copy-done.4
  89.1 0.0 copy-done.6
  89.1 0.0 copy-done.8
  89.1 0.0 copy-start.23
  89.1 0.0 copy-start.24
  89.1 6.0 %collective-permute-done.3.refs_7_.refs_9_ = bf16[528,768]{1,0:T(8,128)(2,1)S(1)} collective-permute-done((bf16[528,768]{1,0:T(8,128)(2,1)S(1)}, bf16[528,768]{1,0:T(8,128)(2,1)S(1)}, u32[]{:S(2)}, u32[]{:S(2)}) %collective-permute-start.3) | collective-permute-done | bytes 811040 | tf_op jit(solution)/shard_map/ppermute | solution.py:60
  95.1 0.9 copy-done.10
  96.0 0.0 collective-permute-done.4.refs_8_.refs_10_
  96.0 0.9 copy-done.13
  96.9 5.0 %all-to-all-done.1.cells_ref = bf16[32,200,128]{2,1,0:T(8,128)(2,1)S(1)} async-done(((bf16[32,200,128]{2,1,0:T(8,128)(2,1)}), bf16[32,200,128]{2,1,0:T(8,128)(2,1)S(1)}, u32[]{:S(2)}, u32[]{:S(2)}) %all-to-all-start.1) | async-done | bytes 1638432 | tf_op jit(solution)/shard_map/all_to_all | solution.py:56
  101.9 0.4 split.1
  102.3 1.0 collective-permute-start.5
  103.3 1.7 %collective-permute-start.6 = (bf16[528,768]{1,0:T(8,128)(2,1)S(1)}, bf16[528,768]{1,0:T(8,128)(2,1)}, u32[]{:S(2)}, u32[]{:S(2)}) collective-permute-start(bf16[528,768]{1,0:T(8,128)(2,1)S(1)} %get-tuple-element.32.refs_4_.refs_2_), channel_id=1, source_target_pairs={{0,3},{4,196},{1,0},{5,197},{2,1},{6,198},{3,2},{7,199},{8,11},{12... | collective-permute-start | bytes 2433032 | tf_op jit(solution)/shard_map/ppermute | solution.py:60
  105.1 1.1 copy-done.2
  106.2 1.1 copy-done.5
  107.3 1.1 copy-done.7
  108.5 1.1 copy-done.9
  109.6 1.1 copy-done.11
  110.8 1.1 copy-done.14
  111.9 0.0 copy-start.15
  111.9 0.0 copy-start.18
  111.9 11.7 %own.1.refs_7_ = f32[64,128]{1,0:T(8,128)S(1)} custom-call(s32[42]{0:T(128)S(1)} %broadcast_select_fusion.refs_0_, bf16[528,768]{1,0:T(8,128)(2,1)S(1)} %copy-done.2, bf16[528,768]{1,0:T(8,128)(2,1)S(1)} %copy-done.5, bf16[528,768]{1,0:T(8,128)(2,1)S(1)} %get-tuple-element.31.refs_3_.refs_1_, bf16[528,768]{1,0:T(8,128)(2,1)S(1)} %get-tuple-element.32.refs_4_.refs_2_, ...), custom_call_target="tpu_custom_call" | custom-call | flops 5637144576 | bytes 6291456 | tf_op jit(solution)/shard_map/own/pallas_call | solution.py:406
  123.6 0.0 collective-permute-done.5.refs_7_.refs_3_
  123.6 0.0 collective-permute-done.6.refs_8_
  123.6 1.1 collective-permute-start.8
  124.7 0.5 collective-permute-start.7
  125.2 10.6 %near.1.refs_8_ = f32[64,128]{1,0:T(8,128)S(1)} custom-call(s32[33]{0:T(128)S(1)} %copy-done.18, bf16[528,768]{1,0:T(8,128)(2,1)S(1)} %copy-done.3, bf16[528,768]{1,0:T(8,128)(2,1)S(1)} %copy-done.5, bf16[528,768]{1,0:T(8,128)(2,1)S(1)} %get-tuple-element.31.refs_3_.refs_1_, bf16[528,768]{1,0:T(8,128)(2,1)S(1)} %get-tuple-element.32.refs_4_.refs_2_, ...), custom_call_target="tpu_custom_call" | custom-call | flops 4429185024 | bytes 7864320 | tf_op jit(solution)/shard_map/near/pallas_call | solution.py:406
  135.8 0.0 collective-permute-done.8.refs_5_
  135.8 1.5 collective-permute-done.7.refs_4_
  137.3 3.7 %far.1 = f32[128,128]{1,0:T(8,128)S(1)} custom-call(s32[6]{0:T(128)S(1)} %broadcast_select_fusion.1.refs_0_, bf16[528,768]{1,0:T(8,128)(2,1)S(1)} %get-tuple-element.31.refs_3_.refs_1_, bf16[528,768]{1,0:T(8,128)(2,1)S(1)} %get-tuple-element.32.refs_4_.refs_2_, bf16[528,768]{1,0:T(8,128)(2,1)S(1)} %collective-permute-done.5.refs_7_.refs_3_, ...), custom_call_target="tpu_custom_call" | custom-call | flops 805306368 | bytes 3932160 | tf_op jit(solution)/shard_map/far/pallas_call | solution.py:406
  141.0 20.5 %all_to_all.15 = f32[128,1,128]{2,1,0:T(1,128)S(1)} all-to-all(f32[128,1,128]{2,1,0:T(1,128)S(1)} %bitcast.7), channel_id=1, replica_groups={{0,8,16,24,32,40,48,56,64,72,80,88,96,104,112,120,128,136,144,152,160,1..., dimensions={0} | all-to-all | bytes 131072 | tf_op jit(solution)/shard_map/all_to_all | solution.py:56
  161.5 3.9 %collective-permute-start.9 = (f32[128,128]{1,0:T(8,128)S(1)}, f32[128,128]{1,0:T(8,128)S(1)}, u32[]{:S(2)}, u32[]{:S(2)}) collective-permute-start(f32[128,128]{1,0:T(8,128)S(1)} %bitcast.8), channel_id=1, source_target_pairs={{0,4},{1,5},{2,6},{3,7},{4,0},{5,1},{6,2},{7,3},{8,12},{9,13},{10,... | collective-permute-start | bytes 196616 | tf_op jit(solution)/shard_map/ppermute | solution.py:60
  165.4 0.5 answer.2.refs_0_
  165.8 0.4 collective-permute-done.9.values_ref
  166.3 1.0 answer.3
  (23 shorter events, 0.0 us)
Async XLA Ops:
  5.5 12.1 %copy-start = (bf16[1024,768]{1,0:T(8,128)(2,1)S(1)}, bf16[1024,768]{1,0:T(8,128)(2,1)}, u32[]{:S(2)}) copy-start(bf16[1024,768]{1,0:T(8,128)(2,1)} %emb_ref.3) | copy-start | bytes 4718596
  5.5 12.1 %copy-start.16 = (s32[1024]{0:T(1024)S(1)}, s32[1024]{0:T(1024)}, u32[]{:S(2)}) copy-start(s32[1024]{0:T(1024)} %param.10) | copy-start | bytes 12292
  5.5 12.1 %copy-start.17 = (s32[1024]{0:T(1024)S(1)}, s32[1024]{0:T(1024)}, u32[]{:S(2)}) copy-start(s32[1024]{0:T(1024)} %param.11) | copy-start | bytes 12292
  5.5 12.1 %copy-start.20 = (s32[8,1024]{1,0:T(8,128)S(1)}, s32[8,1024]{1,0:T(8,128)}, u32[]{:S(2)}) copy-start(s32[8,1024]{1,0:T(8,128)} %get-tuple-element.24.info_ref) | copy-start | bytes 98308
  5.5 50.8 %all-to-all-start = ((bf16[32,200,128]{2,1,0:T(8,128)(2,1)}), bf16[32,200,128]{2,1,0:T(8,128)(2,1)S(1)}, u32[]{:S(2)}, u32[]{:S(2)}) async-start(bf16[32,200,128]{2,1,0:T(8,128)(2,1)} %get-tuple-element.25), calls=%async_computation | async-start | bytes 3276800 | tf_op jit(solution)/shard_map/all_to_all | solution.py:56
  20.0 4.5 %collective-permute-start = (bf16[32,200,128]{2,1,0:T(8,128)(2,1)S(1)}, bf16[32,200,128]{2,1,0:T(8,128)(2,1)}, u32[]{:S(2)}, u32[]{:S(2)}) collective-permute-start(bf16[32,200,128]{2,1,0:T(8,128)(2,1)S(1)} %hand.1), channel_id=1, source_target_pairs={{0,4},{1,5},{2,6},{3,7},{4,0},{5,1},{6,2},{7,3},{8,12},{9,13},{10,... | collective-permute-start | bytes 4915208 | tf_op jit(solution)/shard_map/ppermute | solution.py:60
  56.3 45.6 %all-to-all-start.1 = ((bf16[32,200,128]{2,1,0:T(8,128)(2,1)}), bf16[32,200,128]{2,1,0:T(8,128)(2,1)S(1)}, u32[]{:S(2)}, u32[]{:S(2)}) async-start(bf16[32,200,128]{2,1,0:T(8,128)(2,1)} %collective-permute-done), calls=%async_computation.1 | async-start | bytes 3276800 | tf_op jit(solution)/shard_map/all_to_all | solution.py:56
  63.4 19.4 %copy-start.19 = (s32[21]{0:T(128)S(1)}, s32[21]{0:T(128)}, u32[]{:S(2)}) copy-start(s32[21]{0:T(128)} %constant.29.clone.refs_0_) | copy-start | bytes 256
  64.2 24.9 %copy-start.1 = (bf16[528,768]{1,0:T(8,128)(2,1)}, bf16[528,768]{1,0:T(8,128)(2,1)S(1)}, u32[]{:S(2)}) copy-start(bf16[528,768]{1,0:T(8,128)(2,1)S(1)} %get-tuple-element.33.refs_1_) | copy-start | bytes 2433028
  64.2 24.9 %copy-start.4 = (bf16[528,768]{1,0:T(8,128)(2,1)}, bf16[528,768]{1,0:T(8,128)(2,1)S(1)}, u32[]{:S(2)}) copy-start(bf16[528,768]{1,0:T(8,128)(2,1)S(1)} %get-tuple-element.34.refs_2_) | copy-start | bytes 2433028
  64.2 15.9 %collective-permute-start.1 = (bf16[528,768]{1,0:T(8,128)(2,1)S(1)}, bf16[528,768]{1,0:T(8,128)(2,1)S(1)}, u32[]{:S(2)}, u32[]{:S(2)}) collective-permute-start(bf16[528,768]{1,0:T(8,128)(2,1)S(1)} %get-tuple-element.33.refs_1_), channel_id=1, source_target_pairs={{0,1},{4,68},{1,2},{5,69},{2,3},{6,70},{3,0},{7,71},{8,9},{12,76},... | collective-permute-start | bytes 2433032 | tf_op jit(solution)/shard_map/ppermute | solution.py:60
  65.6 14.6 %collective-permute-start.2 = (bf16[528,768]{1,0:T(8,128)(2,1)S(1)}, bf16[528,768]{1,0:T(8,128)(2,1)S(1)}, u32[]{:S(2)}, u32[]{:S(2)}) collective-permute-start(bf16[528,768]{1,0:T(8,128)(2,1)S(1)} %get-tuple-element.34.refs_2_), channel_id=1, source_target_pairs={{0,3},{4,196},{1,0},{5,197},{2,1},{6,198},{3,2},{7,199},{8,11},{12... | collective-permute-start | bytes 2433032 | tf_op jit(solution)/shard_map/ppermute | solution.py:60
  80.1 8.9 %copy-start.6 = (bf16[528,768]{1,0:T(8,128)(2,1)}, bf16[528,768]{1,0:T(8,128)(2,1)S(1)}, u32[]{:S(2)}) copy-start(bf16[528,768]{1,0:T(8,128)(2,1)S(1)} %collective-permute-done.1.refs_3_.refs_5_) | copy-start | bytes 2433028
  80.2 15.0 %collective-permute-start.3 = (bf16[528,768]{1,0:T(8,128)(2,1)S(1)}, bf16[528,768]{1,0:T(8,128)(2,1)S(1)}, u32[]{:S(2)}, u32[]{:S(2)}) collective-permute-start(bf16[528,768]{1,0:T(8,128)(2,1)S(1)} %collective-permute-done.1.refs_3_.refs_5_), channel_id=1, source_target_pairs={{0,1},{4,68},{1,2},{5,69},{2,3},{6,70},{3,0},{7,71},{8,9},{12,76},... | collective-permute-start | bytes 2433032 | tf_op jit(solution)/shard_map/ppermute | solution.py:60
  80.2 8.9 %copy-start.8 = (bf16[528,768]{1,0:T(8,128)(2,1)}, bf16[528,768]{1,0:T(8,128)(2,1)S(1)}, u32[]{:S(2)}) copy-start(bf16[528,768]{1,0:T(8,128)(2,1)S(1)} %collective-permute-done.2.refs_4_.refs_6_) | copy-start | bytes 2433028
  80.2 15.8 %collective-permute-start.4 = (bf16[528,768]{1,0:T(8,128)(2,1)S(1)}, bf16[528,768]{1,0:T(8,128)(2,1)S(1)}, u32[]{:S(2)}, u32[]{:S(2)}) collective-permute-start(bf16[528,768]{1,0:T(8,128)(2,1)S(1)} %collective-permute-done.2.refs_4_.refs_6_), channel_id=1, source_target_pairs={{0,3},{4,196},{1,0},{5,197},{2,1},{6,198},{3,2},{7,199},{8,11},{12... | collective-permute-start | bytes 2433032 | tf_op jit(solution)/shard_map/ppermute | solution.py:60
  89.1 15.9 %copy-start.23 = (s32[42]{0:T(128)S(1)}, s32[42]{0:T(128)}, u32[]{:S(2)}) copy-start(s32[42]{0:T(128)} %constant.31.clone) | copy-start | bytes 508
  89.1 15.9 %copy-start.24 = (s32[42]{0:T(128)S(1)}, s32[42]{0:T(128)}, u32[]{:S(2)}) copy-start(s32[42]{0:T(128)} %constant.30.clone) | copy-start | bytes 508
  95.1 0.9 copy-start.10
  96.0 0.9 copy-start.13
  102.3 21.3 %collective-permute-start.5 = (bf16[528,768]{1,0:T(8,128)(2,1)S(1)}, bf16[528,768]{1,0:T(8,128)(2,1)S(1)}, u32[]{:S(2)}, u32[]{:S(2)}) collective-permute-start(bf16[528,768]{1,0:T(8,128)(2,1)S(1)} %get-tuple-element.31.refs_3_.refs_1_), channel_id=1, source_target_pairs={{0,1},{4,68},{1,2},{5,69},{2,3},{6,70},{3,0},{7,71},{8,9},{12,76},... | collective-permute-start | bytes 2433032 | tf_op jit(solution)/shard_map/ppermute | solution.py:60
  103.3 20.3 %collective-permute-start.6 = (bf16[528,768]{1,0:T(8,128)(2,1)S(1)}, bf16[528,768]{1,0:T(8,128)(2,1)}, u32[]{:S(2)}, u32[]{:S(2)}) collective-permute-start(bf16[528,768]{1,0:T(8,128)(2,1)S(1)} %get-tuple-element.32.refs_4_.refs_2_), channel_id=1, source_target_pairs={{0,3},{4,196},{1,0},{5,197},{2,1},{6,198},{3,2},{7,199},{8,11},{12... | collective-permute-start | bytes 2433032 | tf_op jit(solution)/shard_map/ppermute | solution.py:60
  105.1 1.1 copy-start.2
  106.2 1.1 copy-start.5
  107.3 1.1 copy-start.7
  108.5 1.1 copy-start.9
  109.6 1.1 copy-start.11
  110.8 1.1 copy-start.14
  111.9 13.3 %copy-start.21 = (s32[6]{0:T(128)S(1)}, s32[6]{0:T(128)}, u32[]{:S(2)}) copy-start(s32[6]{0:T(128)} %constant.34.clone) | copy-start | bytes 76
  111.9 13.3 %copy-start.22 = (s32[6]{0:T(128)S(1)}, s32[6]{0:T(128)}, u32[]{:S(2)}) copy-start(s32[6]{0:T(128)} %constant.33.clone) | copy-start | bytes 76
  111.9 13.3 %copy-start.3 = (bf16[528,768]{1,0:T(8,128)(2,1)S(1)}, bf16[528,768]{1,0:T(8,128)(2,1)}, u32[]{:S(2)}) copy-start(bf16[528,768]{1,0:T(8,128)(2,1)} %copy-done.1) | copy-start | bytes 2433028
  111.9 13.3 %copy-start.12 = (bf16[528,768]{1,0:T(8,128)(2,1)S(1)}, bf16[528,768]{1,0:T(8,128)(2,1)}, u32[]{:S(2)}) copy-start(bf16[528,768]{1,0:T(8,128)(2,1)} %copy-done.10) | copy-start | bytes 2433028
  111.9 13.3 %copy-start.15 = (bf16[528,768]{1,0:T(8,128)(2,1)S(1)}, bf16[528,768]{1,0:T(8,128)(2,1)}, u32[]{:S(2)}) copy-start(bf16[528,768]{1,0:T(8,128)(2,1)} %copy-done.13) | copy-start | bytes 2433028
  111.9 13.3 %copy-start.18 = (s32[33]{0:T(128)S(1)}, s32[33]{0:T(128)}, u32[]{:S(2)}) copy-start(s32[33]{0:T(128)} %constant.32.clone.refs_0_) | copy-start | bytes 400
  123.6 12.2 %collective-permute-start.8 = (bf16[528,768]{1,0:T(8,128)(2,1)}, bf16[528,768]{1,0:T(8,128)(2,1)S(1)}, u32[]{:S(2)}, u32[]{:S(2)}) collective-permute-start(bf16[528,768]{1,0:T(8,128)(2,1)} %collective-permute-done.6.refs_8_), channel_id=1, source_target_pairs={{0,3},{4,196},{1,0},{5,197},{2,1},{6,198},{3,2},{7,199},{8,11},{12... | collective-permute-start | bytes 2433032 | tf_op jit(solution)/shard_map/ppermute | solution.py:60
  124.7 12.6 %collective-permute-start.7 = (bf16[528,768]{1,0:T(8,128)(2,1)S(1)}, bf16[528,768]{1,0:T(8,128)(2,1)S(1)}, u32[]{:S(2)}, u32[]{:S(2)}) collective-permute-start(bf16[528,768]{1,0:T(8,128)(2,1)S(1)} %collective-permute-done.5.refs_7_.refs_3_), channel_id=1, source_target_pairs={{0,1},{4,68},{1,2},{5,69},{2,3},{6,70},{3,0},{7,71},{8,9},{12,76},... | collective-permute-start | bytes 2433032 | tf_op jit(solution)/shard_map/ppermute | solution.py:60
  161.5 4.8 %collective-permute-start.9 = (f32[128,128]{1,0:T(8,128)S(1)}, f32[128,128]{1,0:T(8,128)S(1)}, u32[]{:S(2)}, u32[]{:S(2)}) collective-permute-start(f32[128,128]{1,0:T(8,128)S(1)} %bitcast.8), channel_id=1, source_target_pairs={{0,4},{1,5},{2,6},{3,7},{4,0},{5,1},{6,2},{7,3},{8,12},{9,13},{10,... | collective-permute-start | bytes 196616 | tf_op jit(solution)/shard_map/ppermute | solution.py:60

commit v7 on v6

--- a/solution.py
+++ b/solution.py
@@ -23,7 +23,10 @@
 HALF_ROWS = 512
 ORDERS = 4096
 VMEM = 24 * 1024 * 1024
-FULL = 56 * 1024 * 1024
+FULL = 58 * 1024 * 1024
+PAIRS = 32 * 1024 * 1024
+OWN = 121 * 512 * 1024
+NEAR = 59 * 1024 * 1024
 
 
 def device(x, y, z, core):
@@ -283,7 +286,7 @@
     return parts
 
 
-def similar_kernel(blocks, n_tasks, n_before, *refs):
+def similar_kernel(blocks, early, n_tasks, n_before, *refs):
     n_blocks = len(blocks)
     tasks_ref, refs = refs[0], refs[1:]
     arrays, refs = refs[:n_blocks], refs[n_blocks:]
@@ -300,15 +303,17 @@
     def cluster(key):
         return jnp.where(key >= ORDERS + 128, 2.0, jnp.where(key > 0, 1.0, 0.0))
 
-    for slot, copy in enumerate(copies):
-        copy.wait()
-        parts = rows[slot, HALF_ROWS:, :HALF_ROWS].astype(jnp.float32)
-        key = 128.0 * parts[0:1] + parts[1:2]
-        krow[slot] = jnp.broadcast_to(key, (8, HALF_ROWS))
-        crow[slot] = cluster(krow[slot])
-        key = jnp.transpose(jnp.broadcast_to(key, (128, HALF_ROWS)))
-        kcol[slot] = key
-        ccol[slot] = cluster(key)
+    def arrive(slots):
+        for slot in slots:
+            copies[slot].wait()
+        for slot in slots:
+            parts = rows[slot, HALF_ROWS:, :HALF_ROWS].astype(jnp.float32)
+            key = 128.0 * parts[0:1] + parts[1:2]
+            krow[slot] = jnp.broadcast_to(key, (8, HALF_ROWS))
+            crow[slot] = cluster(krow[slot])
+            key = jnp.transpose(jnp.broadcast_to(key, (128, HALF_ROWS)))
+            kcol[slot] = key
+            ccol[slot] = cluster(key)
 
     def multiply(task, s):
         a, b = tasks_ref[3 * task], tasks_ref[3 * task + 1]
@@ -340,9 +345,14 @@
         return carry
 
     turns = (n_tasks - 1) // 2
+    start, early = early
+    arrive(range(early))
     multiply(0, s0)
-    if turns:
-        lax.fori_loop(0, turns, two, 0)
+    if start:
+        lax.fori_loop(0, start, two, 0)
+    arrive(range(early, n_blocks))
+    if turns > start:
+        lax.fori_loop(start, turns, two, 0)
     if n_tasks % 2 == 0:
         multiply(n_tasks - 1, s1)
     reduce(2 * turns, s0)
@@ -390,8 +400,14 @@
     )
 
 
-def similar(hold, low, high, ring_place, befores, name):
-    blocks = [block for block in BLOCKS if any(block in pair for pair in low + high)]
+def similar(hold, low, high, ring_place, befores, name, limit, start):
+    first_use = {}
+    for number, pairs in enumerate(zip(low, high)):
+        for pair in pairs:
+            for block in pair:
+                first_use.setdefault(block, number)
+    blocks = sorted(first_use, key=lambda block: (first_use[block], BLOCKS.index(block)))
+    early = start, sum(first_use[block] <= 2 * start for block in blocks)
     place = {block: number for number, block in enumerate(blocks)}
     spare = n = len(blocks)
 
@@ -404,7 +420,7 @@
     if low != high:
         tasks = jnp.where(ring_place < 2, tasks, jnp.asarray(table(high)))
     return pl.pallas_call(
-        functools.partial(similar_kernel, blocks, len(low), len(befores)),
+        functools.partial(similar_kernel, blocks, early, len(low), len(befores)),
         out_shape=jax.ShapeDtypeStruct((CHIPS if befores else 2 * SOURCES, 128), jnp.float32),
         in_specs=[pl.BlockSpec(memory_space=pltpu.SMEM)]
         + [pl.BlockSpec(memory_space=pl.ANY)] * n
@@ -422,7 +438,7 @@
             pltpu.VMEM((HALF_ROWS, HALF_ROWS), jnp.float32),
             pltpu.SemaphoreType.DMA((n,)),
         ],
-        compiler_params=pltpu.CompilerParams(vmem_limit_bytes=32 * 1024 * 1024),
+        compiler_params=pltpu.CompilerParams(vmem_limit_bytes=limit),
         cost_estimate=cost(2 * D * HALF_ROWS * HALF_ROWS * len(low), 2 * n * HALF_ROWS * D),
         name=name,
     )(tasks, *[hold[block] for block in blocks], *befores)
@@ -488,12 +504,14 @@
 
     def run(stage, name, befores=()):
         low = [pair for pair in pairs if stage_of(pair) == stage]
+        low.sort(key=lambda pair: sum(chunk == 0 for part, far, chunk in pair))
         high = list(low)
         for one, other in by_place:
             if stage_of(one) == stage:
                 low.append(one)
                 high.append(other)
-        return similar(hold, low, high, ring_place, befores, name)
+        limit, start = ((PAIRS, 0), (OWN, 1), (NEAR, 1), (PAIRS, 0))[stage]
+        return similar(hold, low, high, ring_place, befores, name, limit, start)
 
     own1 = ring_blocks(0, 0, open_cells(chunk1, True))
     near1 = ring_blocks(1, 0, onward(own1))

time: 168 us -> 165 us (0.982)
  local copies, waits for them, and re-layouts: 8.7 us -> 3.77 us
    unnamed x50 -> x46, local copies, waits for them, and re-layouts: 8.7 us -> 3.77 us
  transfers between devices with their start and end apart: 12 -> 12, of which waited for: 7 -> 7; matrix products, arithmetic and copies ran while one was open for 0% -> 0% of each run, Pallas kernels for 19% -> 21%
where the time goes in v7:
time: 165 us; the launch traced here: 164 us
  waiting for transfers between devices  60.2 us (36%)
  Pallas kernels  44.1 us (27%)
  starting transfers between devices  33.9 us (21%)
  blocking collectives  21.6 us (13%)
  local copies, waits for them, and re-layouts  3.77 us (2%)
    all_to_all x2, waiting for transfers between devices, exchange(): lax.all_to_all(rows, AXES, split_axis=0, concat_axis=0, tiled=True, axis_...  36.8 us
    pallas_call x4, Pallas kernels, similar(): pl.pallas_call(functools.partial(similar_kernel, blocks, early, len(low),...  33.6 us
    ppermute x10, waiting for transfers between devices, send(): return lax.ppermute(rows, AXES, pairs)  23.4 us
    all_to_all x1, blocking collectives, exchange(): lax.all_to_all(rows, AXES, split_axis=0, concat_axis=0, tiled=True, axis_...  21.6 us
    all_to_all x2, starting transfers between devices, exchange(): lax.all_to_all(rows, AXES, split_axis=0, concat_axis=0, tiled=True, axis_...  19.1 us
    ppermute x10, starting transfers between devices, send(): return lax.ppermute(rows, AXES, pairs)  14.8 us
    pallas_call x1, Pallas kernels, prep(): pl.pallas_call(prep_kernel, out_shape=(jax.ShapeDtypeStruct((SOURCES, CEL...  5.45 us
    unnamed x46, local copies, waits for them, and re-layouts  3.77 us
  transfers between devices with their start and end apart: 12, of which 7 were waited for; matrix products, arithmetic and copies ran while one was open for 0% of the time, Pallas kernels for 21%

profile of v7, /device:TPU:1, one launch (start us, length us, event | category | flops | bytes accessed | tf_op | source)
XLA Modules:
  0.0 164.5 jit_solution(4133077447854970892)
XLA Ops:
  0.0 5.5 %prep.1 = (bf16[32,200,128]{2,1,0:T(8,128)(2,1)}, s32[8,1024]{1,0:T(8,128)}) custom-call(bf16[1024,768]{1,0:T(8,128)(2,1)} %emb_ref.3, s32[1,1024]{1,0:T(1,128)} %bitcast.10, s32[1,1024]{1,0:T(1,128)} %bitcast.12), custom_call_target="tpu_custom_call" | custom-call | flops 1610612736 | bytes 3145728 | tf_op jit(solution)/shard_map/prep/pallas_call | solution.py:163
  5.5 0.0 copy-start.8
  5.5 0.0 copy-start.13
  5.5 0.0 copy-start.14
  5.5 0.0 copy-start.16
  5.5 12.0 %all-to-all-start = ((bf16[32,200,128]{2,1,0:T(8,128)(2,1)}), bf16[32,200,128]{2,1,0:T(8,128)(2,1)S(1)}, u32[]{:S(2)}, u32[]{:S(2)}) async-start(bf16[32,200,128]{2,1,0:T(8,128)(2,1)} %get-tuple-element.25), calls=%async_computation | async-start | bytes 3276800 | tf_op jit(solution)/shard_map/all_to_all | solution.py:59
  17.5 0.0 copy-done.8
  17.5 0.0 copy-done.13
  17.6 0.0 copy-done.14
  17.6 0.0 copy-done.16
  17.6 2.4 %hand.1 = bf16[32,200,128]{2,1,0:T(8,128)(2,1)S(1)} custom-call(bf16[1024,768]{1,0:T(8,128)(2,1)S(1)} %copy-done.8, s32[8,1024]{1,0:T(8,128)S(1)} %copy-done.16, s32[1,1024]{1,0:T(1,128)S(1)} %bitcast.11, s32[1,1024]{1,0:T(1,128)S(1)} %bitcast.13), custom_call_target="tpu_custom_call" | custom-call | flops 1610612736 | bytes 3145728 | tf_op jit(solution)/shard_map/hand/pallas_call | solution.py:192
  20.0 1.2 collective-permute-start
  21.2 3.3 %collective-permute-done = bf16[32,200,128]{2,1,0:T(8,128)(2,1)} collective-permute-done((bf16[32,200,128]{2,1,0:T(8,128)(2,1)S(1)}, bf16[32,200,128]{2,1,0:T(8,128)(2,1)}, u32[]{:S(2)}, u32[]{:S(2)}) %collective-permute-start) | collective-permute-done | bytes 1638432 | tf_op jit(solution)/shard_map/ppermute | solution.py:63
  24.5 31.8 %all-to-all-done.cells_ref = bf16[32,200,128]{2,1,0:T(8,128)(2,1)S(1)} async-done(((bf16[32,200,128]{2,1,0:T(8,128)(2,1)}), bf16[32,200,128]{2,1,0:T(8,128)(2,1)S(1)}, u32[]{:S(2)}, u32[]{:S(2)}) %all-to-all-start) | async-done | bytes 1638432 | tf_op jit(solution)/shard_map/all_to_all | solution.py:59
  56.3 7.1 %all-to-all-start.1 = ((bf16[32,200,128]{2,1,0:T(8,128)(2,1)}), bf16[32,200,128]{2,1,0:T(8,128)(2,1)S(1)}, u32[]{:S(2)}, u32[]{:S(2)}) async-start(bf16[32,200,128]{2,1,0:T(8,128)(2,1)} %collective-permute-done), calls=%async_computation.1 | async-start | bytes 3276800 | tf_op jit(solution)/shard_map/all_to_all | solution.py:59
  63.4 0.0 copy-start.15
  63.4 0.8 settle.1
  64.2 0.0 copy-start.9
  64.2 0.0 copy-start.10
  64.2 1.4 collective-permute-start.1
  65.6 1.5 collective-permute-start.2
  67.1 13.1 %collective-permute-done.1.refs_2_.refs_4_.refs_7_ = bf16[528,768]{1,0:T(8,128)(2,1)S(1)} collective-permute-done((bf16[528,768]{1,0:T(8,128)(2,1)S(1)}, bf16[528,768]{1,0:T(8,128)(2,1)S(1)}, u32[]{:S(2)}, u32[]{:S(2)}) %collective-permute-start.1) | collective-permute-done | bytes 811040 | tf_op jit(solution)/shard_map/ppermute | solution.py:63
  80.1 0.0 collective-permute-start.3
  80.2 0.0 collective-permute-done.2.refs_4_.refs_7_.refs_8_
  80.2 0.0 copy-start.12
  80.2 2.7 %collective-permute-start.4 = (bf16[528,768]{1,0:T(8,128)(2,1)S(1)}, bf16[528,768]{1,0:T(8,128)(2,1)S(1)}, u32[]{:S(2)}, u32[]{:S(2)}) collective-permute-start(bf16[528,768]{1,0:T(8,128)(2,1)S(1)} %collective-permute-done.2.refs_4_.refs_7_.refs_8_), channel_id=1, source_target_pairs={{0,3},{4,196},{1,0},{5,197},{2,1},{6,198},{3,2},{7,199},{8,11},{12... | collective-permute-start | bytes 2433032 | tf_op jit(solution)/shard_map/ppermute | solution.py:63
  82.8 0.0 copy-done.15
  82.8 6.0 %first.1.refs_6_ = f32[64,128]{1,0:T(8,128)S(1)} custom-call(s32[21]{0:T(128)S(1)} %copy-done.15, bf16[528,768]{1,0:T(8,128)(2,1)S(1)} %get-tuple-element.33.refs_1_.refs_3_.refs_5_, bf16[528,768]{1,0:T(8,128)(2,1)S(1)} %collective-permute-done.1.refs_2_.refs_4_.refs_7_, bf16[528,768]{1,0:T(8,128)(2,1)S(1)} %get-tuple-element.36.refs_3_.refs_6_, ...), custom_call_target="tpu_custom_call" | custom-call | flops 2818572288 | bytes 3145728 | tf_op jit(solution)/shard_map/first/pallas_call | solution.py:422
  88.8 0.0 copy-done.9
  88.8 0.0 copy-done.10
  88.8 0.0 copy-done.11
  88.8 0.0 copy-done.12
  88.8 0.0 copy-start.19
  88.9 0.0 copy-start.20
  88.9 6.3 %collective-permute-done.3.refs_5_.refs_10_ = bf16[528,768]{1,0:T(8,128)(2,1)S(1)} collective-permute-done((bf16[528,768]{1,0:T(8,128)(2,1)S(1)}, bf16[528,768]{1,0:T(8,128)(2,1)S(1)}, u32[]{:S(2)}, u32[]{:S(2)}) %collective-permute-start.3) | collective-permute-done | bytes 811040 | tf_op jit(solution)/shard_map/ppermute | solution.py:63
  95.1 0.9 copy-done.21
  96.0 0.0 collective-permute-done.4.refs_8_.refs_9_
  96.0 0.9 copy-done.22
  96.9 5.0 %all-to-all-done.1.cells_ref = bf16[32,200,128]{2,1,0:T(8,128)(2,1)S(1)} async-done(((bf16[32,200,128]{2,1,0:T(8,128)(2,1)}), bf16[32,200,128]{2,1,0:T(8,128)(2,1)S(1)}, u32[]{:S(2)}, u32[]{:S(2)}) %all-to-all-start.1) | async-done | bytes 1638432 | tf_op jit(solution)/shard_map/all_to_all | solution.py:59
  101.9 0.4 split.1
  102.3 0.0 copy-start
  102.3 1.0 collective-permute-start.5
  103.3 1.7 %collective-permute-start.6 = (bf16[528,768]{1,0:T(8,128)(2,1)S(1)}, bf16[528,768]{1,0:T(8,128)(2,1)}, u32[]{:S(2)}, u32[]{:S(2)}) collective-permute-start(bf16[528,768]{1,0:T(8,128)(2,1)S(1)} %get-tuple-element.32.refs_2_.refs_3_.refs_4_), channel_id=1, source_target_pairs={{0,3},{4,196},{1,0},{5,197},{2,1},{6,198},{3,2},{7,199},{8,11},{12... | collective-permute-start | bytes 2433032 | tf_op jit(solution)/shard_map/ppermute | solution.py:63
  105.1 0.0 copy-done.20
  105.1 0.5 broadcast_select_fusion.refs_0_
  105.6 0.0 copy-done
  105.6 12.5 %own.1.refs_7_ = f32[64,128]{1,0:T(8,128)} custom-call(s32[42]{0:T(128)} %broadcast_select_fusion.refs_0_, bf16[528,768]{1,0:T(8,128)(2,1)} %copy-done, bf16[528,768]{1,0:T(8,128)(2,1)} %copy-done.2, bf16[528,768]{1,0:T(8,128)(2,1)} %copy-done.9, bf16[528,768]{1,0:T(8,128)(2,1)} %copy-done.11, bf16[528,768]{1,0:T(8,128)(2,1)} %copy-done.21, ...), custom_call_target="tpu_custom_call" | custom-call | flops 5637144576 | bytes 6291456 | tf_op jit(solution)/shard_map/own/pallas_call | solution.py:422
  118.1 0.0 collective-permute-done.5.refs_2_.refs_1_
  118.1 0.0 copy-start.4
  118.1 0.0 collective-permute-done.6.refs_4_
  118.1 1.1 collective-permute-start.7
  119.2 0.5 collective-permute-start.8
  119.7 11.7 %near.1.refs_8_ = f32[64,128]{1,0:T(8,128)} custom-call(s32[33]{0:T(128)} %constant.32.clone.refs_0_, bf16[528,768]{1,0:T(8,128)(2,1)} %copy-done, bf16[528,768]{1,0:T(8,128)(2,1)} %copy-done.4, bf16[528,768]{1,0:T(8,128)(2,1)} %copy-done.2, bf16[528,768]{1,0:T(8,128)(2,1)} %collective-permute-done.6.refs_4_, bf16[528,768]{1,0:T(8,128)(2,1)} %copy-done.9, ...), custom_call_target="tpu_custom_call" | custom-call | flops 4429185024 | bytes 7864320 | tf_op jit(solution)/shard_map/near/pallas_call | solution.py:422
  131.4 0.0 collective-permute-done.7.refs_2_
  131.4 0.4 collective-permute-done.8.refs_5_
  131.8 0.0 copy-done.3
  131.8 1.1 copy-done.5
  132.9 0.8 copy-done.7
  133.7 3.5 %far.1 = f32[128,128]{1,0:T(8,128)S(1)} custom-call(s32[6]{0:T(128)S(1)} %broadcast_select_fusion.1.refs_0_, bf16[528,768]{1,0:T(8,128)(2,1)S(1)} %copy-done.5, bf16[528,768]{1,0:T(8,128)(2,1)S(1)} %collective-permute-done.7.refs_2_, bf16[528,768]{1,0:T(8,128)(2,1)S(1)} %copy-done.1, bf16[528,768]{1,0:T(8,128)(2,1)S(1)} %copy-done.3, ...), custom_call_target="tpu_custom_call" | custom-call | flops 805306368 | bytes 3932160 | tf_op jit(solution)/shard_map/far/pallas_call | solution.py:422
  137.1 21.6 %all_to_all.15 = f32[128,1,128]{2,1,0:T(1,128)S(1)} all-to-all(f32[128,1,128]{2,1,0:T(1,128)S(1)} %bitcast.7), channel_id=1, replica_groups={{0,8,16,24,32,40,48,56,64,72,80,88,96,104,112,120,128,136,144,152,160,1..., dimensions={0} | all-to-all | bytes 131072 | tf_op jit(solution)/shard_map/all_to_all | solution.py:59
  158.8 3.7 %collective-permute-start.9 = (f32[128,128]{1,0:T(8,128)S(1)}, f32[128,128]{1,0:T(8,128)S(1)}, u32[]{:S(2)}, u32[]{:S(2)}) collective-permute-start(f32[128,128]{1,0:T(8,128)S(1)} %bitcast.8), channel_id=1, source_target_pairs={{0,4},{1,5},{2,6},{3,7},{4,0},{5,1},{6,2},{7,3},{8,12},{9,13},{10,... | collective-permute-start | bytes 196616 | tf_op jit(solution)/shard_map/ppermute | solution.py:63
  162.5 0.5 answer.2.refs_0_
  163.0 0.4 collective-permute-done.9.values_ref
  163.4 1.0 answer.3
  (19 shorter events, 0.0 us)
Async XLA Ops:
  5.5 12.1 %copy-start.8 = (bf16[1024,768]{1,0:T(8,128)(2,1)S(1)}, bf16[1024,768]{1,0:T(8,128)(2,1)}, u32[]{:S(2)}) copy-start(bf16[1024,768]{1,0:T(8,128)(2,1)} %emb_ref.3) | copy-start | bytes 4718596
  5.5 12.1 %copy-start.13 = (s32[1024]{0:T(1024)S(1)}, s32[1024]{0:T(1024)}, u32[]{:S(2)}) copy-start(s32[1024]{0:T(1024)} %param.10) | copy-start | bytes 12292
  5.5 12.1 %copy-start.14 = (s32[1024]{0:T(1024)S(1)}, s32[1024]{0:T(1024)}, u32[]{:S(2)}) copy-start(s32[1024]{0:T(1024)} %param.11) | copy-start | bytes 12292
  5.5 12.1 %copy-start.16 = (s32[8,1024]{1,0:T(8,128)S(1)}, s32[8,1024]{1,0:T(8,128)}, u32[]{:S(2)}) copy-start(s32[8,1024]{1,0:T(8,128)} %get-tuple-element.24.info_ref) | copy-start | bytes 98308
  5.5 50.8 %all-to-all-start = ((bf16[32,200,128]{2,1,0:T(8,128)(2,1)}), bf16[32,200,128]{2,1,0:T(8,128)(2,1)S(1)}, u32[]{:S(2)}, u32[]{:S(2)}) async-start(bf16[32,200,128]{2,1,0:T(8,128)(2,1)} %get-tuple-element.25), calls=%async_computation | async-start | bytes 3276800 | tf_op jit(solution)/shard_map/all_to_all | solution.py:59
  20.0 4.5 %collective-permute-start = (bf16[32,200,128]{2,1,0:T(8,128)(2,1)S(1)}, bf16[32,200,128]{2,1,0:T(8,128)(2,1)}, u32[]{:S(2)}, u32[]{:S(2)}) collective-permute-start(bf16[32,200,128]{2,1,0:T(8,128)(2,1)S(1)} %hand.1), channel_id=1, source_target_pairs={{0,4},{1,5},{2,6},{3,7},{4,0},{5,1},{6,2},{7,3},{8,12},{9,13},{10,... | collective-permute-start | bytes 4915208 | tf_op jit(solution)/shard_map/ppermute | solution.py:63
  56.3 45.6 %all-to-all-start.1 = ((bf16[32,200,128]{2,1,0:T(8,128)(2,1)}), bf16[32,200,128]{2,1,0:T(8,128)(2,1)S(1)}, u32[]{:S(2)}, u32[]{:S(2)}) async-start(bf16[32,200,128]{2,1,0:T(8,128)(2,1)} %collective-permute-done), calls=%async_computation.1 | async-start | bytes 3276800 | tf_op jit(solution)/shard_map/all_to_all | solution.py:59
  63.4 19.4 %copy-start.15 = (s32[21]{0:T(128)S(1)}, s32[21]{0:T(128)}, u32[]{:S(2)}) copy-start(s32[21]{0:T(128)} %constant.29.clone.refs_0_) | copy-start | bytes 256
  64.2 24.6 %copy-start.9 = (bf16[528,768]{1,0:T(8,128)(2,1)}, bf16[528,768]{1,0:T(8,128)(2,1)S(1)}, u32[]{:S(2)}) copy-start(bf16[528,768]{1,0:T(8,128)(2,1)S(1)} %get-tuple-element.33.refs_1_.refs_3_.refs_5_) | copy-start | bytes 2433028
  64.2 24.6 %copy-start.10 = (bf16[528,768]{1,0:T(8,128)(2,1)}, bf16[528,768]{1,0:T(8,128)(2,1)S(1)}, u32[]{:S(2)}) copy-start(bf16[528,768]{1,0:T(8,128)(2,1)S(1)} %get-tuple-element.36.refs_3_.refs_6_) | copy-start | bytes 2433028
  64.2 15.9 %collective-permute-start.1 = (bf16[528,768]{1,0:T(8,128)(2,1)S(1)}, bf16[528,768]{1,0:T(8,128)(2,1)S(1)}, u32[]{:S(2)}, u32[]{:S(2)}) collective-permute-start(bf16[528,768]{1,0:T(8,128)(2,1)S(1)} %get-tuple-element.33.refs_1_.refs_3_.refs_5_), channel_id=1, source_target_pairs={{0,1},{4,68},{1,2},{5,69},{2,3},{6,70},{3,0},{7,71},{8,9},{12,76},... | collective-permute-start | bytes 2433032 | tf_op jit(solution)/shard_map/ppermute | solution.py:63
  65.6 14.6 %collective-permute-start.2 = (bf16[528,768]{1,0:T(8,128)(2,1)S(1)}, bf16[528,768]{1,0:T(8,128)(2,1)S(1)}, u32[]{:S(2)}, u32[]{:S(2)}) collective-permute-start(bf16[528,768]{1,0:T(8,128)(2,1)S(1)} %get-tuple-element.36.refs_3_.refs_6_), channel_id=1, source_target_pairs={{0,3},{4,196},{1,0},{5,197},{2,1},{6,198},{3,2},{7,199},{8,11},{12... | collective-permute-start | bytes 2433032 | tf_op jit(solution)/shard_map/ppermute | solution.py:63
  80.1 8.7 %copy-start.11 = (bf16[528,768]{1,0:T(8,128)(2,1)}, bf16[528,768]{1,0:T(8,128)(2,1)S(1)}, u32[]{:S(2)}) copy-start(bf16[528,768]{1,0:T(8,128)(2,1)S(1)} %collective-permute-done.1.refs_2_.refs_4_.refs_7_) | copy-start | bytes 2433028
  80.1 15.0 %collective-permute-start.3 = (bf16[528,768]{1,0:T(8,128)(2,1)S(1)}, bf16[528,768]{1,0:T(8,128)(2,1)S(1)}, u32[]{:S(2)}, u32[]{:S(2)}) collective-permute-start(bf16[528,768]{1,0:T(8,128)(2,1)S(1)} %collective-permute-done.1.refs_2_.refs_4_.refs_7_), channel_id=1, source_target_pairs={{0,1},{4,68},{1,2},{5,69},{2,3},{6,70},{3,0},{7,71},{8,9},{12,76},... | collective-permute-start | bytes 2433032 | tf_op jit(solution)/shard_map/ppermute | solution.py:63
  80.2 8.7 %copy-start.12 = (bf16[528,768]{1,0:T(8,128)(2,1)}, bf16[528,768]{1,0:T(8,128)(2,1)S(1)}, u32[]{:S(2)}) copy-start(bf16[528,768]{1,0:T(8,128)(2,1)S(1)} %collective-permute-done.2.refs_4_.refs_7_.refs_8_) | copy-start | bytes 2433028
  80.2 15.8 %collective-permute-start.4 = (bf16[528,768]{1,0:T(8,128)(2,1)S(1)}, bf16[528,768]{1,0:T(8,128)(2,1)S(1)}, u32[]{:S(2)}, u32[]{:S(2)}) collective-permute-start(bf16[528,768]{1,0:T(8,128)(2,1)S(1)} %collective-permute-done.2.refs_4_.refs_7_.refs_8_), channel_id=1, source_target_pairs={{0,3},{4,196},{1,0},{5,197},{2,1},{6,198},{3,2},{7,199},{8,11},{12... | collective-permute-start | bytes 2433032 | tf_op jit(solution)/shard_map/ppermute | solution.py:63
  88.8 16.2 %copy-start.19 = (s32[42]{0:T(128)S(1)}, s32[42]{0:T(128)}, u32[]{:S(2)}) copy-start(s32[42]{0:T(128)} %constant.31.clone) | copy-start | bytes 508
  88.9 16.2 %copy-start.20 = (s32[42]{0:T(128)S(1)}, s32[42]{0:T(128)}, u32[]{:S(2)}) copy-start(s32[42]{0:T(128)} %constant.30.clone) | copy-start | bytes 508
  95.1 0.9 copy-start.21
  96.0 0.9 copy-start.22
  102.3 3.3 %copy-start = (bf16[528,768]{1,0:T(8,128)(2,1)}, bf16[528,768]{1,0:T(8,128)(2,1)S(1)}, u32[]{:S(2)}) copy-start(bf16[528,768]{1,0:T(8,128)(2,1)S(1)} %get-tuple-element.31.refs_1_.refs_3_) | copy-start | bytes 2433028
  102.3 3.3 %copy-start.2 = (bf16[528,768]{1,0:T(8,128)(2,1)}, bf16[528,768]{1,0:T(8,128)(2,1)S(1)}, u32[]{:S(2)}) copy-start(bf16[528,768]{1,0:T(8,128)(2,1)S(1)} %get-tuple-element.32.refs_2_.refs_3_.refs_4_) | copy-start | bytes 2433028
  102.3 15.8 %collective-permute-start.5 = (bf16[528,768]{1,0:T(8,128)(2,1)S(1)}, bf16[528,768]{1,0:T(8,128)(2,1)S(1)}, u32[]{:S(2)}, u32[]{:S(2)}) collective-permute-start(bf16[528,768]{1,0:T(8,128)(2,1)S(1)} %get-tuple-element.31.refs_1_.refs_3_), channel_id=1, source_target_pairs={{0,1},{4,68},{1,2},{5,69},{2,3},{6,70},{3,0},{7,71},{8,9},{12,76},... | collective-permute-start | bytes 2433032 | tf_op jit(solution)/shard_map/ppermute | solution.py:63
  103.3 14.8 %collective-permute-start.6 = (bf16[528,768]{1,0:T(8,128)(2,1)S(1)}, bf16[528,768]{1,0:T(8,128)(2,1)}, u32[]{:S(2)}, u32[]{:S(2)}) collective-permute-start(bf16[528,768]{1,0:T(8,128)(2,1)S(1)} %get-tuple-element.32.refs_2_.refs_3_.refs_4_), channel_id=1, source_target_pairs={{0,3},{4,196},{1,0},{5,197},{2,1},{6,198},{3,2},{7,199},{8,11},{12... | collective-permute-start | bytes 2433032 | tf_op jit(solution)/shard_map/ppermute | solution.py:63
  105.6 14.0 %copy-start.17 = (s32[6]{0:T(128)S(1)}, s32[6]{0:T(128)}, u32[]{:S(2)}) copy-start(s32[6]{0:T(128)} %constant.34.clone) | copy-start | bytes 76
  105.6 14.0 %copy-start.18 = (s32[6]{0:T(128)S(1)}, s32[6]{0:T(128)}, u32[]{:S(2)}) copy-start(s32[6]{0:T(128)} %constant.33.clone) | copy-start | bytes 76
  118.1 1.6 copy-start.4
  118.1 13.3 %collective-permute-start.7 = (bf16[528,768]{1,0:T(8,128)(2,1)}, bf16[528,768]{1,0:T(8,128)(2,1)S(1)}, u32[]{:S(2)}, u32[]{:S(2)}) collective-permute-start(bf16[528,768]{1,0:T(8,128)(2,1)} %collective-permute-done.6.refs_4_), channel_id=1, source_target_pairs={{0,3},{4,196},{1,0},{5,197},{2,1},{6,198},{3,2},{7,199},{8,11},{12... | collective-permute-start | bytes 2433032 | tf_op jit(solution)/shard_map/ppermute | solution.py:63
  119.2 12.6 %collective-permute-start.8 = (bf16[528,768]{1,0:T(8,128)(2,1)S(1)}, bf16[528,768]{1,0:T(8,128)(2,1)S(1)}, u32[]{:S(2)}, u32[]{:S(2)}) collective-permute-start(bf16[528,768]{1,0:T(8,128)(2,1)S(1)} %collective-permute-done.5.refs_2_.refs_1_), channel_id=1, source_target_pairs={{0,1},{4,68},{1,2},{5,69},{2,3},{6,70},{3,0},{7,71},{8,9},{12,76},... | collective-permute-start | bytes 2433032 | tf_op jit(solution)/shard_map/ppermute | solution.py:63
  119.7 12.1 %copy-start.1 = (bf16[528,768]{1,0:T(8,128)(2,1)S(1)}, bf16[528,768]{1,0:T(8,128)(2,1)}, u32[]{:S(2)}) copy-start(bf16[528,768]{1,0:T(8,128)(2,1)} %copy-done) | copy-start | bytes 2433028
  119.7 12.1 %copy-start.3 = (bf16[528,768]{1,0:T(8,128)(2,1)S(1)}, bf16[528,768]{1,0:T(8,128)(2,1)}, u32[]{:S(2)}) copy-start(bf16[528,768]{1,0:T(8,128)(2,1)} %copy-done.2) | copy-start | bytes 2433028
  119.7 12.1 %copy-start.6 = (f32[64,128]{1,0:T(8,128)S(1)}, f32[64,128]{1,0:T(8,128)}, u32[]{:S(2)}) copy-start(f32[64,128]{1,0:T(8,128)} %own.1.refs_7_) | copy-start | bytes 98308
  131.8 1.1 copy-start.5
  132.9 0.8 copy-start.7
  158.8 4.6 %collective-permute-start.9 = (f32[128,128]{1,0:T(8,128)S(1)}, f32[128,128]{1,0:T(8,128)S(1)}, u32[]{:S(2)}, u32[]{:S(2)}) collective-permute-start(f32[128,128]{1,0:T(8,128)S(1)} %bitcast.8), channel_id=1, source_target_pairs={{0,4},{1,5},{2,6},{3,7},{4,0},{5,1},{6,2},{7,3},{8,12},{9,13},{10,... | collective-permute-start | bytes 196616 | tf_op jit(solution)/shard_map/ppermute | solution.py:63

commit v8 on v7

--- a/solution.py
+++ b/solution.py
@@ -23,10 +23,10 @@
 HALF_ROWS = 512
 ORDERS = 4096
 VMEM = 24 * 1024 * 1024
-FULL = 58 * 1024 * 1024
+FULL = 62 * 1024 * 1024
 PAIRS = 32 * 1024 * 1024
 OWN = 121 * 512 * 1024
-NEAR = 59 * 1024 * 1024
+NEAR = 233 * 256 * 1024
 
 
 def device(x, y, z, core):
@@ -122,7 +122,7 @@
 SPAN = 256
 
 
-def prep_kernel(emb_ref, ids_ref, order_ref, box_ref, info_ref, rows, out, in_sem, out_sems):
+def prep_kernel(emb_ref, ids_ref, order_ref, box_ref, info_ref, rows, in_sem):
     load = pltpu.make_async_copy(emb_ref, rows, in_sem)
     load.start()
     group = ids_ref[...] >> 1
@@ -146,17 +146,11 @@
     slot = slots_of(info, core, True)
     high, low = key_tables(info, ids_ref[...], order_ref[...], core, True)
     load.wait()
-    stores = []
     for n in range(PIECES):
         count = PIECE // CAP
         pick = onehot(slot, n * PIECE, PIECE)
         found = jnp.dot(pick, rows[...], preferred_element_type=jnp.float32)
-        fill_cells(out, n * count, count, found, high, low)
-        cells = pl.ds(n * count, count)
-        stores.append(pltpu.make_async_copy(out.at[cells], box_ref.at[cells], out_sems.at[n]))
-        stores[-1].start()
-    for store in stores:
-        store.wait()
+        fill_cells(box_ref, n * count, count, found, high, low)
 
 
 def prep(embeddings, ids, order):
@@ -167,13 +161,8 @@
             jax.ShapeDtypeStruct((8, ROWS), jnp.int32),
         ),
         in_specs=[pl.BlockSpec(memory_space=pl.ANY)] + [pl.BlockSpec(memory_space=pltpu.VMEM)] * 2,
-        out_specs=(pl.BlockSpec(memory_space=pl.ANY), pl.BlockSpec(memory_space=pltpu.VMEM)),
-        scratch_shapes=[
-            pltpu.VMEM((ROWS, D), jnp.bfloat16),
-            pltpu.VMEM((SOURCES, CELL, 128), jnp.bfloat16),
-            pltpu.SemaphoreType.DMA,
-            pltpu.SemaphoreType.DMA((PIECES,)),
-        ],
+        out_specs=tuple([pl.BlockSpec(memory_space=pltpu.VMEM)] * 2),
+        scratch_shapes=[pltpu.VMEM((ROWS, D), jnp.bfloat16), pltpu.SemaphoreType.DMA],
         compiler_params=pltpu.CompilerParams(vmem_limit_bytes=FULL),
         cost_estimate=cost(2 * ROWS * ROWS * D, 4 * ROWS * D),
         name="prep",
@@ -273,9 +262,9 @@
 
 
 def stage_of(pair):
-    if all(chunk == 0 and far < 2 for part, far, chunk in pair):
-        return 0
-    return 1 + max([far for part, far, chunk in pair if chunk == 1] + [0])
+    if all(chunk == 0 for part, far, chunk in pair):
+        return 0 if all(far < 2 for part, far, chunk in pair) else 2
+    return 1 + max(far for part, far, chunk in pair if chunk == 1)
 
 
 def three_parts(values):
@@ -315,14 +304,18 @@
             kcol[slot] = key
             ccol[slot] = cluster(key)
 
+    x, y, z, core = where_am_i()
+    here = jnp.where(core == 0, x, y)
+    table = jnp.where(here < 2, 0, 3 * n_tasks)
+
     def multiply(task, s):
-        a, b = tasks_ref[3 * task], tasks_ref[3 * task + 1]
+        a, b = tasks_ref[table + 3 * task], tasks_ref[table + 3 * task + 1]
         s[...] = across(rows[a, :HALF_ROWS], rows[b, :HALF_ROWS])
 
     step = 16
 
     def reduce(task, s):
-        a, b, sink = tasks_ref[3 * task], tasks_ref[3 * task + 1], tasks_ref[3 * task + 2]
+        a, b, sink = [tasks_ref[table + 3 * task + n] for n in range(3)]
         kb, cb = krow[b], crow[b]
         for row in range(0, HALF_ROWS, step):
             ka = kcol[a, row : row + step].reshape(step // 8, 8, 128)
@@ -385,8 +378,6 @@
     if not befores:
         out_ref[...] = values
         return
-    x, y, z, core = where_am_i()
-    here = jnp.where(core == 0, x, y)
     row = lax.broadcasted_iota(jnp.int32, (CHIPS, 2 * SOURCES), 0)
     column = lax.broadcasted_iota(jnp.int32, (CHIPS, 2 * SOURCES), 1)
     source = row & (SOURCES - 1)
@@ -400,7 +391,7 @@
     )
 
 
-def similar(hold, low, high, ring_place, befores, name, limit, start):
+def similar(hold, low, high, befores, name, limit, start):
     first_use = {}
     for number, pairs in enumerate(zip(low, high)):
         for pair in pairs:
@@ -416,9 +407,7 @@
             [(place[a], place[b], spare if a == b else place[b]) for a, b in pairs], np.int32
         ).reshape(-1)
 
-    tasks = jnp.asarray(table(low))
-    if low != high:
-        tasks = jnp.where(ring_place < 2, tasks, jnp.asarray(table(high)))
+    tasks = jnp.asarray(np.concatenate([table(low), table(high)]))
     return pl.pallas_call(
         functools.partial(similar_kernel, blocks, early, len(low), len(befores)),
         out_shape=jax.ShapeDtypeStruct((CHIPS if befores else 2 * SOURCES, 128), jnp.float32),
@@ -480,8 +469,6 @@
 
 
 def local(embeddings, cluster_ids, member_order):
-    x, y, z, core = where_am_i()
-    ring_place = jnp.where(core == 0, x, y)
     ids, order = cluster_ids.reshape(1, ROWS), member_order.reshape(1, ROWS)
 
     box, info = prep(embeddings, ids, order)
@@ -511,7 +498,7 @@
                 low.append(one)
                 high.append(other)
         limit, start = ((PAIRS, 0), (OWN, 1), (NEAR, 1), (PAIRS, 0))[stage]
-        return similar(hold, low, high, ring_place, befores, name, limit, start)
+        return similar(hold, low, high, befores, name, limit, start)
 
     own1 = ring_blocks(0, 0, open_cells(chunk1, True))
     near1 = ring_blocks(1, 0, onward(own1))

time: 165 us -> 164 us (level)
    unnamed x46 -> x40, local copies, waits for them, and re-layouts: 3.77 us -> 4.07 us
  transfers between devices with their start and end apart: 12 -> 12, of which waited for: 7 -> 6; matrix products, arithmetic and copies ran while one was open for 0% -> 0% of each run, Pallas kernels for 21% -> 20%
where the time goes in v8:
time: 164 us
  waiting for transfers between devices  59.6 us (36%)
  Pallas kernels  43.2 us (26%)
  starting transfers between devices  34.6 us (21%)
  blocking collectives  22 us (13%)
  local copies, waits for them, and re-layouts  4.07 us (2%)
    all_to_all x2, waiting for transfers between devices, exchange(): lax.all_to_all(rows, AXES, split_axis=0, concat_axis=0, tiled=True, axis_...  36.6 us
    pallas_call x4, Pallas kernels, similar(): pl.pallas_call(functools.partial(similar_kernel, blocks, early, len(low),...  33 us
    ppermute x10, waiting for transfers between devices, send(): return lax.ppermute(rows, AXES, pairs)  22.9 us
    all_to_all x1, blocking collectives, exchange(): lax.all_to_all(rows, AXES, split_axis=0, concat_axis=0, tiled=True, axis_...  22 us
    all_to_all x2, starting transfers between devices, exchange(): lax.all_to_all(rows, AXES, split_axis=0, concat_axis=0, tiled=True, axis_...  19.1 us
    ppermute x10, starting transfers between devices, send(): return lax.ppermute(rows, AXES, pairs)  15.5 us
    pallas_call x1, Pallas kernels, prep(): pl.pallas_call(prep_kernel, out_shape=(jax.ShapeDtypeStruct((SOURCES, CEL...  5.09 us
    unnamed x40, local copies, waits for them, and re-layouts  4.07 us
  transfers between devices with their start and end apart: 12, of which 6 were waited for; matrix products, arithmetic and copies ran while one was open for 0% of the time, Pallas kernels for 20%

profile of v8, /device:TPU:1, one launch (start us, length us, event | category | flops | bytes accessed | tf_op | source)
XLA Modules:
  0.0 163.7 jit_solution(3686817417228731089)
XLA Ops:
  0.0 5.1 %prep.1 = (bf16[32,200,128]{2,1,0:T(8,128)(2,1)}, s32[8,1024]{1,0:T(8,128)}) custom-call(bf16[1024,768]{1,0:T(8,128)(2,1)} %emb_ref.3, s32[1,1024]{1,0:T(1,128)} %bitcast.10, s32[1,1024]{1,0:T(1,128)} %bitcast.12), custom_call_target="tpu_custom_call" | custom-call | flops 1610612736 | bytes 3145728 | tf_op jit(solution)/shard_map/prep/pallas_call | solution.py:157
  5.1 0.0 copy-start.9
  5.1 0.0 copy-start.14
  5.1 0.0 copy-start.15
  5.1 0.0 copy-start.17
  5.1 12.0 %all-to-all-start = ((bf16[32,200,128]{2,1,0:T(8,128)(2,1)}), bf16[32,200,128]{2,1,0:T(8,128)(2,1)S(1)}, u32[]{:S(2)}, u32[]{:S(2)}) async-start(bf16[32,200,128]{2,1,0:T(8,128)(2,1)} %get-tuple-element.25), calls=%async_computation | async-start | bytes 3276800 | tf_op jit(solution)/shard_map/all_to_all | solution.py:59
  17.2 0.0 copy-done.9
  17.2 0.0 copy-done.14
  17.2 0.0 copy-done.15
  17.2 0.0 copy-done.17
  17.2 2.4 %hand.1 = bf16[32,200,128]{2,1,0:T(8,128)(2,1)S(1)} custom-call(bf16[1024,768]{1,0:T(8,128)(2,1)S(1)} %copy-done.9, s32[8,1024]{1,0:T(8,128)S(1)} %copy-done.17, s32[1,1024]{1,0:T(1,128)S(1)} %bitcast.11, s32[1,1024]{1,0:T(1,128)S(1)} %bitcast.13), custom_call_target="tpu_custom_call" | custom-call | flops 1610612736 | bytes 3145728 | tf_op jit(solution)/shard_map/hand/pallas_call | solution.py:181
  19.7 1.2 collective-permute-start
  20.9 3.1 %collective-permute-done = bf16[32,200,128]{2,1,0:T(8,128)(2,1)S(1)} collective-permute-done((bf16[32,200,128]{2,1,0:T(8,128)(2,1)S(1)}, bf16[32,200,128]{2,1,0:T(8,128)(2,1)S(1)}, u32[]{:S(2)}, u32[]{:S(2)}) %collective-permute-start) | collective-permute-done | bytes 1638432 | tf_op jit(solution)/shard_map/ppermute | solution.py:63
  24.0 1.2 copy-done.18
  25.2 30.7 %all-to-all-done.cells_ref = bf16[32,200,128]{2,1,0:T(8,128)(2,1)S(1)} async-done(((bf16[32,200,128]{2,1,0:T(8,128)(2,1)}), bf16[32,200,128]{2,1,0:T(8,128)(2,1)S(1)}, u32[]{:S(2)}, u32[]{:S(2)}) %all-to-all-start) | async-done | bytes 1638432 | tf_op jit(solution)/shard_map/all_to_all | solution.py:59
  55.9 7.1 %all-to-all-start.1 = ((bf16[32,200,128]{2,1,0:T(8,128)(2,1)}), bf16[32,200,128]{2,1,0:T(8,128)(2,1)S(1)}, u32[]{:S(2)}, u32[]{:S(2)}) async-start(bf16[32,200,128]{2,1,0:T(8,128)(2,1)} %copy-done.18), calls=%async_computation.1 | async-start | bytes 3276800 | tf_op jit(solution)/shard_map/all_to_all | solution.py:59
  63.0 0.0 copy-start.16
  63.0 0.8 settle.1
  63.8 0.0 copy-start.10
  63.8 0.0 copy-start.11
  63.8 1.4 collective-permute-start.1
  65.2 1.5 collective-permute-start.2
  66.7 13.1 %collective-permute-done.1.refs_2_.refs_4_.refs_7_ = bf16[528,768]{1,0:T(8,128)(2,1)S(1)} collective-permute-done((bf16[528,768]{1,0:T(8,128)(2,1)S(1)}, bf16[528,768]{1,0:T(8,128)(2,1)S(1)}, u32[]{:S(2)}, u32[]{:S(2)}) %collective-permute-start.1) | collective-permute-done | bytes 811040 | tf_op jit(solution)/shard_map/ppermute | solution.py:63
  79.8 0.0 collective-permute-start.3
  79.8 0.0 collective-permute-done.2.refs_4_.refs_7_.refs_8_
  79.8 0.0 copy-start.13
  79.8 2.7 %collective-permute-start.4 = (bf16[528,768]{1,0:T(8,128)(2,1)S(1)}, bf16[528,768]{1,0:T(8,128)(2,1)}, u32[]{:S(2)}, u32[]{:S(2)}) collective-permute-start(bf16[528,768]{1,0:T(8,128)(2,1)S(1)} %collective-permute-done.2.refs_4_.refs_7_.refs_8_), channel_id=1, source_target_pairs={{0,3},{4,196},{1,0},{5,197},{2,1},{6,198},{3,2},{7,199},{8,11},{12... | collective-permute-start | bytes 2433032 | tf_op jit(solution)/shard_map/ppermute | solution.py:63
  82.5 0.0 copy-done.16
  82.5 6.0 %first.1.refs_6_ = f32[64,128]{1,0:T(8,128)S(1)} custom-call(s32[42]{0:T(128)S(1)} %copy-done.16, bf16[528,768]{1,0:T(8,128)(2,1)S(1)} %get-tuple-element.33.refs_1_.refs_3_.refs_5_, bf16[528,768]{1,0:T(8,128)(2,1)S(1)} %collective-permute-done.1.refs_2_.refs_4_.refs_7_, bf16[528,768]{1,0:T(8,128)(2,1)S(1)} %get-tuple-element.36.refs_3_.refs_6_, ...), custom_call_target="tpu_custom_call" | custom-call | flops 2818572288 | bytes 3145728 | tf_op jit(solution)/shard_map/first/pallas_call | solution.py:411
  88.4 0.0 copy-done.10
  88.4 0.0 copy-done.11
  88.5 0.0 copy-done.12
  88.5 0.0 copy-done.13
  88.5 6.3 %collective-permute-done.3.refs_5_.refs_10_ = bf16[528,768]{1,0:T(8,128)(2,1)S(1)} collective-permute-done((bf16[528,768]{1,0:T(8,128)(2,1)S(1)}, bf16[528,768]{1,0:T(8,128)(2,1)S(1)}, u32[]{:S(2)}, u32[]{:S(2)}) %collective-permute-start.3) | collective-permute-done | bytes 811040 | tf_op jit(solution)/shard_map/ppermute | solution.py:63
  94.8 0.9 copy-done.19
  95.6 0.0 collective-permute-done.4.refs_8_.refs_9_
  95.6 5.9 %all-to-all-done.1.cells_ref = bf16[32,200,128]{2,1,0:T(8,128)(2,1)S(1)} async-done(((bf16[32,200,128]{2,1,0:T(8,128)(2,1)}), bf16[32,200,128]{2,1,0:T(8,128)(2,1)S(1)}, u32[]{:S(2)}, u32[]{:S(2)}) %all-to-all-start.1) | async-done | bytes 1638432 | tf_op jit(solution)/shard_map/all_to_all | solution.py:59
  101.6 0.4 split.1
  101.9 0.0 copy-start
  101.9 0.0 copy-start.2
  101.9 1.0 collective-permute-start.5
  102.9 1.7 %collective-permute-start.6 = (bf16[528,768]{1,0:T(8,128)(2,1)S(1)}, bf16[528,768]{1,0:T(8,128)(2,1)}, u32[]{:S(2)}, u32[]{:S(2)}) collective-permute-start(bf16[528,768]{1,0:T(8,128)(2,1)S(1)} %get-tuple-element.32.refs_2_.refs_3_.refs_4_), channel_id=1, source_target_pairs={{0,3},{4,196},{1,0},{5,197},{2,1},{6,198},{3,2},{7,199},{8,11},{12... | collective-permute-start | bytes 2433032 | tf_op jit(solution)/shard_map/ppermute | solution.py:63
  104.7 0.0 copy-done
  104.7 0.0 copy-done.2
  104.7 11.1 %own.1.refs_7_ = f32[64,128]{1,0:T(8,128)} custom-call(s32[72]{0:T(128)} %constant.9.clone.refs_0_, bf16[528,768]{1,0:T(8,128)(2,1)} %copy-done, bf16[528,768]{1,0:T(8,128)(2,1)} %copy-done.2, bf16[528,768]{1,0:T(8,128)(2,1)} %copy-done.10, bf16[528,768]{1,0:T(8,128)(2,1)} %copy-done.12, bf16[528,768]{1,0:T(8,128)(2,1)} %copy-done.19, ...), custom_call_target="tpu_custom_call" | custom-call | flops 4831838208 | bytes 6291456 | tf_op jit(solution)/shard_map/own/pallas_call | solution.py:411
  115.8 0.0 copy-start.1
  115.9 0.0 copy-start.3
  115.9 0.0 copy-start.8
  115.9 0.0 collective-permute-done.5.refs_2_.refs_1_
  115.9 0.0 collective-permute-done.6.refs_4_
  115.9 1.4 collective-permute-start.7
  117.3 0.2 collective-permute-start.8
  117.5 0.0 copy-done.4
  117.5 12.5 %near.1.refs_8_ = f32[64,128]{1,0:T(8,128)} custom-call(s32[78]{0:T(128)} %constant.10.clone.refs_0_, bf16[528,768]{1,0:T(8,128)(2,1)} %copy-done, bf16[528,768]{1,0:T(8,128)(2,1)} %copy-done.4, bf16[528,768]{1,0:T(8,128)(2,1)} %copy-done.2, bf16[528,768]{1,0:T(8,128)(2,1)} %collective-permute-done.6.refs_4_, bf16[528,768]{1,0:T(8,128)(2,1)} %copy-done.10, ...), custom_call_target="tpu_custom_call" | custom-call | flops 5234491392 | bytes 7864320 | tf_op jit(solution)/shard_map/near/pallas_call | solution.py:411
  129.9 0.0 collective-permute-done.7.refs_2_
  130.0 0.0 collective-permute-done.8.refs_5_
  130.0 1.1 copy-done.5
  131.2 0.8 copy-done.7
  131.9 3.4 %far.1 = f32[128,128]{1,0:T(8,128)S(1)} custom-call(s32[12]{0:T(128)S(1)} %copy-done.8, bf16[528,768]{1,0:T(8,128)(2,1)S(1)} %copy-done.5, bf16[528,768]{1,0:T(8,128)(2,1)S(1)} %collective-permute-done.7.refs_2_, bf16[528,768]{1,0:T(8,128)(2,1)S(1)} %copy-done.1, bf16[528,768]{1,0:T(8,128)(2,1)S(1)} %copy-done.3, ...), custom_call_target="tpu_custom_call" | custom-call | flops 805306368 | bytes 3932160 | tf_op jit(solution)/shard_map/far/pallas_call | solution.py:411
  135.4 22.0 %all_to_all.15 = f32[128,1,128]{2,1,0:T(1,128)S(1)} all-to-all(f32[128,1,128]{2,1,0:T(1,128)S(1)} %bitcast.7), channel_id=1, replica_groups={{0,8,16,24,32,40,48,56,64,72,80,88,96,104,112,120,128,136,144,152,160,1..., dimensions={0} | all-to-all | bytes 131072 | tf_op jit(solution)/shard_map/all_to_all | solution.py:59
  157.3 4.4 %collective-permute-start.9 = (f32[128,128]{1,0:T(8,128)S(1)}, f32[128,128]{1,0:T(8,128)S(1)}, u32[]{:S(2)}, u32[]{:S(2)}) collective-permute-start(f32[128,128]{1,0:T(8,128)S(1)} %bitcast.8), channel_id=1, source_target_pairs={{0,4},{1,5},{2,6},{3,7},{4,0},{5,1},{6,2},{7,3},{8,12},{9,13},{10,... | collective-permute-start | bytes 196616 | tf_op jit(solution)/shard_map/ppermute | solution.py:63
  161.8 0.5 answer.2.refs_0_
  162.2 0.4 collective-permute-done.9.values_ref
  162.7 1.0 answer.3
  (11 shorter events, 0.0 us)
Async XLA Ops:
  5.1 12.1 %copy-start.9 = (bf16[1024,768]{1,0:T(8,128)(2,1)S(1)}, bf16[1024,768]{1,0:T(8,128)(2,1)}, u32[]{:S(2)}) copy-start(bf16[1024,768]{1,0:T(8,128)(2,1)} %emb_ref.3) | copy-start | bytes 4718596
  5.1 12.1 %copy-start.14 = (s32[1024]{0:T(1024)S(1)}, s32[1024]{0:T(1024)}, u32[]{:S(2)}) copy-start(s32[1024]{0:T(1024)} %param.8) | copy-start | bytes 12292
  5.1 12.1 %copy-start.15 = (s32[1024]{0:T(1024)S(1)}, s32[1024]{0:T(1024)}, u32[]{:S(2)}) copy-start(s32[1024]{0:T(1024)} %param.9) | copy-start | bytes 12292
  5.1 12.1 %copy-start.17 = (s32[8,1024]{1,0:T(8,128)S(1)}, s32[8,1024]{1,0:T(8,128)}, u32[]{:S(2)}) copy-start(s32[8,1024]{1,0:T(8,128)} %get-tuple-element.24.info_ref) | copy-start | bytes 98308
  5.1 50.8 %all-to-all-start = ((bf16[32,200,128]{2,1,0:T(8,128)(2,1)}), bf16[32,200,128]{2,1,0:T(8,128)(2,1)S(1)}, u32[]{:S(2)}, u32[]{:S(2)}) async-start(bf16[32,200,128]{2,1,0:T(8,128)(2,1)} %get-tuple-element.25), calls=%async_computation | async-start | bytes 3276800 | tf_op jit(solution)/shard_map/all_to_all | solution.py:59
  19.7 4.3 %collective-permute-start = (bf16[32,200,128]{2,1,0:T(8,128)(2,1)S(1)}, bf16[32,200,128]{2,1,0:T(8,128)(2,1)S(1)}, u32[]{:S(2)}, u32[]{:S(2)}) collective-permute-start(bf16[32,200,128]{2,1,0:T(8,128)(2,1)S(1)} %hand.1), channel_id=1, source_target_pairs={{0,4},{1,5},{2,6},{3,7},{4,0},{5,1},{6,2},{7,3},{8,12},{9,13},{10,... | collective-permute-start | bytes 4915208 | tf_op jit(solution)/shard_map/ppermute | solution.py:63
  24.0 1.2 copy-start.18
  55.9 45.6 %all-to-all-start.1 = ((bf16[32,200,128]{2,1,0:T(8,128)(2,1)}), bf16[32,200,128]{2,1,0:T(8,128)(2,1)S(1)}, u32[]{:S(2)}, u32[]{:S(2)}) async-start(bf16[32,200,128]{2,1,0:T(8,128)(2,1)} %copy-done.18), calls=%async_computation.1 | async-start | bytes 3276800 | tf_op jit(solution)/shard_map/all_to_all | solution.py:59
  63.0 19.4 %copy-start.16 = (s32[42]{0:T(128)S(1)}, s32[42]{0:T(128)}, u32[]{:S(2)}) copy-start(s32[42]{0:T(128)} %constant.8.clone.refs_0_) | copy-start | bytes 508
  63.8 24.6 %copy-start.10 = (bf16[528,768]{1,0:T(8,128)(2,1)}, bf16[528,768]{1,0:T(8,128)(2,1)S(1)}, u32[]{:S(2)}) copy-start(bf16[528,768]{1,0:T(8,128)(2,1)S(1)} %get-tuple-element.33.refs_1_.refs_3_.refs_5_) | copy-start | bytes 2433028
  63.8 24.6 %copy-start.11 = (bf16[528,768]{1,0:T(8,128)(2,1)}, bf16[528,768]{1,0:T(8,128)(2,1)S(1)}, u32[]{:S(2)}) copy-start(bf16[528,768]{1,0:T(8,128)(2,1)S(1)} %get-tuple-element.36.refs_3_.refs_6_) | copy-start | bytes 2433028
  63.8 15.9 %collective-permute-start.1 = (bf16[528,768]{1,0:T(8,128)(2,1)S(1)}, bf16[528,768]{1,0:T(8,128)(2,1)S(1)}, u32[]{:S(2)}, u32[]{:S(2)}) collective-permute-start(bf16[528,768]{1,0:T(8,128)(2,1)S(1)} %get-tuple-element.33.refs_1_.refs_3_.refs_5_), channel_id=1, source_target_pairs={{0,1},{4,68},{1,2},{5,69},{2,3},{6,70},{3,0},{7,71},{8,9},{12,76},... | collective-permute-start | bytes 2433032 | tf_op jit(solution)/shard_map/ppermute | solution.py:63
  65.2 14.6 %collective-permute-start.2 = (bf16[528,768]{1,0:T(8,128)(2,1)S(1)}, bf16[528,768]{1,0:T(8,128)(2,1)S(1)}, u32[]{:S(2)}, u32[]{:S(2)}) collective-permute-start(bf16[528,768]{1,0:T(8,128)(2,1)S(1)} %get-tuple-element.36.refs_3_.refs_6_), channel_id=1, source_target_pairs={{0,3},{4,196},{1,0},{5,197},{2,1},{6,198},{3,2},{7,199},{8,11},{12... | collective-permute-start | bytes 2433032 | tf_op jit(solution)/shard_map/ppermute | solution.py:63
  79.8 8.7 %copy-start.12 = (bf16[528,768]{1,0:T(8,128)(2,1)}, bf16[528,768]{1,0:T(8,128)(2,1)S(1)}, u32[]{:S(2)}) copy-start(bf16[528,768]{1,0:T(8,128)(2,1)S(1)} %collective-permute-done.1.refs_2_.refs_4_.refs_7_) | copy-start | bytes 2433028
  79.8 15.0 %collective-permute-start.3 = (bf16[528,768]{1,0:T(8,128)(2,1)S(1)}, bf16[528,768]{1,0:T(8,128)(2,1)S(1)}, u32[]{:S(2)}, u32[]{:S(2)}) collective-permute-start(bf16[528,768]{1,0:T(8,128)(2,1)S(1)} %collective-permute-done.1.refs_2_.refs_4_.refs_7_), channel_id=1, source_target_pairs={{0,1},{4,68},{1,2},{5,69},{2,3},{6,70},{3,0},{7,71},{8,9},{12,76},... | collective-permute-start | bytes 2433032 | tf_op jit(solution)/shard_map/ppermute | solution.py:63
  79.8 8.7 %copy-start.13 = (bf16[528,768]{1,0:T(8,128)(2,1)}, bf16[528,768]{1,0:T(8,128)(2,1)S(1)}, u32[]{:S(2)}) copy-start(bf16[528,768]{1,0:T(8,128)(2,1)S(1)} %collective-permute-done.2.refs_4_.refs_7_.refs_8_) | copy-start | bytes 2433028
  79.8 15.8 %collective-permute-start.4 = (bf16[528,768]{1,0:T(8,128)(2,1)S(1)}, bf16[528,768]{1,0:T(8,128)(2,1)}, u32[]{:S(2)}, u32[]{:S(2)}) collective-permute-start(bf16[528,768]{1,0:T(8,128)(2,1)S(1)} %collective-permute-done.2.refs_4_.refs_7_.refs_8_), channel_id=1, source_target_pairs={{0,3},{4,196},{1,0},{5,197},{2,1},{6,198},{3,2},{7,199},{8,11},{12... | collective-permute-start | bytes 2433032 | tf_op jit(solution)/shard_map/ppermute | solution.py:63
  94.8 0.9 copy-start.19
  101.9 2.8 %copy-start = (bf16[528,768]{1,0:T(8,128)(2,1)}, bf16[528,768]{1,0:T(8,128)(2,1)S(1)}, u32[]{:S(2)}) copy-start(bf16[528,768]{1,0:T(8,128)(2,1)S(1)} %get-tuple-element.31.refs_1_.refs_3_) | copy-start | bytes 2433028
  101.9 2.8 %copy-start.2 = (bf16[528,768]{1,0:T(8,128)(2,1)}, bf16[528,768]{1,0:T(8,128)(2,1)S(1)}, u32[]{:S(2)}) copy-start(bf16[528,768]{1,0:T(8,128)(2,1)S(1)} %get-tuple-element.32.refs_2_.refs_3_.refs_4_) | copy-start | bytes 2433028
  101.9 14.0 %collective-permute-start.5 = (bf16[528,768]{1,0:T(8,128)(2,1)S(1)}, bf16[528,768]{1,0:T(8,128)(2,1)S(1)}, u32[]{:S(2)}, u32[]{:S(2)}) collective-permute-start(bf16[528,768]{1,0:T(8,128)(2,1)S(1)} %get-tuple-element.31.refs_1_.refs_3_), channel_id=1, source_target_pairs={{0,1},{4,68},{1,2},{5,69},{2,3},{6,70},{3,0},{7,71},{8,9},{12,76},... | collective-permute-start | bytes 2433032 | tf_op jit(solution)/shard_map/ppermute | solution.py:63
  102.9 13.0 %collective-permute-start.6 = (bf16[528,768]{1,0:T(8,128)(2,1)S(1)}, bf16[528,768]{1,0:T(8,128)(2,1)}, u32[]{:S(2)}, u32[]{:S(2)}) collective-permute-start(bf16[528,768]{1,0:T(8,128)(2,1)S(1)} %get-tuple-element.32.refs_2_.refs_3_.refs_4_), channel_id=1, source_target_pairs={{0,3},{4,196},{1,0},{5,197},{2,1},{6,198},{3,2},{7,199},{8,11},{12... | collective-permute-start | bytes 2433032 | tf_op jit(solution)/shard_map/ppermute | solution.py:63
  115.8 14.1 %copy-start.1 = (bf16[528,768]{1,0:T(8,128)(2,1)S(1)}, bf16[528,768]{1,0:T(8,128)(2,1)}, u32[]{:S(2)}) copy-start(bf16[528,768]{1,0:T(8,128)(2,1)} %copy-done) | copy-start | bytes 2433028
  115.9 14.1 %copy-start.3 = (bf16[528,768]{1,0:T(8,128)(2,1)S(1)}, bf16[528,768]{1,0:T(8,128)(2,1)}, u32[]{:S(2)}) copy-start(bf16[528,768]{1,0:T(8,128)(2,1)} %copy-done.2) | copy-start | bytes 2433028
  115.9 14.1 %copy-start.6 = (f32[64,128]{1,0:T(8,128)S(1)}, f32[64,128]{1,0:T(8,128)}, u32[]{:S(2)}) copy-start(f32[64,128]{1,0:T(8,128)} %own.1.refs_7_) | copy-start | bytes 98308
  115.9 14.1 %copy-start.8 = (s32[12]{0:T(128)S(1)}, s32[12]{0:T(128)}, u32[]{:S(2)}) copy-start(s32[12]{0:T(128)} %constant.11.clone.refs_0_) | copy-start | bytes 148
  115.9 1.6 copy-start.4
  115.9 14.0 %collective-permute-start.7 = (bf16[528,768]{1,0:T(8,128)(2,1)}, bf16[528,768]{1,0:T(8,128)(2,1)S(1)}, u32[]{:S(2)}, u32[]{:S(2)}) collective-permute-start(bf16[528,768]{1,0:T(8,128)(2,1)} %collective-permute-done.6.refs_4_), channel_id=1, source_target_pairs={{0,3},{4,196},{1,0},{5,197},{2,1},{6,198},{3,2},{7,199},{8,11},{12... | collective-permute-start | bytes 2433032 | tf_op jit(solution)/shard_map/ppermute | solution.py:63
  117.3 12.7 %collective-permute-start.8 = (bf16[528,768]{1,0:T(8,128)(2,1)S(1)}, bf16[528,768]{1,0:T(8,128)(2,1)S(1)}, u32[]{:S(2)}, u32[]{:S(2)}) collective-permute-start(bf16[528,768]{1,0:T(8,128)(2,1)S(1)} %collective-permute-done.5.refs_2_.refs_1_), channel_id=1, source_target_pairs={{0,1},{4,68},{1,2},{5,69},{2,3},{6,70},{3,0},{7,71},{8,9},{12,76},... | collective-permute-start | bytes 2433032 | tf_op jit(solution)/shard_map/ppermute | solution.py:63
  130.0 1.1 copy-start.5
  131.2 0.8 copy-start.7
  157.3 5.3 %collective-permute-start.9 = (f32[128,128]{1,0:T(8,128)S(1)}, f32[128,128]{1,0:T(8,128)S(1)}, u32[]{:S(2)}, u32[]{:S(2)}) collective-permute-start(f32[128,128]{1,0:T(8,128)S(1)} %bitcast.8), channel_id=1, source_target_pairs={{0,4},{1,5},{2,6},{3,7},{4,0},{5,1},{6,2},{7,3},{8,12},{9,13},{10,... | collective-permute-start | bytes 196616 | tf_op jit(solution)/shard_map/ppermute | solution.py:63

commit v9 on v8

--- a/solution.py
+++ b/solution.py
@@ -253,7 +253,7 @@
     pairs.append((("P", 1, 0), ("M", 2, 0)))
     pairs.append((("P", 1, 1), ("M", 2, 0)))
     pairs.append((("P", 2, 0), ("M", 1, 1)))
-    pairs.append((("P", 1, 1), ("M", 2, 1)))
+    pairs.append((("P", 2, 1), ("M", 1, 1)))
     by_place = [
         ((("P", 0, 0), ("P", 2, 0)), (("M", 0, 0), ("M", 2, 0))),
         ((("M", 0, 1), ("M", 2, 1)), (("P", 0, 1), ("P", 2, 1))),
@@ -295,6 +295,8 @@
     def arrive(slots):
         for slot in slots:
             copies[slot].wait()
+
+    def make_keys(slots):
         for slot in slots:
             parts = rows[slot, HALF_ROWS:, :HALF_ROWS].astype(jnp.float32)
             key = 128.0 * parts[0:1] + parts[1:2]
@@ -312,7 +314,7 @@
         a, b = tasks_ref[table + 3 * task], tasks_ref[table + 3 * task + 1]
         s[...] = across(rows[a, :HALF_ROWS], rows[b, :HALF_ROWS])
 
-    step = 16
+    step = 8
 
     def reduce(task, s):
         a, b, sink = [tasks_ref[table + 3 * task + n] for n in range(3)]
@@ -341,13 +343,17 @@
     start, early = early
     arrive(range(early))
     multiply(0, s0)
+    make_keys(range(early))
     if start:
         lax.fori_loop(0, start, two, 0)
     arrive(range(early, n_blocks))
     if turns > start:
+        make_keys(range(early, n_blocks))
         lax.fori_loop(start, turns, two, 0)
     if n_tasks % 2 == 0:
         multiply(n_tasks - 1, s1)
+    if turns == start:
+        make_keys(range(early, n_blocks))
     reduce(2 * turns, s0)
     if n_tasks % 2 == 0:
         reduce(n_tasks - 1, s1)

time: 164 us -> 163 us (level)
  blocking collectives: 22 us -> 19.7 us
    all_to_all x1, blocking collectives: 22 us -> 19.7 us  [exchange(): lax.all_to_all(rows, AXES, split_axis=0, concat_axis=0, tiled=True, axis_...]
where the time goes in v9:
time: 163 us; the launch traced here: 162 us
  waiting for transfers between devices  59.7 us (37%)
  Pallas kernels  42.6 us (26%)
  starting transfers between devices  35.9 us (22%)
  blocking collectives  19.7 us (12%)
  local copies, waits for them, and re-layouts  4.07 us (2%)
    all_to_all x2, waiting for transfers between devices, exchange(): lax.all_to_all(rows, AXES, split_axis=0, concat_axis=0, tiled=True, axis_...  36.6 us
    pallas_call x4, Pallas kernels, similar(): pl.pallas_call(functools.partial(similar_kernel, blocks, early, len(low),...  32.5 us
    ppermute x10, waiting for transfers between devices, send(): return lax.ppermute(rows, AXES, pairs)  23 us
    all_to_all x1, blocking collectives, exchange(): lax.all_to_all(rows, AXES, split_axis=0, concat_axis=0, tiled=True, axis_...  19.7 us
    all_to_all x2, starting transfers between devices, exchange(): lax.all_to_all(rows, AXES, split_axis=0, concat_axis=0, tiled=True, axis_...  19.1 us
    ppermute x10, starting transfers between devices, send(): return lax.ppermute(rows, AXES, pairs)  16.8 us
    pallas_call x1, Pallas kernels, prep(): pl.pallas_call(prep_kernel, out_shape=(jax.ShapeDtypeStruct((SOURCES, CEL...  5.09 us
    unnamed x40, local copies, waits for them, and re-layouts  4.07 us
  transfers between devices with their start and end apart: 12, of which 6 were waited for; matrix products, arithmetic and copies ran while one was open for 0% of the time, Pallas kernels for 20%

profile of v9, /device:TPU:1, one launch (start us, length us, event | category | flops | bytes accessed | tf_op | source)
XLA Modules:
  0.0 162.3 jit_solution(1523016319014054281)
XLA Ops:
  0.0 5.1 %prep.1 = (bf16[32,200,128]{2,1,0:T(8,128)(2,1)}, s32[8,1024]{1,0:T(8,128)}) custom-call(bf16[1024,768]{1,0:T(8,128)(2,1)} %emb_ref.3, s32[1,1024]{1,0:T(1,128)} %bitcast.10, s32[1,1024]{1,0:T(1,128)} %bitcast.12), custom_call_target="tpu_custom_call" | custom-call | flops 1610612736 | bytes 3145728 | tf_op jit(solution)/shard_map/prep/pallas_call | solution.py:157
  5.1 0.0 copy-start.9
  5.1 0.0 copy-start.14
  5.1 0.0 copy-start.15
  5.1 0.0 copy-start.17
  5.1 12.0 %all-to-all-start = ((bf16[32,200,128]{2,1,0:T(8,128)(2,1)}), bf16[32,200,128]{2,1,0:T(8,128)(2,1)S(1)}, u32[]{:S(2)}, u32[]{:S(2)}) async-start(bf16[32,200,128]{2,1,0:T(8,128)(2,1)} %get-tuple-element.25), calls=%async_computation | async-start | bytes 3276800 | tf_op jit(solution)/shard_map/all_to_all | solution.py:59
  17.2 0.0 copy-done.9
  17.2 0.0 copy-done.14
  17.2 0.0 copy-done.15
  17.2 0.0 copy-done.17
  17.2 2.4 %hand.1 = bf16[32,200,128]{2,1,0:T(8,128)(2,1)S(1)} custom-call(bf16[1024,768]{1,0:T(8,128)(2,1)S(1)} %copy-done.9, s32[8,1024]{1,0:T(8,128)S(1)} %copy-done.17, s32[1,1024]{1,0:T(1,128)S(1)} %bitcast.11, s32[1,1024]{1,0:T(1,128)S(1)} %bitcast.13), custom_call_target="tpu_custom_call" | custom-call | flops 1610612736 | bytes 3145728 | tf_op jit(solution)/shard_map/hand/pallas_call | solution.py:181
  19.7 1.2 collective-permute-start
  20.9 3.1 %collective-permute-done = bf16[32,200,128]{2,1,0:T(8,128)(2,1)S(1)} collective-permute-done((bf16[32,200,128]{2,1,0:T(8,128)(2,1)S(1)}, bf16[32,200,128]{2,1,0:T(8,128)(2,1)S(1)}, u32[]{:S(2)}, u32[]{:S(2)}) %collective-permute-start) | collective-permute-done | bytes 1638432 | tf_op jit(solution)/shard_map/ppermute | solution.py:63
  24.0 1.2 copy-done.18
  25.2 30.7 %all-to-all-done.cells_ref = bf16[32,200,128]{2,1,0:T(8,128)(2,1)S(1)} async-done(((bf16[32,200,128]{2,1,0:T(8,128)(2,1)}), bf16[32,200,128]{2,1,0:T(8,128)(2,1)S(1)}, u32[]{:S(2)}, u32[]{:S(2)}) %all-to-all-start) | async-done | bytes 1638432 | tf_op jit(solution)/shard_map/all_to_all | solution.py:59
  55.9 7.1 %all-to-all-start.1 = ((bf16[32,200,128]{2,1,0:T(8,128)(2,1)}), bf16[32,200,128]{2,1,0:T(8,128)(2,1)S(1)}, u32[]{:S(2)}, u32[]{:S(2)}) async-start(bf16[32,200,128]{2,1,0:T(8,128)(2,1)} %copy-done.18), calls=%async_computation.1 | async-start | bytes 3276800 | tf_op jit(solution)/shard_map/all_to_all | solution.py:59
  63.0 0.0 copy-start.16
  63.0 0.8 settle.1
  63.8 0.0 copy-start.10
  63.8 0.0 copy-start.11
  63.8 1.4 collective-permute-start.1
  65.2 1.5 collective-permute-start.2
  66.7 13.1 %collective-permute-done.1.refs_2_.refs_4_.refs_7_ = bf16[528,768]{1,0:T(8,128)(2,1)S(1)} collective-permute-done((bf16[528,768]{1,0:T(8,128)(2,1)S(1)}, bf16[528,768]{1,0:T(8,128)(2,1)S(1)}, u32[]{:S(2)}, u32[]{:S(2)}) %collective-permute-start.1) | collective-permute-done | bytes 811040 | tf_op jit(solution)/shard_map/ppermute | solution.py:63
  79.8 0.0 collective-permute-start.3
  79.8 0.0 collective-permute-done.2.refs_4_.refs_7_.refs_8_
  79.8 0.0 copy-start.13
  79.8 2.7 %collective-permute-start.4 = (bf16[528,768]{1,0:T(8,128)(2,1)S(1)}, bf16[528,768]{1,0:T(8,128)(2,1)}, u32[]{:S(2)}, u32[]{:S(2)}) collective-permute-start(bf16[528,768]{1,0:T(8,128)(2,1)S(1)} %collective-permute-done.2.refs_4_.refs_7_.refs_8_), channel_id=1, source_target_pairs={{0,3},{4,196},{1,0},{5,197},{2,1},{6,198},{3,2},{7,199},{8,11},{12... | collective-permute-start | bytes 2433032 | tf_op jit(solution)/shard_map/ppermute | solution.py:63
  82.5 0.0 copy-done.16
  82.5 5.8 %first.1.refs_6_ = f32[64,128]{1,0:T(8,128)S(1)} custom-call(s32[42]{0:T(128)S(1)} %copy-done.16, bf16[528,768]{1,0:T(8,128)(2,1)S(1)} %get-tuple-element.33.refs_1_.refs_3_.refs_5_, bf16[528,768]{1,0:T(8,128)(2,1)S(1)} %collective-permute-done.1.refs_2_.refs_4_.refs_7_, bf16[528,768]{1,0:T(8,128)(2,1)S(1)} %get-tuple-element.36.refs_3_.refs_6_, ...), custom_call_target="tpu_custom_call" | custom-call | flops 2818572288 | bytes 3145728 | tf_op jit(solution)/shard_map/first/pallas_call | solution.py:417
  88.3 0.0 copy-done.10
  88.3 0.0 copy-done.11
  88.3 0.0 copy-done.12
  88.4 0.0 copy-done.13
  88.4 6.4 %collective-permute-done.3.refs_5_.refs_10_ = bf16[528,768]{1,0:T(8,128)(2,1)S(1)} collective-permute-done((bf16[528,768]{1,0:T(8,128)(2,1)S(1)}, bf16[528,768]{1,0:T(8,128)(2,1)S(1)}, u32[]{:S(2)}, u32[]{:S(2)}) %collective-permute-start.3) | collective-permute-done | bytes 811040 | tf_op jit(solution)/shard_map/ppermute | solution.py:63
  94.8 0.9 copy-done.19
  95.6 0.0 collective-permute-done.4.refs_8_.refs_9_
  95.6 5.9 %all-to-all-done.1.cells_ref = bf16[32,200,128]{2,1,0:T(8,128)(2,1)S(1)} async-done(((bf16[32,200,128]{2,1,0:T(8,128)(2,1)}), bf16[32,200,128]{2,1,0:T(8,128)(2,1)S(1)}, u32[]{:S(2)}, u32[]{:S(2)}) %all-to-all-start.1) | async-done | bytes 1638432 | tf_op jit(solution)/shard_map/all_to_all | solution.py:59
  101.6 0.4 split.1
  101.9 0.0 copy-start
  101.9 0.0 copy-start.2
  101.9 1.2 collective-permute-start.5
  103.1 1.7 %collective-permute-start.6 = (bf16[528,768]{1,0:T(8,128)(2,1)S(1)}, bf16[528,768]{1,0:T(8,128)(2,1)S(1)}, u32[]{:S(2)}, u32[]{:S(2)}) collective-permute-start(bf16[528,768]{1,0:T(8,128)(2,1)S(1)} %get-tuple-element.32.refs_2_.refs_3_.refs_4_), channel_id=1, source_target_pairs={{0,3},{4,196},{1,0},{5,197},{2,1},{6,198},{3,2},{7,199},{8,11},{12... | collective-permute-start | bytes 2433032 | tf_op jit(solution)/shard_map/ppermute | solution.py:63
  104.9 0.0 copy-done
  104.9 0.0 copy-done.2
  104.9 10.9 %own.1.refs_7_ = f32[64,128]{1,0:T(8,128)} custom-call(s32[72]{0:T(128)} %constant.9.clone.refs_0_, bf16[528,768]{1,0:T(8,128)(2,1)} %copy-done, bf16[528,768]{1,0:T(8,128)(2,1)} %copy-done.2, bf16[528,768]{1,0:T(8,128)(2,1)} %copy-done.10, bf16[528,768]{1,0:T(8,128)(2,1)} %copy-done.12, bf16[528,768]{1,0:T(8,128)(2,1)} %copy-done.19, ...), custom_call_target="tpu_custom_call" | custom-call | flops 4831838208 | bytes 6291456 | tf_op jit(solution)/shard_map/own/pallas_call | solution.py:417
  115.8 0.0 copy-start.1
  115.8 0.0 copy-start.3
  115.9 0.0 copy-start.6
  115.9 0.0 copy-start.8
  115.9 0.0 collective-permute-done.5.refs_2_
  115.9 0.0 collective-permute-done.6.refs_4_.refs_1_
  115.9 0.1 collective-permute-start.7
  116.0 2.7 %collective-permute-start.8 = (bf16[528,768]{1,0:T(8,128)(2,1)S(1)}, bf16[528,768]{1,0:T(8,128)(2,1)S(1)}, u32[]{:S(2)}, u32[]{:S(2)}) collective-permute-start(bf16[528,768]{1,0:T(8,128)(2,1)S(1)} %collective-permute-done.6.refs_4_.refs_1_), channel_id=1, source_target_pairs={{0,3},{4,196},{1,0},{5,197},{2,1},{6,198},{3,2},{7,199},{8,11},{12... | collective-permute-start | bytes 2433032 | tf_op jit(solution)/shard_map/ppermute | solution.py:63
  118.7 12.3 %near.1.refs_8_ = f32[64,128]{1,0:T(8,128)} custom-call(s32[78]{0:T(128)} %constant.10.clone.refs_0_, bf16[528,768]{1,0:T(8,128)(2,1)} %copy-done, bf16[528,768]{1,0:T(8,128)(2,1)} %collective-permute-done.5.refs_2_, bf16[528,768]{1,0:T(8,128)(2,1)} %copy-done.2, bf16[528,768]{1,0:T(8,128)(2,1)} %copy-done.4, bf16[528,768]{1,0:T(8,128)(2,1)} %copy-done.10, ...), custom_call_target="tpu_custom_call" | custom-call | flops 5234491392 | bytes 7864320 | tf_op jit(solution)/shard_map/near/pallas_call | solution.py:417
  130.9 0.0 collective-permute-done.7.refs_2_
  130.9 0.0 collective-permute-done.8.refs_5_
  131.0 1.1 copy-done.5
  132.1 0.8 copy-done.7
  132.9 3.4 %far.1 = f32[128,128]{1,0:T(8,128)S(1)} custom-call(s32[12]{0:T(128)S(1)} %copy-done.8, bf16[528,768]{1,0:T(8,128)(2,1)S(1)} %copy-done.5, bf16[528,768]{1,0:T(8,128)(2,1)S(1)} %collective-permute-done.7.refs_2_, bf16[528,768]{1,0:T(8,128)(2,1)S(1)} %copy-done.1, bf16[528,768]{1,0:T(8,128)(2,1)S(1)} %copy-done.3, ...), custom_call_target="tpu_custom_call" | custom-call | flops 805306368 | bytes 3932160 | tf_op jit(solution)/shard_map/far/pallas_call | solution.py:417
  136.3 19.7 %all_to_all.15 = f32[128,1,128]{2,1,0:T(1,128)S(1)} all-to-all(f32[128,1,128]{2,1,0:T(1,128)S(1)} %bitcast.7), channel_id=1, replica_groups={{0,8,16,24,32,40,48,56,64,72,80,88,96,104,112,120,128,136,144,152,160,1..., dimensions={0} | all-to-all | bytes 131072 | tf_op jit(solution)/shard_map/all_to_all | solution.py:59
  156.0 4.4 %collective-permute-start.9 = (f32[128,128]{1,0:T(8,128)S(1)}, f32[128,128]{1,0:T(8,128)S(1)}, u32[]{:S(2)}, u32[]{:S(2)}) collective-permute-start(f32[128,128]{1,0:T(8,128)S(1)} %bitcast.8), channel_id=1, source_target_pairs={{0,4},{1,5},{2,6},{3,7},{4,0},{5,1},{6,2},{7,3},{8,12},{9,13},{10,... | collective-permute-start | bytes 196616 | tf_op jit(solution)/shard_map/ppermute | solution.py:63
  160.4 0.5 answer.2.refs_0_
  160.9 0.4 collective-permute-done.9.values_ref
  161.3 1.0 answer.3
  (11 shorter events, 0.0 us)
Async XLA Ops:
  5.1 12.1 %copy-start.9 = (bf16[1024,768]{1,0:T(8,128)(2,1)S(1)}, bf16[1024,768]{1,0:T(8,128)(2,1)}, u32[]{:S(2)}) copy-start(bf16[1024,768]{1,0:T(8,128)(2,1)} %emb_ref.3) | copy-start | bytes 4718596
  5.1 12.1 %copy-start.14 = (s32[1024]{0:T(1024)S(1)}, s32[1024]{0:T(1024)}, u32[]{:S(2)}) copy-start(s32[1024]{0:T(1024)} %param.8) | copy-start | bytes 12292
  5.1 12.1 %copy-start.15 = (s32[1024]{0:T(1024)S(1)}, s32[1024]{0:T(1024)}, u32[]{:S(2)}) copy-start(s32[1024]{0:T(1024)} %param.9) | copy-start | bytes 12292
  5.1 12.1 %copy-start.17 = (s32[8,1024]{1,0:T(8,128)S(1)}, s32[8,1024]{1,0:T(8,128)}, u32[]{:S(2)}) copy-start(s32[8,1024]{1,0:T(8,128)} %get-tuple-element.24.info_ref) | copy-start | bytes 98308
  5.1 50.8 %all-to-all-start = ((bf16[32,200,128]{2,1,0:T(8,128)(2,1)}), bf16[32,200,128]{2,1,0:T(8,128)(2,1)S(1)}, u32[]{:S(2)}, u32[]{:S(2)}) async-start(bf16[32,200,128]{2,1,0:T(8,128)(2,1)} %get-tuple-element.25), calls=%async_computation | async-start | bytes 3276800 | tf_op jit(solution)/shard_map/all_to_all | solution.py:59
  19.7 4.3 %collective-permute-start = (bf16[32,200,128]{2,1,0:T(8,128)(2,1)S(1)}, bf16[32,200,128]{2,1,0:T(8,128)(2,1)S(1)}, u32[]{:S(2)}, u32[]{:S(2)}) collective-permute-start(bf16[32,200,128]{2,1,0:T(8,128)(2,1)S(1)} %hand.1), channel_id=1, source_target_pairs={{0,4},{1,5},{2,6},{3,7},{4,0},{5,1},{6,2},{7,3},{8,12},{9,13},{10,... | collective-permute-start | bytes 4915208 | tf_op jit(solution)/shard_map/ppermute | solution.py:63
  24.0 1.2 copy-start.18
  55.9 45.6 %all-to-all-start.1 = ((bf16[32,200,128]{2,1,0:T(8,128)(2,1)}), bf16[32,200,128]{2,1,0:T(8,128)(2,1)S(1)}, u32[]{:S(2)}, u32[]{:S(2)}) async-start(bf16[32,200,128]{2,1,0:T(8,128)(2,1)} %copy-done.18), calls=%async_computation.1 | async-start | bytes 3276800 | tf_op jit(solution)/shard_map/all_to_all | solution.py:59
  63.0 19.4 %copy-start.16 = (s32[42]{0:T(128)S(1)}, s32[42]{0:T(128)}, u32[]{:S(2)}) copy-start(s32[42]{0:T(128)} %constant.8.clone.refs_0_) | copy-start | bytes 508
  63.8 24.5 %copy-start.10 = (bf16[528,768]{1,0:T(8,128)(2,1)}, bf16[528,768]{1,0:T(8,128)(2,1)S(1)}, u32[]{:S(2)}) copy-start(bf16[528,768]{1,0:T(8,128)(2,1)S(1)} %get-tuple-element.33.refs_1_.refs_3_.refs_5_) | copy-start | bytes 2433028
  63.8 24.5 %copy-start.11 = (bf16[528,768]{1,0:T(8,128)(2,1)}, bf16[528,768]{1,0:T(8,128)(2,1)S(1)}, u32[]{:S(2)}) copy-start(bf16[528,768]{1,0:T(8,128)(2,1)S(1)} %get-tuple-element.36.refs_3_.refs_6_) | copy-start | bytes 2433028
  63.8 15.9 %collective-permute-start.1 = (bf16[528,768]{1,0:T(8,128)(2,1)S(1)}, bf16[528,768]{1,0:T(8,128)(2,1)S(1)}, u32[]{:S(2)}, u32[]{:S(2)}) collective-permute-start(bf16[528,768]{1,0:T(8,128)(2,1)S(1)} %get-tuple-element.33.refs_1_.refs_3_.refs_5_), channel_id=1, source_target_pairs={{0,1},{4,68},{1,2},{5,69},{2,3},{6,70},{3,0},{7,71},{8,9},{12,76},... | collective-permute-start | bytes 2433032 | tf_op jit(solution)/shard_map/ppermute | solution.py:63
  65.2 14.6 %collective-permute-start.2 = (bf16[528,768]{1,0:T(8,128)(2,1)S(1)}, bf16[528,768]{1,0:T(8,128)(2,1)S(1)}, u32[]{:S(2)}, u32[]{:S(2)}) collective-permute-start(bf16[528,768]{1,0:T(8,128)(2,1)S(1)} %get-tuple-element.36.refs_3_.refs_6_), channel_id=1, source_target_pairs={{0,3},{4,196},{1,0},{5,197},{2,1},{6,198},{3,2},{7,199},{8,11},{12... | collective-permute-start | bytes 2433032 | tf_op jit(solution)/shard_map/ppermute | solution.py:63
  79.8 8.6 %copy-start.12 = (bf16[528,768]{1,0:T(8,128)(2,1)}, bf16[528,768]{1,0:T(8,128)(2,1)S(1)}, u32[]{:S(2)}) copy-start(bf16[528,768]{1,0:T(8,128)(2,1)S(1)} %collective-permute-done.1.refs_2_.refs_4_.refs_7_) | copy-start | bytes 2433028
  79.8 15.0 %collective-permute-start.3 = (bf16[528,768]{1,0:T(8,128)(2,1)S(1)}, bf16[528,768]{1,0:T(8,128)(2,1)S(1)}, u32[]{:S(2)}, u32[]{:S(2)}) collective-permute-start(bf16[528,768]{1,0:T(8,128)(2,1)S(1)} %collective-permute-done.1.refs_2_.refs_4_.refs_7_), channel_id=1, source_target_pairs={{0,1},{4,68},{1,2},{5,69},{2,3},{6,70},{3,0},{7,71},{8,9},{12,76},... | collective-permute-start | bytes 2433032 | tf_op jit(solution)/shard_map/ppermute | solution.py:63
  79.8 8.6 %copy-start.13 = (bf16[528,768]{1,0:T(8,128)(2,1)}, bf16[528,768]{1,0:T(8,128)(2,1)S(1)}, u32[]{:S(2)}) copy-start(bf16[528,768]{1,0:T(8,128)(2,1)S(1)} %collective-permute-done.2.refs_4_.refs_7_.refs_8_) | copy-start | bytes 2433028
  79.8 15.8 %collective-permute-start.4 = (bf16[528,768]{1,0:T(8,128)(2,1)S(1)}, bf16[528,768]{1,0:T(8,128)(2,1)}, u32[]{:S(2)}, u32[]{:S(2)}) collective-permute-start(bf16[528,768]{1,0:T(8,128)(2,1)S(1)} %collective-permute-done.2.refs_4_.refs_7_.refs_8_), channel_id=1, source_target_pairs={{0,3},{4,196},{1,0},{5,197},{2,1},{6,198},{3,2},{7,199},{8,11},{12... | collective-permute-start | bytes 2433032 | tf_op jit(solution)/shard_map/ppermute | solution.py:63
  94.8 0.9 copy-start.19
  101.9 3.0 %copy-start = (bf16[528,768]{1,0:T(8,128)(2,1)}, bf16[528,768]{1,0:T(8,128)(2,1)S(1)}, u32[]{:S(2)}) copy-start(bf16[528,768]{1,0:T(8,128)(2,1)S(1)} %get-tuple-element.31.refs_1_.refs_3_) | copy-start | bytes 2433028
  101.9 3.0 %copy-start.2 = (bf16[528,768]{1,0:T(8,128)(2,1)}, bf16[528,768]{1,0:T(8,128)(2,1)S(1)}, u32[]{:S(2)}) copy-start(bf16[528,768]{1,0:T(8,128)(2,1)S(1)} %get-tuple-element.32.refs_2_.refs_3_.refs_4_) | copy-start | bytes 2433028
  101.9 13.9 %collective-permute-start.5 = (bf16[528,768]{1,0:T(8,128)(2,1)S(1)}, bf16[528,768]{1,0:T(8,128)(2,1)}, u32[]{:S(2)}, u32[]{:S(2)}) collective-permute-start(bf16[528,768]{1,0:T(8,128)(2,1)S(1)} %get-tuple-element.31.refs_1_.refs_3_), channel_id=1, source_target_pairs={{0,1},{4,68},{1,2},{5,69},{2,3},{6,70},{3,0},{7,71},{8,9},{12,76},... | collective-permute-start | bytes 2433032 | tf_op jit(solution)/shard_map/ppermute | solution.py:63
  103.1 12.8 %collective-permute-start.6 = (bf16[528,768]{1,0:T(8,128)(2,1)S(1)}, bf16[528,768]{1,0:T(8,128)(2,1)S(1)}, u32[]{:S(2)}, u32[]{:S(2)}) collective-permute-start(bf16[528,768]{1,0:T(8,128)(2,1)S(1)} %get-tuple-element.32.refs_2_.refs_3_.refs_4_), channel_id=1, source_target_pairs={{0,3},{4,196},{1,0},{5,197},{2,1},{6,198},{3,2},{7,199},{8,11},{12... | collective-permute-start | bytes 2433032 | tf_op jit(solution)/shard_map/ppermute | solution.py:63
  115.8 15.1 %copy-start.1 = (bf16[528,768]{1,0:T(8,128)(2,1)S(1)}, bf16[528,768]{1,0:T(8,128)(2,1)}, u32[]{:S(2)}) copy-start(bf16[528,768]{1,0:T(8,128)(2,1)} %copy-done) | copy-start | bytes 2433028
  115.8 15.1 %copy-start.3 = (bf16[528,768]{1,0:T(8,128)(2,1)S(1)}, bf16[528,768]{1,0:T(8,128)(2,1)}, u32[]{:S(2)}) copy-start(bf16[528,768]{1,0:T(8,128)(2,1)} %copy-done.2) | copy-start | bytes 2433028
  115.9 15.1 %copy-start.6 = (f32[64,128]{1,0:T(8,128)S(1)}, f32[64,128]{1,0:T(8,128)}, u32[]{:S(2)}) copy-start(f32[64,128]{1,0:T(8,128)} %own.1.refs_7_) | copy-start | bytes 98308
  115.9 15.1 %copy-start.8 = (s32[12]{0:T(128)S(1)}, s32[12]{0:T(128)}, u32[]{:S(2)}) copy-start(s32[12]{0:T(128)} %constant.11.clone.refs_0_) | copy-start | bytes 148
  115.9 2.8 %copy-start.4 = (bf16[528,768]{1,0:T(8,128)(2,1)}, bf16[528,768]{1,0:T(8,128)(2,1)S(1)}, u32[]{:S(2)}) copy-start(bf16[528,768]{1,0:T(8,128)(2,1)S(1)} %collective-permute-done.6.refs_4_.refs_1_) | copy-start | bytes 2433028
  115.9 15.0 %collective-permute-start.7 = (bf16[528,768]{1,0:T(8,128)(2,1)}, bf16[528,768]{1,0:T(8,128)(2,1)S(1)}, u32[]{:S(2)}, u32[]{:S(2)}) collective-permute-start(bf16[528,768]{1,0:T(8,128)(2,1)} %collective-permute-done.5.refs_2_), channel_id=1, source_target_pairs={{0,1},{4,68},{1,2},{5,69},{2,3},{6,70},{3,0},{7,71},{8,9},{12,76},... | collective-permute-start | bytes 2433032 | tf_op jit(solution)/shard_map/ppermute | solution.py:63
  116.0 15.0 %collective-permute-start.8 = (bf16[528,768]{1,0:T(8,128)(2,1)S(1)}, bf16[528,768]{1,0:T(8,128)(2,1)S(1)}, u32[]{:S(2)}, u32[]{:S(2)}) collective-permute-start(bf16[528,768]{1,0:T(8,128)(2,1)S(1)} %collective-permute-done.6.refs_4_.refs_1_), channel_id=1, source_target_pairs={{0,3},{4,196},{1,0},{5,197},{2,1},{6,198},{3,2},{7,199},{8,11},{12... | collective-permute-start | bytes 2433032 | tf_op jit(solution)/shard_map/ppermute | solution.py:63
  131.0 1.1 copy-start.5
  132.1 0.8 copy-start.7
  156.0 5.3 %collective-permute-start.9 = (f32[128,128]{1,0:T(8,128)S(1)}, f32[128,128]{1,0:T(8,128)S(1)}, u32[]{:S(2)}, u32[]{:S(2)}) collective-permute-start(f32[128,128]{1,0:T(8,128)S(1)} %bitcast.8), channel_id=1, source_target_pairs={{0,4},{1,5},{2,6},{3,7},{4,0},{5,1},{6,2},{7,3},{8,12},{9,13},{10,... | collective-permute-start | bytes 196616 | tf_op jit(solution)/shard_map/ppermute | solution.py:63
